TPU v7x, 32 devices: a whole 2x2x4 slice. The times are simulated.
32 devices in a mesh: dp: 2 (over x), expert: 16 (over z, y, core).
Axes of the slice: x: 2, y: 2, z: 4, core: 2. Of those that a mesh axis runs over, the one named last changes fastest.
Arguments:
- cache_lat: bfloat16 [1536, 64, 512], P(('dp', 'expert')), may hold values from -6 to 6
- cache_rope: bfloat16 [1536, 4096], P(('dp', 'expert')), may hold values from -6 to 6
- page_scale: bfloat16 [1536], P(('dp', 'expert')), may hold values from 0.5 to 2
- move_list: int32 [32, 2, 4], P(('dp', 'expert')), may hold values from 0 to 47
- page_table: int32 [64, 32], P(('dp', 'expert')), may hold values from 0 to 55, as said below
- lengths: int32 [64], P(('dp', 'expert')), may hold values from 193 to 2048, as said below
- q_lat: bfloat16 [64, 2, 32, 512], P(('dp', 'expert')), may hold values from -72 to 72
- q_rope: bfloat16 [64, 2, 32, 64], P(('dp', 'expert')), may hold values from -12 to 12
- new_lat: bfloat16 [64, 2, 512], P(('dp', 'expert')), may hold values from -6 to 6
- new_rope: bfloat16 [64, 2, 64], P(('dp', 'expert')), may hold values from -6 to 6
- w_uv: bfloat16 [32, 512, 128], P('expert'), may hold values from -6 to 6
- w_out: bfloat16 [4096, 3584], P('expert'), may hold values from -0.09375 to 0.09375
- residual: bfloat16 [128, 3584], P(('dp', 'expert')), may hold values from -400 to 400
- norm_gain: float32 [3584], replicated, may hold values from 0.1 to 1.9
- w_router: bfloat16 [3584, 16], replicated, may hold values from -0.09375 to 0.09375
- routes: int32 [128, 8], P(('dp', 'expert')), may hold values from 0 to 15, all different within a row; in each aligned block of 4 rows (0 to 3, 4 to 7, ...) at most 4 rows name the same one
- w_gate: bfloat16 [16, 3584, 2048], P('expert', None, 'dp'), may hold values from -0.09375 to 0.09375
- w_up: bfloat16 [16, 3584, 2048], P('expert', None, 'dp'), may hold values from -0.09375 to 0.09375
- w_down: bfloat16 [16, 2048, 3584], P('expert', 'dp'), may hold values from -0.125 to 0.125
Outputs:
- attn_out: bfloat16 [128, 3584], P(('dp', 'expert'))
- moe_out: bfloat16 [128, 3584], P(('dp', 'expert'))
Inputs may be any that keep to these rules, and one draw needn't show every extreme that they name: `lengths`: cached tokens of a rollout besides its 2 new ones; some rollout holds 2048. `page_table`: a rollout names no page index twice. `routes`: among the rows of one device no expert is named more than 4 times; some expert is named exactly 4 times.
All inputs are finite; a program needn't handle non-finite values.
Results may differ from a plain program's by a relative error of at most 0.03.
Values may be sent and summed in bfloat16 or wider, within the bound.
No kernel may reach another device: no remote copies, remote signals or barrier semaphores. Data moves between devices by JAX's collectives and lax.ppermute only.
A program may use at most 128 MiB of HBM per device.

v0:
```python
import jax
import jax.numpy as jnp
from jax import lax
from jax.sharding import PartitionSpec as P

SCORE_SCALE = 0.07216878364870322
ROUTE_SCALE = 2.5
NORM_EPS = 1e-06


def slot_masks(weight_table, capacity):
    chosen = (weight_table > 0.0).astype(jnp.int32)
    earlier = jnp.cumsum(chosen, axis=-2) - chosen
    slot_ids = jnp.arange(capacity, dtype=jnp.int32)
    return (earlier[..., None] == slot_ids) & (chosen[..., None] > 0)


def body(
    cache_lat,
    cache_rope,
    page_scale,
    move_list,
    page_table,
    lengths,
    q_lat,
    q_rope,
    new_lat,
    new_rope,
    w_uv,
    w_out,
    residual,
    norm_gain,
    w_router,
    routes,
    w_gate,
    w_up,
    w_down,
):
    dp_count = lax.axis_size("dp")
    page_len = cache_lat.shape[1]
    latent_dim = cache_lat.shape[2]
    rope_dim = q_rope.shape[3]
    moves_each = move_list.shape[2]
    rollouts = q_lat.shape[0]
    next_count = q_lat.shape[1]
    table_len = page_table.shape[1]
    model_dim = residual.shape[1]
    highest = lax.Precision.HIGHEST
    picked = move_list[0]
    sent = (cache_lat[picked], cache_rope[picked], page_scale[picked])
    got_lat, got_rope, got_scale = (
        lax.all_to_all(sent[0], "dp", split_axis=0, concat_axis=0, tiled=True),
        lax.all_to_all(sent[1], "dp", split_axis=0, concat_axis=0, tiled=True),
        lax.all_to_all(sent[2], "dp", split_axis=0, concat_axis=0, tiled=True),
    )
    view_lat = jnp.concatenate(
        [cache_lat, got_lat.reshape(dp_count * moves_each, page_len, latent_dim)], axis=0
    )
    view_rope = jnp.concatenate([cache_rope, got_rope.reshape(dp_count * moves_each, -1)], axis=0)
    view_scale = jnp.concatenate([page_scale, got_scale.reshape(-1)], axis=0)
    cached = table_len * page_len
    keys_lat = view_lat[page_table].reshape(rollouts, cached, latent_dim)
    keys_rope = view_rope[page_table].reshape(rollouts, cached, rope_dim)
    page_factor = view_scale[page_table].astype(jnp.float32)
    token_scale = jnp.broadcast_to(
        page_factor[:, :, None], (rollouts, table_len, page_len)
    ).reshape(rollouts, cached)
    old_scores = jnp.einsum("rphl,rtl->rpht", q_lat, keys_lat, preferred_element_type=jnp.float32)
    old_scores = old_scores + jnp.einsum(
        "rphk,rtk->rpht", q_rope, keys_rope, preferred_element_type=jnp.float32
    )
    old_scores = old_scores * (token_scale * SCORE_SCALE)[:, None, None, :]
    live = jnp.arange(cached, dtype=jnp.int32)[None, :] < lengths[:, None]
    old_scores = jnp.where(live[:, None, None, :], old_scores, -jnp.inf)
    new_scores = jnp.einsum("rphl,rul->rphu", q_lat, new_lat, preferred_element_type=jnp.float32)
    new_scores = new_scores + jnp.einsum(
        "rphk,ruk->rphu", q_rope, new_rope, preferred_element_type=jnp.float32
    )
    new_scores = new_scores * SCORE_SCALE
    causal = jnp.arange(next_count)[None, :] <= jnp.arange(next_count)[:, None]
    new_scores = jnp.where(causal[None, :, None, :], new_scores, -jnp.inf)
    peak = jnp.maximum(jnp.max(old_scores, -1), jnp.max(new_scores, -1))
    old_exp = jnp.exp(old_scores - peak[..., None])
    new_exp = jnp.exp(new_scores - peak[..., None])
    total = jnp.sum(old_exp, -1) + jnp.sum(new_exp, -1)
    old_weights = (old_exp / total[..., None] * token_scale[:, None, None, :]).astype(jnp.bfloat16)
    new_weights = (new_exp / total[..., None]).astype(jnp.bfloat16)
    latent_sum = jnp.einsum(
        "rpht,rtl->rphl", old_weights, keys_lat, preferred_element_type=jnp.float32
    )
    latent_sum = latent_sum + jnp.einsum(
        "rphu,rul->rphl", new_weights, new_lat, preferred_element_type=jnp.float32
    )
    latent_out = latent_sum.astype(jnp.bfloat16)
    head_group = lax.all_to_all(latent_out, "expert", split_axis=2, concat_axis=0, tiled=True)
    head_values = jnp.einsum(
        "rphl,hlv->rphv", head_group, w_uv, preferred_element_type=jnp.float32
    ).astype(jnp.bfloat16)
    value_rows = head_values.reshape(head_values.shape[0] * next_count, -1)
    attn_sum = lax.psum_scatter(
        jnp.dot(value_rows, w_out, preferred_element_type=jnp.float32).astype(jnp.bfloat16),
        "expert",
        scatter_dimension=0,
        tiled=True,
    ).astype(jnp.float32)
    attn_out = attn_sum.astype(jnp.bfloat16)
    hidden = (residual.astype(jnp.float32) + attn_sum).astype(jnp.bfloat16)
    hidden_f = hidden.astype(jnp.float32)
    normed = (
        hidden_f
        * lax.rsqrt(jnp.mean(hidden_f * hidden_f, -1, keepdims=True) + NORM_EPS)
        * norm_gain
    ).astype(jnp.bfloat16)
    logits = jnp.dot(normed, w_router, preferred_element_type=jnp.float32)
    expert_total = w_router.shape[1]
    top_count = routes.shape[1]
    onehot = routes[:, :, None] == jnp.arange(expert_total, dtype=jnp.int32)[None, None, :]
    selected = jnp.sum(jnp.where(onehot, logits[:, None, :], jnp.float32(0.0)), -1)
    sig = jax.nn.sigmoid(selected)
    gates = ROUTE_SCALE * sig / jnp.sum(sig, -1, keepdims=True)
    weight_table = jnp.sum(jnp.where(onehot, gates[:, :, None], jnp.float32(0.0)), 1)
    capacity = min(2 * rollouts, max(2, 4 * rollouts * top_count // expert_total))
    own_slots = slot_masks(weight_table, capacity)
    send_rows = jnp.einsum(
        "tec,td->ecd", own_slots.astype(jnp.bfloat16), normed, preferred_element_type=jnp.float32
    ).astype(jnp.bfloat16)
    arrived = lax.all_to_all(send_rows, "expert", split_axis=0, concat_axis=0, tiled=True)
    grouped = lax.all_gather(arrived, "dp", axis=1, tiled=True)
    flat_rows = grouped.reshape(-1, model_dim)
    gate_part = jnp.dot(flat_rows, w_gate[0], preferred_element_type=jnp.float32)
    up_part = jnp.dot(flat_rows, w_up[0], preferred_element_type=jnp.float32)
    expert_hidden = (jax.nn.silu(gate_part) * up_part).astype(jnp.bfloat16)
    partial_out = jnp.dot(expert_hidden, w_down[0], preferred_element_type=jnp.float32)
    partial_out = partial_out.reshape(expert_total, dp_count, capacity, model_dim)
    group_table = lax.all_gather(weight_table, "dp", axis=0, tiled=True)
    group_table = group_table.reshape(dp_count, -1, expert_total)
    group_slots = slot_masks(group_table, capacity)
    combine_weights = jnp.where(group_slots, group_table[..., None], jnp.float32(0.0))
    returned = lax.all_to_all(
        partial_out.astype(jnp.bfloat16), "expert", split_axis=0, concat_axis=0, tiled=True
    ).astype(partial_out.dtype)
    mixed = jnp.einsum("ktec,ekcd->ktd", combine_weights, returned, precision=highest)
    moe_sum = lax.psum_scatter(
        mixed.astype(jnp.bfloat16), "dp", scatter_dimension=0, tiled=True
    ).astype(jnp.float32)[0]
    return (attn_out, moe_sum.astype(jnp.bfloat16))


def solution(mesh):
    return jax.shard_map(
        body,
        mesh=mesh,
        in_specs=(
            P(("dp", "expert"), None, None),
            P(("dp", "expert"), None),
            P(("dp", "expert")),
            P(("dp", "expert"), None, None),
            P(("dp", "expert"), None),
            P(("dp", "expert")),
            P(("dp", "expert"), None, None, None),
            P(("dp", "expert"), None, None, None),
            P(("dp", "expert"), None, None),
            P(("dp", "expert"), None, None),
            P("expert", None, None),
            P("expert", None),
            P(("dp", "expert"), None),
            P(),
            P(),
            P(("dp", "expert"), None),
            P("expert", None, "dp"),
            P("expert", None, "dp"),
            P("expert", "dp", None),
        ),
        out_specs=(P(("dp", "expert"), None), P(("dp", "expert"), None)),
        check_vma=False,
    )
```

profile of v0, /device:TPU:0, one launch (start us, length us, event | category | flops | bytes accessed | tf_op | source)
XLA Modules:
  0.0 247.7 jit_solution(2784961414634606934)
XLA Ops:
  10.1 4.2 %all-to-all-start.2 = ((bf16[2,1,4]{2,1,0:T(2,128)(2,1)}), bf16[2,1,4]{2,1,0:T(2,128)(2,1)S(1)}, u32[]{:S(2)}, u32[]{:S(2)}) async-start(bf16[2,1,4]{2,1,0:T(2,128)(2,1)} %all_to_all.41), calls=%async_computation.2 | async-start | bytes 2048 | tf_op jit(solution)/shard_map/all_to_all | solution.py:54
  14.3 3.3 %gather_fusion = bf16[8,64,512]{2,1,0:T(8,128)(2,1)} fusion(bf16[48,64,512]{2,1,0:T(8,128)(2,1)} %param.19, s32[1024]{0:T(1024)S(1)} %pad_clamp_fusion.1), kind=kCustom, calls=%fused_computation | custom fusion | bytes 1048608 | tf_op jit(solution)/shard_map/gather | solution.py:50
  18.3 1.7 gather_fusion.2
  23.5 3.3 %all-to-all-start.1 = ((bf16[2,4,4096]{2,1,0:T(4,128)(2,1)}), bf16[2,4,4096]{2,1,0:T(4,128)(2,1)S(1)}, u32[]{:S(2)}, u32[]{:S(2)}) async-start(bf16[2,4,4096]{2,1,0:T(4,128)(2,1)} %reshape.215), calls=%async_computation.1 | async-start | bytes 131072 | tf_op jit(solution)/shard_map/all_to_all | solution.py:53
  28.7 2.2 all-to-all-done.1
  30.9 3.6 %all-to-all-start = ((bf16[2,4,64,512]{3,2,1,0:T(8,128)(2,1)}), bf16[2,4,64,512]{3,2,1,0:T(8,128)(2,1)S(1)}, u32[]{:S(2)}, u32[]{:S(2)}) async-start(bf16[2,4,64,512]{3,2,1,0:T(8,128)(2,1)} %bitcast.100), calls=%async_computation | async-start | bytes 1048576 | tf_op jit(solution)/shard_map/all_to_all | solution.py:52
  34.6 1.7 gather_fusion.3
  36.3 2.1 reshape.192
  40.0 1.8 all-to-all-done
  41.8 4.0 %pad_maximum_fusion = bf16[56,64,512]{2,1,0:T(8,128)(2,1)} fusion(bf16[8,64,512]{2,1,0:T(8,128)(2,1)S(1)} %bitcast.99, bf16[48,64,512]{2,1,0:T(8,128)(2,1)} %param.19), kind=kLoop, calls=%fused_computation.17 | loop fusion | flops 1835008 | bytes 7340032 | tf_op jit(solution)/shard_map/concatenate | solution.py:56
  45.8 4.9 %gather_fusion.1 = bf16[64,64,512]{2,1,0:T(8,128)(2,1)} fusion(bf16[56,64,512]{2,1,0:T(8,128)(2,1)} %pad_maximum_fusion, s32[1024]{0:T(1024)S(1)} %pad_clamp_fusion), kind=kCustom, calls=%fused_computation.1 | custom fusion | bytes 8388864 | tf_op jit(solution)/shard_map/gather | solution.py:62
  50.7 3.8 %fusion.65 = (f32[2,2,32]{2,1,0:T(2,128)S(1)}, f32[2,2,32,2048]{3,2,1,0:T(8,128)S(1)}) fusion(f32[2,2048]{1,0:T(2,128)S(1)} %broadcast_multiply_fusion, f32[2,2048,2,32]{1,3,2,0:T(8,128)S(1)} %copy-done.2, bf16[2,2048,512,1]{2,1,3,0:T(8,128)(2,1)} %bitcast.97, bf16[2,2,32,512]{3,2,1,0:T(8,128)(2,1)S(1)} %copy-done.5, ...), kind=kOutput, calls=%fused_computation.102 | convolution fusion | flops 269483904 | bytes 6443520 | tf_op jit(solution)/shard_map/rphl,rtl->rpht/dot_general | solution.py:68
  56.3 13.9 %all_to_all.48 = bf16[2,2,32,512]{3,1,0,2:T(2,128)(2,1)S(1)} all-to-all(bf16[2,2,32,512]{3,1,0,2:T(2,128)(2,1)S(1)} %copy.51), channel_id=1, replica_groups=mesh['dp'=2,'expert'=16] {'expert'}, dimensions={2} | all-to-all | bytes 262144 | tf_op jit(solution)/shard_map/all_to_all | solution.py:95
  73.1 85.5 %all-reduce.4.cloned.1.call-done = bf16[64,3584]{1,0:T(8,128)(2,1)} async-done(((bf16[64,3584]{1,0:T(8,128)(2,1)}), bf16[64,3584]{1,0:T(8,128)(2,1)}) %all-reduce.4.cloned.1.call-update) | async-done | bytes 458768
  161.1 18.1 %all_to_all.49 = bf16[16,4,3584]{2,1,0:T(4,128)(2,1)S(1)} all-to-all(bf16[16,4,3584]{2,1,0:T(4,128)(2,1)S(1)} %copy.54), channel_id=1, replica_groups=mesh['dp'=2,'expert'=16] {'expert'}, dimensions={0} | all-to-all | bytes 917504 | tf_op jit(solution)/shard_map/all_to_all | solution.py:127
  179.3 13.5 %all_gather.7 = bf16[16,8,3584]{2,0,1:T(8,128)(2,1)S(1)} all-gather(bf16[16,4,3584]{2,0,1:T(8,128)(2,1)S(1)} %copy.55), channel_id=1, replica_groups=mesh['dp'=2,'expert'=16] {'dp'}, dimensions={1}, use_global_device_ids=true | all-gather | bytes 1376256 | tf_op jit(solution)/shard_map/all_gather | solution.py:128
  192.9 4.8 %fusion.4 = f32[128,1024]{1,0:T(8,128)S(1)} fusion(bf16[1,3584,1024]{2,1,0:T(8,128)(2,1)} %param.35, bf16[16,8,3584]{2,0,1:T(8,128)(2,1)S(1)} %all_gather.7), kind=kOutput, calls=%fused_computation.10 | convolution fusion | flops 939524096 | bytes 8781824 | tf_op jit(solution)/shard_map/dot_general | solution.py:130
  197.7 1.6 fusion.16
  199.4 4.3 %fusion.6 = bf16[16,2,4,3584]{3,0,2,1:T(8,128)(2,1)S(1)} fusion(bf16[1,1024,3584]{2,1,0:T(8,128)(2,1)} %param.37, bf16[16,2,4,1024]{3,2,1,0:T(4,128)(2,1)S(1)} %dot_general.56), kind=kOutput, calls=%fused_computation.12 | convolution fusion | flops 939982848 | bytes 8519680 | tf_op jit(solution)/shard_map/dot_general | solution.py:133
  203.7 1.6 copy.58
  205.4 4.1 %all-to-all-start.5 = ((bf16[16,2,4,3584]{3,2,1,0:T(4,128)(2,1)}), bf16[16,2,4,3584]{3,2,1,0:T(4,128)(2,1)S(1)}, u32[]{:S(2)}, u32[]{:S(2)}) async-start(bf16[16,2,4,3584]{3,2,1,0:T(4,128)(2,1)} %copy.58), calls=%async_computation.5 | async-start | bytes 1835008 | tf_op jit(solution)/shard_map/all_to_all | solution.py:139
  210.1 4.3 %all-gather = f32[2,4,16]{2,1,0:T(4,128)S(1)} all-gather(f32[1,4,16]{2,1,0:T(4,128)S(1)} %bitcast.104), channel_id=1, replica_groups=mesh['dp'=2,'expert'=16] {'dp'}, dimensions={0}, use_global_device_ids=true | all-gather | bytes 768 | tf_op jit(solution)/shard_map/all_gather | solution.py:135
  214.5 15.8 %all-to-all-done.5 = bf16[16,2,4,3584]{3,2,1,0:T(4,128)(2,1)S(1)} async-done(((bf16[16,2,4,3584]{3,2,1,0:T(4,128)(2,1)}), bf16[16,2,4,3584]{3,2,1,0:T(4,128)(2,1)S(1)}, u32[]{:S(2)}, u32[]{:S(2)}) %all-to-all-start.5) | async-done | bytes 917536 | tf_op jit(solution)/shard_map/all_to_all | solution.py:139
  230.9 8.7 %all-reduce.1 = bf16[2,4,3584]{2,1,0:T(4,128)(2,1)S(1)} all-reduce(bf16[2,4,3584]{2,1,0:T(4,128)(2,1)S(1)} %fusion.9), channel_id=3, replica_groups=mesh['dp'=2,'expert'=16] {'dp'}, use_global_device_ids=true, to_apply=%region_11.12.clone | all-reduce | flops 28672 | bytes 114688
  (96 shorter events, 19.7 us)
Async XLA Ops:
  7.2 63.4 %copy-start = (bf16[256,3584]{1,0:T(8,128)(2,1)S(1)}, bf16[256,3584]{1,0:T(8,128)(2,1)}, u32[]{:S(2)}) copy-start(bf16[256,3584]{1,0:T(8,128)(2,1)} %param.30) | copy-start | bytes 5505028
  7.2 27.4 %copy-start.3 = (bf16[48,4096]{1,0:T(8,128)(2,1)S(1)}, bf16[48,4096]{1,0:T(8,128)(2,1)}, u32[]{:S(2)}) copy-start(bf16[48,4096]{1,0:T(8,128)(2,1)} %param.20) | copy-start | bytes 1179652
  10.1 13.4 %all-to-all-start.2 = ((bf16[2,1,4]{2,1,0:T(2,128)(2,1)}), bf16[2,1,4]{2,1,0:T(2,128)(2,1)S(1)}, u32[]{:S(2)}, u32[]{:S(2)}) async-start(bf16[2,1,4]{2,1,0:T(2,128)(2,1)} %all_to_all.41), calls=%async_computation.2 | async-start | bytes 2048 | tf_op jit(solution)/shard_map/all_to_all | solution.py:54
  23.5 7.4 %all-to-all-start.1 = ((bf16[2,4,4096]{2,1,0:T(4,128)(2,1)}), bf16[2,4,4096]{2,1,0:T(4,128)(2,1)S(1)}, u32[]{:S(2)}, u32[]{:S(2)}) async-start(bf16[2,4,4096]{2,1,0:T(4,128)(2,1)} %reshape.215), calls=%async_computation.1 | async-start | bytes 131072 | tf_op jit(solution)/shard_map/all_to_all | solution.py:53
  30.9 7.5 %copy-start.8 = (bf16[2,2,32,64]{3,2,1,0:T(8,128)(2,1)S(1)}, bf16[2,2,32,64]{3,2,1,0:T(8,128)(2,1)}, u32[]{:S(2)}) copy-start(bf16[2,2,32,64]{3,2,1,0:T(8,128)(2,1)} %param.26) | copy-start | bytes 49156
  30.9 10.9 %all-to-all-start = ((bf16[2,4,64,512]{3,2,1,0:T(8,128)(2,1)}), bf16[2,4,64,512]{3,2,1,0:T(8,128)(2,1)S(1)}, u32[]{:S(2)}, u32[]{:S(2)}) async-start(bf16[2,4,64,512]{3,2,1,0:T(8,128)(2,1)} %bitcast.100), calls=%async_computation | async-start | bytes 1048576 | tf_op jit(solution)/shard_map/all_to_all | solution.py:52
  34.5 124.1 %all-reduce.4.cloned.1.call-start = ((), (), s32[]{:S(2)}) async-start(), calls=%async_computation.6 | async-start | bytes 917504
  45.8 4.9 %copy-start.2 = (f32[2,2048,2,32]{1,3,2,0:T(8,128)S(1)}, f32[2,2048,2,32]{1,3,2,0:T(8,128)}, u32[]{:S(2)}) copy-start(f32[2,2048,2,32]{1,3,2,0:T(8,128)} %fusion.23) | copy-start | bytes 3145732
  45.8 4.9 %copy-start.5 = (bf16[2,2,32,512]{3,2,1,0:T(8,128)(2,1)S(1)}, bf16[2,2,32,512]{3,2,1,0:T(8,128)(2,1)}, u32[]{:S(2)}) copy-start(bf16[2,2,32,512]{3,2,1,0:T(8,128)(2,1)} %param.25) | copy-start | bytes 393220
  50.7 4.2 %copy-start.11 = (bf16[2,2,512]{2,1,0:T(2,128)(2,1)S(1)}, bf16[2,2,512]{2,1,0:T(2,128)(2,1)}, u32[]{:S(2)}) copy-start(bf16[2,2,512]{2,1,0:T(2,128)(2,1)} %param.27) | copy-start | bytes 12292
  50.7 4.4 %copy-start.1 = (bf16[64,64,512]{2,1,0:T(8,128)(2,1)S(1)}, bf16[64,64,512]{2,1,0:T(8,128)(2,1)}, u32[]{:S(2)}) copy-start(bf16[64,64,512]{2,1,0:T(8,128)(2,1)} %gather_fusion.1) | copy-start | bytes 12582916
  55.1 15.2 %copy-start.4 = (bf16[2,512,128]{2,1,0:T(8,128)(2,1)S(1)}, bf16[2,512,128]{2,1,0:T(8,128)(2,1)}, u32[]{:S(2)}) copy-start(bf16[2,512,128]{2,1,0:T(8,128)(2,1)} %param.29) | copy-start | bytes 786436
  55.1 16.7 %copy-start.14 = (u32[32]{0:T(128)S(1)}, u32[32]{0:T(128)}, u32[]{:S(2)}) copy-start(u32[32]{0:T(128)} %constant.53) | copy-start | bytes 388
  55.2 103.4 %copy-start.6 = (bf16[4,3584]{1,0:T(4,128)(2,1)S(1)}, bf16[4,3584]{1,0:T(4,128)(2,1)}, u32[]{:S(2)}) copy-start(bf16[4,3584]{1,0:T(4,128)(2,1)} %param.31) | copy-start | bytes 86020
  55.2 104.4 %copy-start.9 = (f32[3584]{0:T(1024)S(1)}, f32[3584]{0:T(1024)}, u32[]{:S(2)}) copy-start(f32[3584]{0:T(1024)} %param.32) | copy-start | bytes 43012
  55.2 104.5 %copy-start.12 = (bf16[3584,16]{0,1:T(8,128)(2,1)S(1)}, bf16[3584,16]{0,1:T(8,128)(2,1)}, u32[]{:S(2)}) copy-start(bf16[3584,16]{0,1:T(8,128)(2,1)} %param.33) | copy-start | bytes 344068
  56.1 103.7 %copy-start.10 = (s32[4,8]{1,0:T(4,128)S(1)}, s32[4,8]{1,0:T(4,128)}, u32[]{:S(2)}) copy-start(s32[4,8]{1,0:T(4,128)} %param.34) | copy-start | bytes 388
  159.6 38.1 %copy-start.7 = (bf16[4,3584]{1,0:T(4,128)(2,1)}, bf16[4,3584]{1,0:T(4,128)(2,1)S(1)}, u32[]{:S(2)}) copy-start(bf16[4,3584]{1,0:T(4,128)(2,1)S(1)} %get-tuple-element.3) | copy-start | bytes 86020
  179.3 18.3 %slice-start = ((s8[7340032]{0:T(1024)(128)(4,1)}), s8[4194304]{0:T(1024)(128)(4,1)S(1)}, s32[]{:S(2)}) async-start(s8[7340032]{0:T(1024)(128)(4,1)} %bitcast.105), calls=%async_computation.7 | async-start | bytes 8388608
  192.9 4.8 %slice-start.1 = ((s8[7340032]{0:T(1024)(128)(4,1)}), s8[3145728]{0:T(1024)(128)(4,1)S(1)}, s32[]{:S(2)}) async-start(s8[7340032]{0:T(1024)(128)(4,1)} %bitcast.105), calls=%async_computation.8 | async-start | bytes 6291456
  199.4 10.1 %copy-start.13 = (u32[32]{0:T(128)S(1)}, u32[32]{0:T(128)}, u32[]{:S(2)}) copy-start(u32[32]{0:T(128)} %constant.57) | copy-start | bytes 388
  205.4 24.9 %all-to-all-start.5 = ((bf16[16,2,4,3584]{3,2,1,0:T(4,128)(2,1)}), bf16[16,2,4,3584]{3,2,1,0:T(4,128)(2,1)S(1)}, u32[]{:S(2)}, u32[]{:S(2)}) async-start(bf16[16,2,4,3584]{3,2,1,0:T(4,128)(2,1)} %copy.58), calls=%async_computation.5 | async-start | bytes 1835008 | tf_op jit(solution)/shard_map/all_to_all | solution.py:139
Sparse Core Ops, SparseCore 0:
  72.0 86.5 all-reduce.3
where the time goes:
time: 249 us; the launch traced here: 248 us
  waiting for transfers between devices  105 us (42%)
  blocking collectives  58.6 us (24%)
  local copies, waits for them, and re-layouts  22.5 us (9%)
  matrix products  21.8 us (9%)
  starting transfers between devices  15.3 us (6%)
  between operations  15.1 us (6%)
  other arithmetic  9.05 us (4%)
    unnamed x2, waiting for transfers between devices  85.5 us
    all_to_all x1, blocking collectives, body(): lax.all_to_all(send_rows, 'expert', split_axis=0, concat_axis=0, tiled=True)  18.1 us
    all_to_all x1, waiting for transfers between devices, body(): lax.all_to_all(partial_out.astype(jnp.bfloat16), 'expert', split_axis=0,...  15.8 us
    all_to_all x1, blocking collectives, body(): lax.all_to_all(latent_out, 'expert', split_axis=2, concat_axis=0, tiled=T...  13.9 us
    all_gather x1, blocking collectives, body(): grouped = lax.all_gather(arrived, 'dp', axis=1, tiled=True)  13.5 us
    unnamed x1, blocking collectives  8.71 us
    gather x4, local copies, waits for them, and re-layouts, body(): sent = (cache_lat[picked], cache_rope[picked], page_scale[picked])  6.9 us
  transfers between devices with their start and end apart: 5, of which 4 were waited for; matrix products, arithmetic and copies ran while one was open for 7% of the time, Pallas kernels for 0%

commit v1 on v0

v1 whole, which is shorter than its diff:
```python
import functools

import jax
import jax.numpy as jnp
from jax import lax
from jax.experimental import pallas as pl
from jax.experimental.pallas import tpu as pltpu
from jax.sharding import Mesh, PartitionSpec as P

SCORE_SCALE = 0.07216878364870322
ROUTE_SCALE = 2.5
NORM_EPS = 1e-06
LOW = -1e30
LANES = 128
MIB = 1 << 20
BF16 = jnp.bfloat16
F32 = jnp.float32
VMEM = pl.BlockSpec(memory_space=pltpu.VMEM)
SMEM = pl.BlockSpec(memory_space=pltpu.SMEM)
ANY = pl.BlockSpec(memory_space=pl.ANY)
HBM = pl.BlockSpec(memory_space=pltpu.HBM)
DP = ("top", "low")
EXPERT = ("far", "side", "core")
ROWS = DP + EXPERT
FAR = ("low", "far")
LOAD_MIB = 28


def dot_nt(a, b):
    return lax.dot_general(a, b, (((1,), (1,)), ((), ())), preferred_element_type=F32)


def dot_tn(a, b):
    return lax.dot_general(a, b, (((0,), (0,)), ((), ())), preferred_element_type=F32)


def dot_nn(a, b):
    return jnp.dot(a, b, preferred_element_type=F32)


def call(kernel, outs, operands, in_specs=None, out_specs=None, scratch=(), vmem=16, cost=None):
    flops, moved = cost or (0, 0)
    return pl.pallas_call(
        kernel,
        out_shape=outs,
        in_specs=in_specs or [VMEM] * len(operands),
        out_specs=out_specs or [VMEM] * len(outs),
        scratch_shapes=list(scratch),
        compiler_params=pltpu.CompilerParams(vmem_limit_bytes=vmem * MIB),
        cost_estimate=pl.CostEstimate(flops=flops, bytes_accessed=moved, transcendentals=0),
    )(*operands)


def shape(dims, dtype):
    return jax.ShapeDtypeStruct(dims, dtype)


def iota(dims, axis):
    return lax.broadcasted_iota(jnp.int32, dims, axis)


def fetch(copies):
    for copy in copies:
        copy.start()
    return copies


def pick_kernel(partners, moves, move_hbm, scale_ref, lat, rope_hbm, *rest):
    lat_outs, rope_outs = rest[:partners], rest[partners : 2 * partners]
    scale_out, move, rope, wide_scale, lat_sems, sems = rest[2 * partners :]
    slots, width = rope.shape
    half = width // 2
    me = lax.axis_index(DP)
    get_move, get_rope = fetch(
        [
            pltpu.make_async_copy(move_hbm, move, sems.at[0]),
            pltpu.make_async_copy(rope_hbm, rope, sems.at[1]),
        ]
    )
    wide_scale[...] = scale_ref[...].astype(F32)
    (put_scale,) = fetch([pltpu.make_async_copy(wide_scale, scale_out, sems.at[2])])
    get_move.wait()
    copies = []
    for k in range(partners):
        for m in range(moves):
            copies.append(
                pltpu.make_async_copy(
                    lat.at[move[0, me ^ (k + 1), m]], lat_outs[k].at[m], lat_sems.at[k, m]
                )
            )
    fetch(copies)
    put_scale.wait()
    get_rope.wait()
    row = iota((2 * moves, 1), 0)
    column = iota((2 * moves, slots), 1)
    for k in range(partners):
        target = jnp.zeros((2 * moves, 1), jnp.int32)
        factor = jnp.zeros((2 * moves, 1), F32)
        for m in range(moves):
            page = move[0, me ^ (k + 1), m]
            target = jnp.where(row // 2 == m, page, target)
            factor = jnp.where(row // 2 == m, scale_out[page], factor)
        hit = column == target
        even = row % 2 == 0
        first = jnp.where(hit & even, 1.0, 0.0).astype(BF16)
        second = jnp.where(hit & (~even), 1.0, 0.0).astype(BF16)
        both = dot_nn(first, rope[:, :half]) + dot_nn(second, rope[:, half:])
        rope_outs[k][:, :half] = both.astype(BF16)
        rope_outs[k][:, half:] = jnp.broadcast_to(factor, (2 * moves, LANES)).astype(BF16)
    for copy in copies:
        copy.wait()


def spread(scores, start, count, stride, part):
    for b in range(scores.shape[0]):
        scores.at[b][pl.ds(start, count, stride=stride), :] = part[:, b * LANES : (b + 1) * LANES]


def read(scores, span):
    parts = [scores[b, span, :] for b in range(scores.shape[0])]
    return parts[0] if len(parts) == 1 else jnp.concatenate(parts, axis=1)


def write(scores, span, part):
    for b in range(scores.shape[0]):
        scores[b, span, :] = part[:, b * LANES : (b + 1) * LANES]


GROUP = 8


def local_kernel(
    sizes,
    partners,
    scale,
    table_hbm,
    lengths_hbm,
    move_hbm,
    lat_hbm,
    rope_hbm,
    q_hbm,
    turn_hbm,
    new_lat_hbm,
    new_rope_hbm,
    acc_out,
    peak_out,
    total_out,
    qrel_out,
    q2_out,
    limit_out,
    table,
    lengths,
    move,
    lat,
    rope,
    q_lat,
    q_rope,
    new_lat,
    new_rope,
    scores,
    limits,
    new_keys,
    new_turns,
    sems,
    lat_sems,
):
    heads, per_device, rollouts, following, view = sizes
    slots, page_len, latent = lat.shape
    rows = rollouts * following * heads
    rope_dim = q_rope.shape[3]
    moves = move.shape[2]
    me = lax.axis_index(DP)
    pairs = (
        (table_hbm, table),
        (lengths_hbm, lengths),
        (move_hbm, move),
        (rope_hbm, rope),
        (turn_hbm, q_rope),
        (q_hbm, q_lat),
        (new_lat_hbm, new_lat),
        (new_rope_hbm, new_rope),
    )
    small = fetch(
        [pltpu.make_async_copy(src, dst, sems.at[i]) for i, (src, dst) in enumerate(pairs)]
    )
    chunks = fetch(
        [
            pltpu.make_async_copy(
                lat_hbm.at[pl.ds(at, GROUP)], lat.at[pl.ds(at, GROUP)], lat_sems.at[at // GROUP]
            )
            for at in range(0, slots, GROUP)
        ]
    )
    place = iota((rows, rows), 0)
    rollout = (place // following) % rollouts
    token = place % following
    head = place // (following * rollouts)
    source = (rollout * following + token) * heads + head
    order = jnp.where(iota((rows, rows), 1) == source, 1.0, 0.0).astype(BF16)
    at = iota((rope_dim, 2 * rope_dim), 1)
    frm = iota((rope_dim, 2 * rope_dim), 0)
    for copy in small:
        copy.wait()
    for slot in range(rollouts * view):
        limits[slot] = 0
    for r in range(rollouts):
        for a in range(table.shape[1]):
            live = jnp.clip(lengths[r] - a * page_len, 0, page_len)
            limits[r * view + table[r, a]] = live
    q_turn = dot_nn(order, q_rope[...].reshape(rows, rope_dim)).astype(BF16)
    q2_out[:rows, :] = dot_nn(q_turn, jnp.where(at == frm, 1.0, 0.0).astype(BF16)).astype(BF16)
    q2_out[rows:, :] = dot_nn(
        q_turn, jnp.where(at == frm + rope_dim, 1.0, 0.0).astype(BF16)
    ).astype(BF16)
    qrel_out[...] = dot_nn(order, q_lat[...].reshape(rows, latent)).astype(BF16)
    twos = page_len // 2
    wide = 2 * rope_dim
    stacked = jnp.concatenate([rope[:, c * wide : (c + 1) * wide] for c in range(twos)], axis=0)
    turned = dot_nt(stacked, q2_out[...])
    for c in range(twos):
        part = turned[c * slots : (c + 1) * slots]
        spread(scores, 2 * c, slots, page_len, part[:, :rows])
        spread(scores, 2 * c + 1, slots, page_len, part[:, rows:])

    lane_rollout = (iota((1, rows), 1) // following) % rollouts
    lane_token = iota((1, rows), 1) % following
    position = iota((page_len, rows), 0)

    def limit_row(slot):
        row = jnp.full(lane_rollout.shape, limits[slot], jnp.int32)
        for r in range(1, rollouts):
            row = jnp.where(lane_rollout == r, limits[r * view + slot], row)
        return row

    for k in range(partners):
        for m in range(moves):
            limit_out[k * moves + m : k * moves + m + 1, :] = limit_row(
                slots + (me ^ (k + 1)) * moves + m
            )
    queries = qrel_out[...]
    fresh_rows = rollouts * following
    new_keys[...] = jnp.zeros(new_keys.shape, F32)
    new_turns[...] = jnp.zeros(new_turns.shape, F32)
    for r in range(rollouts):
        span = slice(r * following, (r + 1) * following)
        new_keys[span, :] = new_lat[r].astype(F32)
        new_turns[span, :rope_dim] = new_rope[r].astype(F32)
    fresh_keys = new_keys[...].astype(BF16)
    new_part = dot_nt(fresh_keys, queries) + dot_nt(
        new_turns[...].astype(BF16), q2_out[:rows, :]
    )
    new_row = iota(new_part.shape, 0)
    seen = (new_row // following == lane_rollout) & (new_row % following <= lane_token)
    new_part = jnp.where(seen & (new_row < fresh_rows), new_part * SCORE_SCALE, LOW)

    best = jnp.full((page_len, rows), LOW, F32)
    for first in range(0, slots, GROUP):
        chunks[first // GROUP].wait()
        keys = lat[first : first + GROUP].reshape(GROUP * page_len, latent)
        fresh = dot_nt(keys, queries)
        for g in range(GROUP):
            page = first + g
            span = pl.ds(page * page_len, page_len)
            part = fresh[g * page_len : (g + 1) * page_len] + read(scores, span)
            part = part * (scale[page] * SCORE_SCALE)
            write(scores, span, part)
            best = jnp.maximum(best, jnp.where(position < limit_row(page), part, LOW))
    for m in range(moves):
        page = move[0, me, m]
        part = read(scores, pl.ds(pl.multiple_of(page * page_len, page_len), page_len))
        live = position < limit_row(slots + me * moves + m)
        best = jnp.maximum(best, jnp.where(live, part, LOW))
    peak = jnp.max(best, axis=0, keepdims=True)
    peak = jnp.maximum(peak, jnp.max(new_part, axis=0, keepdims=True))

    def weigh(part, slot, factor, total):
        grown = jnp.where(position < limit_row(slot), jnp.exp(part - peak), 0.0)
        return (grown * factor).astype(BF16), total + grown

    new_exp = jnp.exp(new_part - peak)
    total = jnp.zeros((page_len, rows), F32)
    acc = dot_tn(new_exp.astype(BF16), fresh_keys)
    for first in range(0, slots, GROUP):
        weights = []
        for g in range(GROUP):
            page = first + g
            part = read(scores, pl.ds(page * page_len, page_len))
            weight, total = weigh(part, page, scale[page], total)
            weights.append(weight)
        keys = lat[first : first + GROUP].reshape(GROUP * page_len, latent)
        acc = acc + dot_tn(jnp.concatenate(weights, axis=0), keys)
    weights, keys = [], []
    for m in range(moves):
        page = move[0, me, m]
        part = read(scores, pl.ds(pl.multiple_of(page * page_len, page_len), page_len))
        weight, total = weigh(part, slots + me * moves + m, scale[page], total)
        weights.append(weight)
        keys.append(lat[page])
    acc = acc + dot_tn(jnp.concatenate(weights, axis=0), jnp.concatenate(keys, axis=0))
    acc_out[...] = acc
    peak_out[...] = jnp.broadcast_to(peak, peak_out.shape)
    whole = jnp.sum(total, axis=0, keepdims=True) + jnp.sum(new_exp, axis=0, keepdims=True)
    total_out[...] = jnp.broadcast_to(whole, total_out.shape)


def merge_kernel(partners, *refs):
    count = 2 * partners + 6
    sources, out, held = refs[:count], refs[count], refs[count + 1 : 2 * count + 1]
    scores, sems = refs[2 * count + 1 :]
    copies = fetch(
        [
            pltpu.make_async_copy(src, dst, sems.at[i])
            for i, (src, dst) in enumerate(zip(sources, held))
        ]
    )
    for copy in copies:
        copy.wait()
    got_lat, got_rope = held[:partners], held[partners : 2 * partners]
    acc_in, peak_in, total_in, qrel, q2, limit = held[2 * partners :]
    moves, page_len, latent = got_lat[0].shape
    rows = qrel.shape[0]
    wide = q2.shape[1]
    position = iota((page_len, rows), 0)
    queries = qrel[...]
    best = jnp.full((page_len, rows), LOW, F32)
    half_lanes = got_rope[0].shape[1] - LANES
    pieces = half_lanes // wide
    span = moves * page_len
    factors = []
    for k in range(partners):
        turns = got_rope[k]
        stacked = jnp.concatenate(
            [turns[:, c * wide : (c + 1) * wide].astype(F32) for c in range(pieces)], axis=0
        ).astype(BF16)
        turned = dot_nt(stacked, q2[...])
        base = k * span
        for c in range(pieces):
            part = turned[c * 2 * moves : (c + 1) * 2 * moves]
            spread(scores, base + 2 * c, 2 * moves, page_len // 2, part[:, :rows])
            spread(scores, base + 2 * c + 1, 2 * moves, page_len // 2, part[:, rows:])
        fresh = dot_nt(got_lat[k][...].reshape(span, latent), queries)
        marks = turns[:, half_lanes:].astype(F32)
        for m in range(moves):
            factor = marks[2 * m : 2 * m + 1, :1]
            factors.append(factor)
            where_at = pl.ds(base + m * page_len, page_len)
            part = fresh[m * page_len : (m + 1) * page_len] + read(scores, where_at)
            part = part * (factor * SCORE_SCALE)
            at = k * moves + m
            part = jnp.where(position < limit[at : at + 1, :], part, LOW)
            write(scores, where_at, part)
            best = jnp.maximum(best, part)
    peak_local = peak_in[:1, :]
    peak = jnp.maximum(jnp.max(best, axis=0, keepdims=True), peak_local)
    shrink = jnp.exp(peak_local - peak)
    acc = jnp.zeros((rows, latent), F32)
    grown_sum = jnp.zeros((page_len, rows), F32)
    for k in range(partners):
        weights = []
        for m in range(moves):
            part = read(scores, pl.ds(k * span + m * page_len, page_len))
            grown = jnp.exp(part - peak)
            grown_sum = grown_sum + grown
            weights.append((grown * factors[k * moves + m]).astype(BF16))
        acc = acc + dot_tn(
            jnp.concatenate(weights, axis=0), got_lat[k][...].reshape(span, latent)
        )
    total = total_in[:1, :] * shrink + jnp.sum(grown_sum, axis=0, keepdims=True)

    def upright(row):
        return jnp.transpose(jnp.broadcast_to(row, (LANES, rows)))[:, :1]

    result = (acc_in[...] * upright(shrink) + acc) / upright(total)
    out[...] = result.reshape(out.shape).astype(BF16)


def project_kernel(tokens, blocks, w_uv, w_out, away, kept):
    devices = blocks.shape[0]
    per_device = w_uv.shape[0]
    core = lax.axis_index("core")
    stacked = blocks[...].astype(F32).reshape(-1, blocks.shape[2]).astype(BF16)
    rows = stacked.shape[0]
    row_head = (iota((rows, 1), 0) // tokens) % per_device
    values = []
    for head in range(per_device):
        part = dot_nn(stacked, w_uv[head])
        values.append(jnp.where(row_head == head, part, 0.0).astype(BF16))
    values = jnp.concatenate(values, axis=1)
    half = devices // 2 * tokens
    out_row = iota((2 * half, rows), 0)
    in_row = iota((2 * half, rows), 1)
    out_device = (out_row % half) // tokens * 2 + jnp.where(out_row < half, 1 - core, core)
    same = (in_row // (tokens * per_device) == out_device) & (in_row % tokens == out_row % tokens)
    joined = dot_nn(jnp.where(same, 1.0, 0.0).astype(BF16), values).astype(BF16)
    width = w_out.shape[1]
    step = 512 if width % 512 == 0 else width
    for at in range(0, width, step):
        part = dot_nn(joined, w_out[:, at : at + step])
        away[:, at : at + step] = part[:half].astype(BF16)
        kept[:, at : at + step] = part[half:]


def split_kernel(kept, got, out):
    total = kept[...] + got[...].astype(F32)
    out[...] = total.reshape(out.shape).astype(BF16)


def norm_kernel(got, residual, gain, routes, attn_out, out):
    total = jnp.sum(got[...].astype(F32), axis=0)
    attn_out[...] = total.astype(BF16)
    hidden = (residual[...].astype(F32) + total).astype(BF16).astype(F32)
    width = hidden.shape[1]
    power = jnp.sum(hidden * hidden, axis=1, keepdims=True) / width
    normed = (hidden * lax.rsqrt(power + NORM_EPS) * gain[...].reshape(1, width)).astype(BF16)
    named = routes[...].astype(F32).astype(BF16)
    for copy in range(out.shape[0]):
        out[copy, :, :width] = normed
        out[copy, :, width:] = jnp.zeros((hidden.shape[0], LANES), BF16)
        out[copy, :, width : width + routes.shape[1]] = named


def load_kernel(count, passed, *refs):
    sources, passed_out, outs, sems = refs[:count], refs[count], refs[count + 1 : -1], refs[-1]
    split = sems.shape[1]
    copies = []
    for k, (source, out) in enumerate(zip(sources, outs)):
        step = out.shape[0] // split
        for i in range(split):
            span = pl.ds(i * step, step)
            copies.append(
                pltpu.make_async_copy(source.at[0, span], out.at[span], sems.at[k, i])
            )
    fetch(copies)
    passed_out[...] = passed[...]
    for copy in copies:
        copy.wait()


def expert_kernel(top, count, *refs):
    pieces = refs[:count]
    w_router, w_gate, w_up, w_down = refs[count : count + 4]
    kept, away, rows_ref, hidden_ref = refs[count + 4 :]
    expert = lax.axis_index(EXPERT)
    width, units = w_gate.shape
    in_step = 256 if units % 256 == 0 else units
    out_step = 512 if width % 512 == 0 else width
    piece_rows = rows_ref.shape[0] // count
    named = []
    for k, piece in enumerate(pieces):
        whole = piece[...].astype(F32).reshape(piece_rows, -1)
        rows_ref[k * piece_rows : (k + 1) * piece_rows, :] = whole[:, :width].astype(BF16)
        named.append(whole[:, width:])
    named = jnp.concatenate(named, axis=0)
    rows = rows_ref[...]
    logits = dot_nt(rows, w_router[...])
    experts = iota(logits.shape, 1)
    chosen = jnp.zeros(logits.shape, F32)
    for k in range(top):
        route = named[:, k : k + 1].astype(jnp.int32)
        chosen = chosen + jnp.where(route == experts, 1.0, 0.0)
    sig = jax.nn.sigmoid(logits) * chosen
    mine = jnp.sum(jnp.where(experts == expert, sig, 0.0), axis=1, keepdims=True)
    gates = ROUTE_SCALE * mine / jnp.sum(sig, axis=1, keepdims=True)
    for at in range(0, units, in_step):
        gate = dot_nn(rows, w_gate[:, at : at + in_step])
        up = dot_nn(rows, w_up[:, at : at + in_step])
        hidden_ref[:, at : at + in_step] = (gate / (1.0 + jnp.exp(-gate)) * up).astype(BF16)
    hidden = hidden_ref[...]
    half = rows_ref.shape[0] // 2
    for at in range(0, width, out_step):
        part = dot_nn(hidden, w_down[:, at : at + out_step]) * gates
        kept[:, at : at + out_step] = part[:half]
        away[:, at : at + out_step] = part[half:].astype(BF16)


def halve_kernel(kept, got, keep, away):
    total = kept[...] + got[...].astype(F32)
    half = total.shape[0] // 2
    keep[...] = total[:half]
    away[...] = total[half:].astype(BF16)


def sum_kernel(got, out):
    out[...] = jnp.sum(got[...].astype(F32), axis=0).astype(BF16)


def body(dp_count, expert_count, *arrays):
    (
        cache_lat,
        cache_rope,
        page_scale,
        move_list,
        page_table,
        lengths,
        q_lat,
        q_rope,
        new_lat,
        new_rope,
        w_uv,
        w_out,
        residual,
        norm_gain,
        w_router,
        routes,
        w_gate,
        w_up,
        w_down,
    ) = arrays
    total_devices = dp_count * expert_count
    top_bit = total_devices // 2
    side_bit = 2

    def swap(x, mask, mask_odd=None):
        pairs = []
        for i in range(total_devices):
            other = mask if mask_odd is None or i % 2 == 0 else mask_odd
            pairs.append((i, i ^ other))
        return lax.ppermute(x, ROWS, pairs)

    def deal(x, names):
        return lax.all_to_all(x, names, split_axis=0, concat_axis=0, tiled=True)

    slots, page_len, latent = cache_lat.shape
    moves = move_list.shape[2]
    rollouts, following, heads, rope_dim = q_rope.shape
    view = slots + dp_count * moves
    per_device = heads // expert_count
    tokens = rollouts * following
    width = residual.shape[1]
    partners = dp_count - 1
    rows = tokens * heads
    sizes = (heads, per_device, rollouts, following, view)

    picked = call(
        functools.partial(pick_kernel, partners, moves),
        [shape((moves, page_len, latent), BF16)] * partners
        + [shape((2 * moves, cache_rope.shape[1] // 2 + LANES), BF16)] * partners
        + [shape((slots,), F32)],
        (move_list, page_scale, cache_lat, cache_rope),
        in_specs=[HBM, VMEM, HBM, HBM],
        out_specs=[VMEM] * (2 * partners) + [SMEM],
        scratch=[
            pltpu.SMEM(move_list.shape, jnp.int32),
            pltpu.VMEM(cache_rope.shape, BF16),
            pltpu.VMEM((slots,), F32),
            pltpu.SemaphoreType.DMA((partners, moves)),
            pltpu.SemaphoreType.DMA((3,)),
        ],
        vmem=60,
    )
    got_lat = [swap(picked[k], (k + 1) * expert_count) for k in range(partners)]
    got_rope = [swap(picked[partners + k], (k + 1) * expert_count) for k in range(partners)]

    local = call(
        functools.partial(local_kernel, sizes, partners),
        [
            shape((rows, latent), F32),
            shape((8, rows), F32),
            shape((8, rows), F32),
            shape((rows, latent), BF16),
            shape((2 * rows, 2 * rope_dim), BF16),
            shape((-(-partners * moves // 8) * 8, rows), jnp.int32),
        ],
        (
            picked[-1],
            page_table,
            lengths,
            move_list,
            cache_lat,
            cache_rope,
            q_lat,
            q_rope,
            new_lat,
            new_rope,
        ),
        in_specs=[SMEM] + [HBM] * 9,
        scratch=[
            pltpu.SMEM(page_table.shape, jnp.int32),
            pltpu.SMEM(lengths.shape, jnp.int32),
            pltpu.SMEM(move_list.shape, jnp.int32),
            pltpu.VMEM(cache_lat.shape, BF16),
            pltpu.VMEM(cache_rope.shape, BF16),
            pltpu.VMEM(q_lat.shape, BF16),
            pltpu.VMEM(q_rope.shape, BF16),
            pltpu.VMEM(new_lat.shape, BF16),
            pltpu.VMEM(new_rope.shape, BF16),
            pltpu.VMEM((rows // LANES, slots * page_len, LANES), F32),
            pltpu.SMEM((rollouts * view,), jnp.int32),
            pltpu.VMEM((16, latent), F32),
            pltpu.VMEM((16, 2 * rope_dim), F32),
            pltpu.SemaphoreType.DMA((8,)),
            pltpu.SemaphoreType.DMA((slots // GROUP,)),
        ],
        vmem=60,
        cost=(2 * slots * page_len * rows * (2 * latent + 2 * rope_dim), 4 * MIB),
    )
    operands = (*got_lat, *got_rope, *local)
    blocks = call(
        functools.partial(merge_kernel, partners),
        [shape((expert_count, tokens * per_device, latent), BF16)],
        operands,
        in_specs=[HBM] * len(operands),
        scratch=[pltpu.VMEM(x.shape, x.dtype) for x in operands]
        + [
            pltpu.VMEM((rows // LANES, partners * moves * page_len, LANES), F32),
            pltpu.SemaphoreType.DMA((len(operands),)),
        ],
        vmem=60,
        cost=(2 * moves * page_len * rows * 2 * latent, MIB),
    )[0]
    blocks = deal(blocks, EXPERT)

    half_rows = expert_count // 2 * tokens
    away, kept = call(
        functools.partial(project_kernel, tokens),
        [shape((half_rows, width), BF16), shape((half_rows, width), F32)],
        (blocks, w_uv, w_out),
        cost=(4 * half_rows * width * w_out.shape[0], 4 * MIB),
    )
    parts = call(
        split_kernel,
        [shape((expert_count // 2, tokens, width), BF16)],
        (kept, swap(away, 1)),
    )[0]
    parts = deal(parts, ("far", "side"))
    far_count = total_devices // 8
    attn_out, own_rows = call(
        norm_kernel,
        [shape((tokens, width), BF16), shape((far_count, tokens, width + LANES), BF16)],
        (parts, residual, norm_gain, routes),
    )

    def load(passed, sources, vmem):
        return call(
            functools.partial(load_kernel, len(sources)),
            [shape(passed.shape, BF16)] + [shape(w.shape[1:], BF16) for w in sources],
            (passed, *sources),
            in_specs=[VMEM] + [HBM] * len(sources),
            scratch=[pltpu.SemaphoreType.DMA((len(sources), 8))],
            vmem=vmem,
            cost=(0, 2 * sum(w.size for w in sources)),
        )

    piece = deal(own_rows, FAR)
    pieces = [piece, swap(piece, top_bit, side_bit)]
    pieces = pieces + [swap(p, side_bit, top_bit) for p in pieces]
    side_piece, *weights = load(pieces[1], (w_gate, w_up, w_down), LOAD_MIB)
    pieces = [piece, side_piece] + pieces[2:]
    pieces = pieces + [swap(p, 1) for p in pieces]

    all_rows = total_devices * tokens
    hidden_units = w_gate.shape[2]
    half = all_rows // 2
    kept, away = call(
        functools.partial(expert_kernel, routes.shape[1], len(pieces)),
        [shape((half, width), F32), shape((half, width), BF16)],
        (*pieces, w_router.T, *weights),
        scratch=[
            pltpu.VMEM((all_rows, width), BF16),
            pltpu.VMEM((all_rows, hidden_units), BF16),
        ],
        vmem=16 if all_rows <= 256 else 56,
        cost=(6 * all_rows * width * hidden_units, 6 * width * hidden_units),
    )

    got = swap(away, 1)
    kept, away = call(
        halve_kernel,
        [shape((half // 2, width), F32), shape((half // 2, width), BF16)],
        (kept, got),
    )
    got = swap(away, side_bit, top_bit)
    kept, away = call(
        halve_kernel,
        [shape((half // 4, width), F32), shape((half // 4, width), BF16)],
        (kept, got),
    )
    got = swap(away, top_bit, side_bit)
    parts = call(split_kernel, [shape((far_count, tokens, width), BF16)], (kept, got))[0]
    moe_out = call(sum_kernel, [shape((tokens, width), BF16)], (deal(parts, FAR),))[0]
    return (attn_out, moe_out)


def solution(mesh):
    dp_count, expert_count = mesh.shape["dp"], mesh.shape["expert"]
    finer = Mesh(mesh.devices.reshape(2, dp_count // 2, expert_count // 4, 2, 2), ROWS)
    return jax.shard_map(
        functools.partial(body, dp_count, expert_count),
        mesh=finer,
        in_specs=(
            P(ROWS, None, None),
            P(ROWS, None),
            P(ROWS),
            P(ROWS, None, None),
            P(ROWS, None),
            P(ROWS),
            P(ROWS, None, None, None),
            P(ROWS, None, None, None),
            P(ROWS, None, None),
            P(ROWS, None, None),
            P(EXPERT, None, None),
            P(EXPERT, None),
            P(ROWS, None),
            P(),
            P(),
            P(ROWS, None),
            P(EXPERT, None, DP),
            P(EXPERT, None, DP),
            P(EXPERT, DP, None),
        ),
        out_specs=(P(ROWS, None), P(ROWS, None)),
        check_vma=False,
    )
```

time: 249 us -> 96.9 us (0.39)
  waiting for transfers between devices: 105 us -> 14.7 us
  Pallas kernels: 0 us -> 26.9 us
  matrix products: 21.8 us -> 0 us
  local copies, waits for them, and re-layouts: 22.5 us -> 0.71 us
  blocking collectives: 58.6 us -> 42.3 us
  between operations: 15.1 us -> 0.78 us
  other arithmetic: 9.05 us -> 0 us
  starting transfers between devices: 15.3 us -> 11.1 us
    unnamed x2 -> x0, waiting for transfers between devices: 85.5 us -> none
    pallas_call x0 -> x12, Pallas kernels: none -> 26.9 us  [call(): pl.pallas_call(kernel, out_shape=outs, in_specs=in_specs or [VMEM] * len(...]
    dot_general x14 -> x0, matrix products: 21.8 us -> none  [the longest x1 4.76 us: body(): jnp.dot(flat_rows, w_gate[0], preferred_element_type=jnp.float32)]
    all_to_all x4 -> x0, waiting for transfers between devices: 19.9 us -> none  [the longest x1 15.8 us: body(): lax.all_to_all(partial_out.astype(jnp.bfloat16), 'expert', split_axis=0,...]
    all_gather x2 -> x0, blocking collectives: 17.9 us -> none  [the longest x1 13.5 us: body(): grouped = lax.all_gather(arrived, 'dp', axis=1, tiled=True)]
    all_to_all x4 -> x0, starting transfers between devices: 15.2 us -> none  [the longest x1 4.21 us: body(): lax.all_to_all(sent[2], 'dp', split_axis=0, concat_axis=0, tiled=True)]
    ppermute x0 -> x13, waiting for transfers between devices: none -> 14.7 us  [swap(): return lax.ppermute(x, ROWS, pairs)]
    gather x7 -> x0, local copies, waits for them, and re-layouts: 14.2 us -> none  [the longest x4 6.9 us: body(): sent = (cache_lat[picked], cache_rope[picked], page_scale[picked])]
  transfers between devices with their start and end apart: 5 -> 13, of which waited for: 4 -> 7; matrix products, arithmetic and copies ran while one was open for 7% -> 0% of each run, Pallas kernels for 0% -> 16%
where the time goes in v1:
time: 96.9 us; the launch traced here: 96.5 us
  blocking collectives  42.3 us (44%)
  Pallas kernels  26.9 us (28%)
  waiting for transfers between devices  14.7 us (15%)
  starting transfers between devices  11.1 us (11%)
    all_to_all x4, blocking collectives, deal(): return lax.all_to_all(x, names, split_axis=0, concat_axis=0, tiled=True)  42.3 us
    pallas_call x12, Pallas kernels, call(): pl.pallas_call(kernel, out_shape=outs, in_specs=in_specs or [VMEM] * len(...  26.9 us
    ppermute x13, waiting for transfers between devices, swap(): return lax.ppermute(x, ROWS, pairs)  14.7 us
    ppermute x13, starting transfers between devices, swap(): return lax.ppermute(x, ROWS, pairs)  11.1 us
  transfers between devices with their start and end apart: 13, of which 7 were waited for; matrix products, arithmetic and copies ran while one was open for 0% of the time, Pallas kernels for 16%

profile of v1, /device:TPU:0, one launch (start us, length us, event | category | flops | bytes accessed | tf_op | source)
XLA Modules:
  0.0 96.5 jit_solution(1567488748004619870)
XLA Ops:
  0.7 3.2 %shard_map.194 = (bf16[4,64,512]{2,1,0:T(8,128)(2,1)}, bf16[8,2176]{1,0:T(8,128)(2,1)}, f32[48]{0:T(128)}) custom-call(s32[1,2,4]{2,1,0:T(2,128)} %move_hbm.3, bf16[48]{0:T(256)(128)(2,1)} %scale_ref.1, bf16[48,64,512]{2,1,0:T(8,128)(2,1)} %lat_hbm.1, bf16[48,4096]{1,0:T(8,128)(2,1)} %rope_hbm.3), custom_call_target="tpu_custom_call" | custom-call | tf_op jit(solution)/shard_map/pallas_call | solution.py:43
  3.9 3.0 %collective-permute-start = (bf16[4,64,512]{2,1,0:T(8,128)(2,1)}, bf16[4,64,512]{2,1,0:T(8,128)(2,1)S(1)}, u32[]{:S(2)}, u32[]{:S(2)}) collective-permute-start(bf16[4,64,512]{2,1,0:T(8,128)(2,1)} %get-tuple-element.25), channel_id=1, source_target_pairs={{0,16},{1,17},{2,18},{3,19},{4,20},{5,21},{6,22},{7,23},{8,24},{9,... | collective-permute-start | bytes 786440 | tf_op jit(solution)/shard_map/ppermute | solution.py:518
  7.0 7.6 %shard_map.195 = (f32[128,512]{1,0:T(8,128)}, f32[8,128]{1,0:T(8,128)}, f32[8,128]{1,0:T(8,128)}, bf16[128,512]{1,0:T(8,128)(2,1)}, bf16[256,128]{1,0:T(8,128)(2,1)}, /*index=5*/s32[8,128]{1,0:T(8,128)}) custom-call(f32[48]{0:T(128)} %get-tuple-element.27.scale, s32[2,32]{1,0:T(2,128)} %table_hbm.1, s32[2]{0:T(128)} %lengths_hbm.1, s32[1,2,4]{2,1,0:T(2,128)} %move_hbm.3, ...), custom_call_target="tpu_custom_call" | custom-call | flops 905969664 | bytes 4194304 | tf_op jit(solution)/shard_map/pallas_call | solution.py:43
  15.4 2.4 %shard_map.196 = bf16[16,8,512]{2,1,0:T(8,128)(2,1)} custom-call(bf16[4,64,512]{2,1,0:T(8,128)(2,1)} %copy-done.6, bf16[8,2176]{1,0:T(8,128)(2,1)} %copy-done.7, f32[128,512]{1,0:T(8,128)} %get-tuple-element.28.refs_2_, f32[8,128]{1,0:T(8,128)} %get-tuple-element.29.refs_3_, f32[8,128]{1,0:T(8,128)} %get-tuple-element.30.refs_4_, ...), custom_call_target="tpu_custom_call" | custom-call | flops 67108864 | bytes 1048576 | tf_op jit(solution)/shard_map/pallas_call | solution.py:43
  17.7 14.3 %all_to_all.20.blocks = bf16[16,8,512]{2,1,0:T(8,128)(2,1)S(1)} all-to-all(bf16[16,8,512]{2,1,0:T(8,128)(2,1)} %shard_map.196), channel_id=1, replica_groups=mesh['top'=2,'low'=1,'far'=4,'side'=2,'core'=2] {'far','side','core'}, dimensions={0} | all-to-all | bytes 262144 | tf_op jit(solution)/shard_map/all_to_all | solution.py:521
  32.1 0.8 shard_map.197
  32.9 1.5 %collective-permute-done.2.got = bf16[32,3584]{1,0:T(8,128)(2,1)S(1)} collective-permute-done((bf16[32,3584]{1,0:T(8,128)(2,1)S(1)}, bf16[32,3584]{1,0:T(8,128)(2,1)S(1)}, u32[]{:S(2)}, u32[]{:S(2)}) %collective-permute-start.2) | collective-permute-done | bytes 229408 | tf_op jit(solution)/shard_map/ppermute | solution.py:518
  34.5 11.4 %all_to_all.21.got = bf16[8,4,3584]{2,1,0:T(4,128)(2,1)S(1)} all-to-all(bf16[8,4,3584]{2,1,0:T(4,128)(2,1)S(1)} %shard_map.198), channel_id=1, replica_groups=mesh['top'=2,'low'=1,'far'=4,'side'=2,'core'=2] {'far','side'}, dimensions={0} | all-to-all | bytes 458752 | tf_op jit(solution)/shard_map/all_to_all | solution.py:521
  45.9 0.7 shard_map.199
  46.7 8.3 %all_to_all.22.refs_0_ = bf16[4,4,3712]{2,1,0:T(4,128)(2,1)S(1)} all-to-all(bf16[4,4,3712]{2,1,0:T(4,128)(2,1)S(1)} %get-tuple-element.37), channel_id=1, replica_groups=mesh['top'=2,'low'=1,'far'=4,'side'=2,'core'=2] {'low','far'}, dimensions={0} | all-to-all | bytes 237568 | tf_op jit(solution)/shard_map/all_to_all | solution.py:521
  54.9 1.5 %collective-permute-start.3 = (bf16[4,4,3712]{2,1,0:T(4,128)(2,1)S(1)}, bf16[4,4,3712]{2,1,0:T(4,128)(2,1)S(1)}, u32[]{:S(2)}, u32[]{:S(2)}) collective-permute-start(bf16[4,4,3712]{2,1,0:T(4,128)(2,1)S(1)} %all_to_all.22.refs_0_), channel_id=1, source_target_pairs={{0,16},{1,3},{2,18},{3,1},{4,20},{5,7},{6,22},{7,5},{8,24},{9,11},... | collective-permute-start | bytes 356360 | tf_op jit(solution)/shard_map/ppermute | solution.py:518
  56.4 1.4 %collective-permute-start.4 = (bf16[4,4,3712]{2,1,0:T(4,128)(2,1)S(1)}, bf16[4,4,3712]{2,1,0:T(4,128)(2,1)S(1)}, u32[]{:S(2)}, u32[]{:S(2)}) collective-permute-start(bf16[4,4,3712]{2,1,0:T(4,128)(2,1)S(1)} %all_to_all.22.refs_0_), channel_id=1, source_target_pairs={{0,2},{1,17},{2,0},{3,19},{4,6},{5,21},{6,4},{7,23},{8,10},{9,25},... | collective-permute-start | bytes 356360 | tf_op jit(solution)/shard_map/ppermute | solution.py:518
  57.8 2.5 %collective-permute-done.3.passed = bf16[4,4,3712]{2,1,0:T(4,128)(2,1)S(1)} collective-permute-done((bf16[4,4,3712]{2,1,0:T(4,128)(2,1)S(1)}, bf16[4,4,3712]{2,1,0:T(4,128)(2,1)S(1)}, u32[]{:S(2)}, u32[]{:S(2)}) %collective-permute-start.3) | collective-permute-done | bytes 118816 | tf_op jit(solution)/shard_map/ppermute | solution.py:518
  60.3 1.0 collective-permute-start.5
  61.2 7.5 %shard_map.200 = (bf16[4,4,3712]{2,1,0:T(4,128)(2,1)S(1)}, bf16[3584,1024]{1,0:T(8,128)(2,1)S(1)}, bf16[3584,1024]{1,0:T(8,128)(2,1)S(1)}, bf16[1024,3584]{1,0:T(8,128)(2,1)S(1)}) custom-call(bf16[4,4,3712]{2,1,0:T(4,128)(2,1)S(1)} %collective-permute-done.3.passed, bf16[1,3584,1024]{2,1,0:T(8,128)(2,1)} %refs_0_.1, bf16[1,3584,1024]{2,1,0:T(8,128)(2,1)} %refs_1_.1, ...), custom_call_target="tpu_custom_call" | custom-call | bytes 22020096 | tf_op jit(solution)/shard_map/pallas_call | solution.py:43
  69.8 0.8 collective-permute-done.8.refs_6_
  70.8 3.8 %shard_map.201 = (f32[64,3584]{1,0:T(8,128)S(1)}, bf16[64,3584]{1,0:T(8,128)(2,1)S(1)}) custom-call(bf16[4,4,3712]{2,1,0:T(4,128)(2,1)S(1)} %all_to_all.22.refs_0_, bf16[4,4,3712]{2,1,0:T(4,128)(2,1)S(1)} %get-tuple-element.38.refs_1_, bf16[4,4,3712]{2,1,0:T(4,128)(2,1)S(1)} %collective-permute-done.4.refs_2_, ...), custom_call_target="tpu_custom_call" | custom-call | flops 2818572288 | bytes 22020096 | tf_op jit(solution)/shard_map/pallas_call | solution.py:43
  75.0 1.5 %collective-permute-done.10.got = bf16[64,3584]{1,0:T(8,128)(2,1)S(1)} collective-permute-done((bf16[64,3584]{1,0:T(8,128)(2,1)S(1)}, bf16[64,3584]{1,0:T(8,128)(2,1)S(1)}, u32[]{:S(2)}, u32[]{:S(2)}) %collective-permute-start.10) | collective-permute-done | bytes 458784 | tf_op jit(solution)/shard_map/ppermute | solution.py:518
  76.5 1.1 %collective-permute-start.11 = (bf16[32,3584]{1,0:T(8,128)(2,1)S(1)}, bf16[32,3584]{1,0:T(8,128)(2,1)S(1)}, u32[]{:S(2)}, u32[]{:S(2)}) collective-permute-start(bf16[32,3584]{1,0:T(8,128)(2,1)S(1)} %get-tuple-element.45), channel_id=1, source_target_pairs={{0,2},{1,17},{2,0},{3,19},{4,6},{5,21},{6,4},{7,23},{8,10},{9,25},... | collective-permute-start | bytes 688136 | tf_op jit(solution)/shard_map/ppermute | solution.py:518
  77.7 5.0 %collective-permute-done.11.got = bf16[32,3584]{1,0:T(8,128)(2,1)S(1)} collective-permute-done((bf16[32,3584]{1,0:T(8,128)(2,1)S(1)}, bf16[32,3584]{1,0:T(8,128)(2,1)S(1)}, u32[]{:S(2)}, u32[]{:S(2)}) %collective-permute-start.11) | collective-permute-done | bytes 229408 | tf_op jit(solution)/shard_map/ppermute | solution.py:518
  82.7 1.5 %collective-permute-start.12 = (bf16[16,3584]{1,0:T(8,128)(2,1)S(1)}, bf16[16,3584]{1,0:T(8,128)(2,1)S(1)}, u32[]{:S(2)}, u32[]{:S(2)}) collective-permute-start(bf16[16,3584]{1,0:T(8,128)(2,1)S(1)} %get-tuple-element.47), channel_id=1, source_target_pairs={{0,16},{1,3},{2,18},{3,1},{4,20},{5,7},{6,22},{7,5},{8,24},{9,11},... | collective-permute-start | bytes 344072 | tf_op jit(solution)/shard_map/ppermute | solution.py:518
  84.2 3.3 %collective-permute-done.12.got = bf16[16,3584]{1,0:T(8,128)(2,1)S(1)} collective-permute-done((bf16[16,3584]{1,0:T(8,128)(2,1)S(1)}, bf16[16,3584]{1,0:T(8,128)(2,1)S(1)}, u32[]{:S(2)}, u32[]{:S(2)}) %collective-permute-start.12) | collective-permute-done | bytes 114720 | tf_op jit(solution)/shard_map/ppermute | solution.py:518
  87.6 8.3 %all_to_all.23.got = bf16[4,4,3584]{2,1,0:T(4,128)(2,1)S(1)} all-to-all(bf16[4,4,3584]{2,1,0:T(4,128)(2,1)S(1)} %shard_map.204), channel_id=1, replica_groups=mesh['top'=2,'low'=1,'far'=4,'side'=2,'core'=2] {'low','far'}, dimensions={0} | all-to-all | bytes 229376 | tf_op jit(solution)/shard_map/all_to_all | solution.py:521
  95.8 0.7 shard_map.205
  (34 shorter events, 2.8 us)
Async XLA Ops:
  0.6 31.5 %copy-start = (bf16[256,3584]{1,0:T(8,128)(2,1)S(1)}, bf16[256,3584]{1,0:T(8,128)(2,1)}, u32[]{:S(2)}) copy-start(bf16[256,3584]{1,0:T(8,128)(2,1)} %w_out.1) | copy-start | bytes 5505028
  0.6 31.5 %copy-start.1 = (bf16[2,512,128]{2,1,0:T(8,128)(2,1)S(1)}, bf16[2,512,128]{2,1,0:T(8,128)(2,1)}, u32[]{:S(2)}) copy-start(bf16[2,512,128]{2,1,0:T(8,128)(2,1)} %w_uv.1) | copy-start | bytes 786436
  0.7 45.3 %copy-start.5 = (s32[4,8]{1,0:T(4,128)S(1)}, s32[4,8]{1,0:T(4,128)}, u32[]{:S(2)}) copy-start(s32[4,8]{1,0:T(4,128)} %routes.1) | copy-start | bytes 388
  0.7 45.3 %copy-start.4 = (f32[3584]{0:T(1024)S(1)}, f32[3584]{0:T(1024)}, u32[]{:S(2)}) copy-start(f32[3584]{0:T(1024)} %gain.1) | copy-start | bytes 43012
  0.7 45.3 %copy-start.3 = (bf16[4,3584]{1,0:T(4,128)(2,1)S(1)}, bf16[4,3584]{1,0:T(4,128)(2,1)}, u32[]{:S(2)}) copy-start(bf16[4,3584]{1,0:T(4,128)(2,1)} %residual.1) | copy-start | bytes 86020
  3.9 10.7 %collective-permute-start = (bf16[4,64,512]{2,1,0:T(8,128)(2,1)}, bf16[4,64,512]{2,1,0:T(8,128)(2,1)S(1)}, u32[]{:S(2)}, u32[]{:S(2)}) collective-permute-start(bf16[4,64,512]{2,1,0:T(8,128)(2,1)} %get-tuple-element.25), channel_id=1, source_target_pairs={{0,16},{1,17},{2,18},{3,19},{4,20},{5,21},{6,22},{7,23},{8,24},{9,... | collective-permute-start | bytes 786440 | tf_op jit(solution)/shard_map/ppermute | solution.py:518
  6.9 7.7 %collective-permute-start.1 = (bf16[8,2176]{1,0:T(8,128)(2,1)}, bf16[8,2176]{1,0:T(8,128)(2,1)S(1)}, u32[]{:S(2)}, u32[]{:S(2)}) collective-permute-start(bf16[8,2176]{1,0:T(8,128)(2,1)} %get-tuple-element.26), channel_id=1, source_target_pairs={{0,16},{1,17},{2,18},{3,19},{4,20},{5,21},{6,22},{7,23},{8,24},{9,... | collective-permute-start | bytes 104456 | tf_op jit(solution)/shard_map/ppermute | solution.py:518
  14.7 0.6 copy-start.7
  14.7 0.7 copy-start.6
  32.9 1.6 %collective-permute-start.2 = (bf16[32,3584]{1,0:T(8,128)(2,1)S(1)}, bf16[32,3584]{1,0:T(8,128)(2,1)S(1)}, u32[]{:S(2)}, u32[]{:S(2)}) collective-permute-start(bf16[32,3584]{1,0:T(8,128)(2,1)S(1)} %get-tuple-element.35), channel_id=1, source_target_pairs={{0,1},{1,0},{2,3},{3,2},{4,5},{5,4},{6,7},{7,6},{8,9},{9,8},{10,11... | collective-permute-start | bytes 688136 | tf_op jit(solution)/shard_map/ppermute | solution.py:518
  54.9 15.9 %copy-start.2 = (bf16[3584,16]{0,1:T(8,128)(2,1)S(1)}, bf16[3584,16]{0,1:T(8,128)(2,1)}, u32[]{:S(2)}) copy-start(bf16[3584,16]{0,1:T(8,128)(2,1)} %param.33) | copy-start | bytes 344068
  54.9 5.3 %collective-permute-start.3 = (bf16[4,4,3712]{2,1,0:T(4,128)(2,1)S(1)}, bf16[4,4,3712]{2,1,0:T(4,128)(2,1)S(1)}, u32[]{:S(2)}, u32[]{:S(2)}) collective-permute-start(bf16[4,4,3712]{2,1,0:T(4,128)(2,1)S(1)} %all_to_all.22.refs_0_), channel_id=1, source_target_pairs={{0,16},{1,3},{2,18},{3,1},{4,20},{5,7},{6,22},{7,5},{8,24},{9,11},... | collective-permute-start | bytes 356360 | tf_op jit(solution)/shard_map/ppermute | solution.py:518
  56.4 12.9 %collective-permute-start.4 = (bf16[4,4,3712]{2,1,0:T(4,128)(2,1)S(1)}, bf16[4,4,3712]{2,1,0:T(4,128)(2,1)S(1)}, u32[]{:S(2)}, u32[]{:S(2)}) collective-permute-start(bf16[4,4,3712]{2,1,0:T(4,128)(2,1)S(1)} %all_to_all.22.refs_0_), channel_id=1, source_target_pairs={{0,2},{1,17},{2,0},{3,19},{4,6},{5,21},{6,4},{7,23},{8,10},{9,25},... | collective-permute-start | bytes 356360 | tf_op jit(solution)/shard_map/ppermute | solution.py:518
  60.3 9.1 %collective-permute-start.5 = (bf16[4,4,3712]{2,1,0:T(4,128)(2,1)S(1)}, bf16[4,4,3712]{2,1,0:T(4,128)(2,1)S(1)}, u32[]{:S(2)}, u32[]{:S(2)}) collective-permute-start(bf16[4,4,3712]{2,1,0:T(4,128)(2,1)S(1)} %collective-permute-done.3.passed), channel_id=1, source_target_pairs={{0,2},{1,17},{2,0},{3,19},{4,6},{5,21},{6,4},{7,23},{8,10},{9,25},... | collective-permute-start | bytes 356360 | tf_op jit(solution)/shard_map/ppermute | solution.py:518
  61.2 8.6 %collective-permute-start.6 = (bf16[4,4,3712]{2,1,0:T(4,128)(2,1)S(1)}, bf16[4,4,3712]{2,1,0:T(4,128)(2,1)S(1)}, u32[]{:S(2)}, u32[]{:S(2)}) collective-permute-start(bf16[4,4,3712]{2,1,0:T(4,128)(2,1)S(1)} %all_to_all.22.refs_0_), channel_id=1, source_target_pairs={{0,1},{1,0},{2,3},{3,2},{4,5},{5,4},{6,7},{7,6},{8,9},{9,8},{10,11... | collective-permute-start | bytes 356360 | tf_op jit(solution)/shard_map/ppermute | solution.py:518
  68.7 1.9 %collective-permute-start.7 = (bf16[4,4,3712]{2,1,0:T(4,128)(2,1)S(1)}, bf16[4,4,3712]{2,1,0:T(4,128)(2,1)S(1)}, u32[]{:S(2)}, u32[]{:S(2)}) collective-permute-start(bf16[4,4,3712]{2,1,0:T(4,128)(2,1)S(1)} %get-tuple-element.38.refs_1_), channel_id=1, source_target_pairs={{0,1},{1,0},{2,3},{3,2},{4,5},{5,4},{6,7},{7,6},{8,9},{9,8},{10,11... | collective-permute-start | bytes 356360 | tf_op jit(solution)/shard_map/ppermute | solution.py:518
  69.3 1.3 %collective-permute-start.8 = (bf16[4,4,3712]{2,1,0:T(4,128)(2,1)S(1)}, bf16[4,4,3712]{2,1,0:T(4,128)(2,1)S(1)}, u32[]{:S(2)}, u32[]{:S(2)}) collective-permute-start(bf16[4,4,3712]{2,1,0:T(4,128)(2,1)S(1)} %collective-permute-done.4.refs_2_), channel_id=1, source_target_pairs={{0,1},{1,0},{2,3},{3,2},{4,5},{5,4},{6,7},{7,6},{8,9},{9,8},{10,11... | collective-permute-start | bytes 356360 | tf_op jit(solution)/shard_map/ppermute | solution.py:518
  69.4 1.4 %collective-permute-start.9 = (bf16[4,4,3712]{2,1,0:T(4,128)(2,1)S(1)}, bf16[4,4,3712]{2,1,0:T(4,128)(2,1)S(1)}, u32[]{:S(2)}, u32[]{:S(2)}) collective-permute-start(bf16[4,4,3712]{2,1,0:T(4,128)(2,1)S(1)} %collective-permute-done.5.refs_3_), channel_id=1, source_target_pairs={{0,1},{1,0},{2,3},{3,2},{4,5},{5,4},{6,7},{7,6},{8,9},{9,8},{10,11... | collective-permute-start | bytes 356360 | tf_op jit(solution)/shard_map/ppermute | solution.py:518
  74.6 1.9 %collective-permute-start.10 = (bf16[64,3584]{1,0:T(8,128)(2,1)S(1)}, bf16[64,3584]{1,0:T(8,128)(2,1)S(1)}, u32[]{:S(2)}, u32[]{:S(2)}) collective-permute-start(bf16[64,3584]{1,0:T(8,128)(2,1)S(1)} %get-tuple-element.43), channel_id=1, source_target_pairs={{0,1},{1,0},{2,3},{3,2},{4,5},{5,4},{6,7},{7,6},{8,9},{9,8},{10,11... | collective-permute-start | bytes 1376264 | tf_op jit(solution)/shard_map/ppermute | solution.py:518
  76.5 6.1 %collective-permute-start.11 = (bf16[32,3584]{1,0:T(8,128)(2,1)S(1)}, bf16[32,3584]{1,0:T(8,128)(2,1)S(1)}, u32[]{:S(2)}, u32[]{:S(2)}) collective-permute-start(bf16[32,3584]{1,0:T(8,128)(2,1)S(1)} %get-tuple-element.45), channel_id=1, source_target_pairs={{0,2},{1,17},{2,0},{3,19},{4,6},{5,21},{6,4},{7,23},{8,10},{9,25},... | collective-permute-start | bytes 688136 | tf_op jit(solution)/shard_map/ppermute | solution.py:518
  82.7 4.9 %collective-permute-start.12 = (bf16[16,3584]{1,0:T(8,128)(2,1)S(1)}, bf16[16,3584]{1,0:T(8,128)(2,1)S(1)}, u32[]{:S(2)}, u32[]{:S(2)}) collective-permute-start(bf16[16,3584]{1,0:T(8,128)(2,1)S(1)} %get-tuple-element.47), channel_id=1, source_target_pairs={{0,16},{1,3},{2,18},{3,1},{4,20},{5,7},{6,22},{7,5},{8,24},{9,11},... | collective-permute-start | bytes 344072 | tf_op jit(solution)/shard_map/ppermute | solution.py:518

commit v2 on v1

--- a/solution.py
+++ b/solution.py
@@ -23,7 +23,8 @@
 EXPERT = ("far", "side", "core")
 ROWS = DP + EXPERT
 FAR = ("low", "far")
-LOAD_MIB = 28
+LOAD_MIB = 36
+EXPERT_MIB = 36
 
 
 def dot_nt(a, b):
@@ -65,20 +66,19 @@
     return copies
 
 
-def pick_kernel(partners, moves, move_hbm, scale_ref, lat, rope_hbm, *rest):
+def pick_kernel(partners, moves, move_hbm, scale_hbm, lat, rope_hbm, *rest):
     lat_outs, rope_outs = rest[:partners], rest[partners : 2 * partners]
-    scale_out, move, rope, wide_scale, lat_sems, sems = rest[2 * partners :]
+    scale_out, move, rope, scale_ref, wide_scale, lat_sems, sems = rest[2 * partners :]
     slots, width = rope.shape
     half = width // 2
     me = lax.axis_index(DP)
-    get_move, get_rope = fetch(
+    get_move, get_scale, get_rope = fetch(
         [
             pltpu.make_async_copy(move_hbm, move, sems.at[0]),
-            pltpu.make_async_copy(rope_hbm, rope, sems.at[1]),
+            pltpu.make_async_copy(scale_hbm, scale_ref, sems.at[1]),
+            pltpu.make_async_copy(rope_hbm, rope, sems.at[2]),
         ]
     )
-    wide_scale[...] = scale_ref[...].astype(F32)
-    (put_scale,) = fetch([pltpu.make_async_copy(wide_scale, scale_out, sems.at[2])])
     get_move.wait()
     copies = []
     for k in range(partners):
@@ -89,6 +89,9 @@
                 )
             )
     fetch(copies)
+    get_scale.wait()
+    wide_scale[...] = scale_ref[...].astype(F32)
+    (put_scale,) = fetch([pltpu.make_async_copy(wide_scale, scale_out, sems.at[3])])
     put_scale.wait()
     get_rope.wait()
     row = iota((2 * moves, 1), 0)
@@ -132,7 +135,7 @@
 def local_kernel(
     sizes,
     partners,
-    scale,
+    scale_hbm,
     table_hbm,
     lengths_hbm,
     move_hbm,
@@ -142,12 +145,10 @@
     turn_hbm,
     new_lat_hbm,
     new_rope_hbm,
-    acc_out,
-    peak_out,
-    total_out,
+    out,
+    scale,
     qrel_out,
     q2_out,
-    limit_out,
     table,
     lengths,
     move,
@@ -174,6 +175,7 @@
         (table_hbm, table),
         (lengths_hbm, lengths),
         (move_hbm, move),
+        (scale_hbm, scale),
         (rope_hbm, rope),
         (turn_hbm, q_rope),
         (q_hbm, q_lat),
@@ -234,9 +236,9 @@
 
     for k in range(partners):
         for m in range(moves):
-            limit_out[k * moves + m : k * moves + m + 1, :] = limit_row(
-                slots + (me ^ (k + 1)) * moves + m
-            )
+            at = 2 * rows + 2 + k * moves + m
+            limit = limit_row(slots + (me ^ (k + 1)) * moves + m)
+            out[at : at + 1, :rows] = limit.astype(F32)
     queries = qrel_out[...]
     fresh_rows = rollouts * following
     new_keys[...] = jnp.zeros(new_keys.shape, F32)
@@ -297,31 +299,23 @@
         weights.append(weight)
         keys.append(lat[page])
     acc = acc + dot_tn(jnp.concatenate(weights, axis=0), jnp.concatenate(keys, axis=0))
-    acc_out[...] = acc
-    peak_out[...] = jnp.broadcast_to(peak, peak_out.shape)
     whole = jnp.sum(total, axis=0, keepdims=True) + jnp.sum(new_exp, axis=0, keepdims=True)
-    total_out[...] = jnp.broadcast_to(whole, total_out.shape)
+    out[:rows, :latent] = acc
+    out[rows : 2 * rows, :latent] = qrel_out[...].astype(F32)
+    out[2 * rows : 2 * rows + 1, :rows] = peak
+    out[2 * rows + 1 : 2 * rows + 2, :rows] = whole
+    out[: 2 * rows, latent:] = q2_out[...].astype(F32)
 
 
 def merge_kernel(partners, *refs):
-    count = 2 * partners + 6
-    sources, out, held = refs[:count], refs[count], refs[count + 1 : 2 * count + 1]
-    scores, sems = refs[2 * count + 1 :]
-    copies = fetch(
-        [
-            pltpu.make_async_copy(src, dst, sems.at[i])
-            for i, (src, dst) in enumerate(zip(sources, held))
-        ]
-    )
-    for copy in copies:
-        copy.wait()
-    got_lat, got_rope = held[:partners], held[partners : 2 * partners]
-    acc_in, peak_in, total_in, qrel, q2, limit = held[2 * partners :]
+    got_lat, got_rope = refs[:partners], refs[partners : 2 * partners]
+    local, out, scores = refs[2 * partners :]
     moves, page_len, latent = got_lat[0].shape
-    rows = qrel.shape[0]
+    rows = out.shape[0] * out.shape[1]
+    qrel = local[rows : 2 * rows, :latent].astype(BF16)
+    q2 = local[: 2 * rows, latent:].astype(BF16)
     wide = q2.shape[1]
-    position = iota((page_len, rows), 0)
-    queries = qrel[...]
+    position = iota((page_len, rows), 0).astype(F32)
     best = jnp.full((page_len, rows), LOW, F32)
     half_lanes = got_rope[0].shape[1] - LANES
     pieces = half_lanes // wide
@@ -332,13 +326,13 @@
         stacked = jnp.concatenate(
             [turns[:, c * wide : (c + 1) * wide].astype(F32) for c in range(pieces)], axis=0
         ).astype(BF16)
-        turned = dot_nt(stacked, q2[...])
+        turned = dot_nt(stacked, q2)
         base = k * span
         for c in range(pieces):
             part = turned[c * 2 * moves : (c + 1) * 2 * moves]
             spread(scores, base + 2 * c, 2 * moves, page_len // 2, part[:, :rows])
             spread(scores, base + 2 * c + 1, 2 * moves, page_len // 2, part[:, rows:])
-        fresh = dot_nt(got_lat[k][...].reshape(span, latent), queries)
+        fresh = dot_nt(got_lat[k][...].reshape(span, latent), qrel)
         marks = turns[:, half_lanes:].astype(F32)
         for m in range(moves):
             factor = marks[2 * m : 2 * m + 1, :1]
@@ -346,11 +340,11 @@
             where_at = pl.ds(base + m * page_len, page_len)
             part = fresh[m * page_len : (m + 1) * page_len] + read(scores, where_at)
             part = part * (factor * SCORE_SCALE)
-            at = k * moves + m
-            part = jnp.where(position < limit[at : at + 1, :], part, LOW)
+            at = 2 * rows + 2 + k * moves + m
+            part = jnp.where(position < local[at : at + 1, :rows], part, LOW)
             write(scores, where_at, part)
             best = jnp.maximum(best, part)
-    peak_local = peak_in[:1, :]
+    peak_local = local[2 * rows : 2 * rows + 1, :rows]
     peak = jnp.maximum(jnp.max(best, axis=0, keepdims=True), peak_local)
     shrink = jnp.exp(peak_local - peak)
     acc = jnp.zeros((rows, latent), F32)
@@ -365,12 +359,12 @@
         acc = acc + dot_tn(
             jnp.concatenate(weights, axis=0), got_lat[k][...].reshape(span, latent)
         )
-    total = total_in[:1, :] * shrink + jnp.sum(grown_sum, axis=0, keepdims=True)
+    total = local[2 * rows + 1 : 2 * rows + 2, :rows] * shrink + jnp.sum(grown_sum, axis=0, keepdims=True)
 
     def upright(row):
         return jnp.transpose(jnp.broadcast_to(row, (LANES, rows)))[:, :1]
 
-    result = (acc_in[...] * upright(shrink) + acc) / upright(total)
+    result = (local[:rows, :latent] * upright(shrink) + acc) / upright(total)
     out[...] = result.reshape(out.shape).astype(BF16)
 
 
@@ -419,6 +413,25 @@
         out[copy, :, width : width + routes.shape[1]] = named
 
 
+def stack_kernel(*refs):
+    for k, ref in enumerate(refs[:-1]):
+        refs[-1][k] = ref[0]
+
+
+def parts_kernel(kept, got, *outs):
+    total = kept[...] + got[...].astype(F32)
+    rows = outs[0].shape[0]
+    for k, out in enumerate(outs):
+        out[...] = total[k * rows : (k + 1) * rows].astype(out.dtype)
+
+
+def add_kernel(*refs):
+    total = refs[0][...]
+    for ref in refs[1:-1]:
+        total = total + ref[...].astype(F32)
+    refs[-1][...] = total.astype(BF16)
+
+
 def load_kernel(count, passed, *refs):
     sources, passed_out, outs, sems = refs[:count], refs[count], refs[count + 1 : -1], refs[-1]
     split = sems.shape[1]
@@ -438,12 +451,20 @@
 
 def expert_kernel(top, count, *refs):
     pieces = refs[:count]
-    w_router, w_gate, w_up, w_down = refs[count : count + 4]
-    kept, away, rows_ref, hidden_ref = refs[count + 4 :]
+    w_router, w_gate, w_up, down_hbm = refs[count : count + 4]
+    kept, away, rows_ref, hidden_ref, w_down, sems = refs[count + 4 :]
     expert = lax.axis_index(EXPERT)
     width, units = w_gate.shape
     in_step = 256 if units % 256 == 0 else units
     out_step = 512 if width % 512 == 0 else width
+    down_copies = fetch(
+        [
+            pltpu.make_async_copy(
+                down_hbm.at[0, :, pl.ds(at, out_step)], w_down.at[:, pl.ds(at, out_step)], sems.at[i]
+            )
+            for i, at in enumerate(range(0, width, out_step))
+        ]
+    )
     piece_rows = rows_ref.shape[0] // count
     named = []
     for k, piece in enumerate(pieces):
@@ -467,7 +488,8 @@
         hidden_ref[:, at : at + in_step] = (gate / (1.0 + jnp.exp(-gate)) * up).astype(BF16)
     hidden = hidden_ref[...]
     half = rows_ref.shape[0] // 2
-    for at in range(0, width, out_step):
+    for i, at in enumerate(range(0, width, out_step)):
+        down_copies[i].wait()
         part = dot_nn(hidden, w_down[:, at : at + out_step]) * gates
         kept[:, at : at + out_step] = part[:half]
         away[:, at : at + out_step] = part[half:].astype(BF16)
@@ -537,30 +559,25 @@
         + [shape((2 * moves, cache_rope.shape[1] // 2 + LANES), BF16)] * partners
         + [shape((slots,), F32)],
         (move_list, page_scale, cache_lat, cache_rope),
-        in_specs=[HBM, VMEM, HBM, HBM],
+        in_specs=[HBM] * 4,
         out_specs=[VMEM] * (2 * partners) + [SMEM],
         scratch=[
             pltpu.SMEM(move_list.shape, jnp.int32),
             pltpu.VMEM(cache_rope.shape, BF16),
+            pltpu.VMEM(page_scale.shape, BF16),
             pltpu.VMEM((slots,), F32),
             pltpu.SemaphoreType.DMA((partners, moves)),
-            pltpu.SemaphoreType.DMA((3,)),
+            pltpu.SemaphoreType.DMA((4,)),
         ],
         vmem=60,
     )
     got_lat = [swap(picked[k], (k + 1) * expert_count) for k in range(partners)]
     got_rope = [swap(picked[partners + k], (k + 1) * expert_count) for k in range(partners)]
 
+    extra = -(-(2 + partners * moves) // 8) * 8
     local = call(
         functools.partial(local_kernel, sizes, partners),
-        [
-            shape((rows, latent), F32),
-            shape((8, rows), F32),
-            shape((8, rows), F32),
-            shape((rows, latent), BF16),
-            shape((2 * rows, 2 * rope_dim), BF16),
-            shape((-(-partners * moves // 8) * 8, rows), jnp.int32),
-        ],
+        [shape((2 * rows + extra, latent + 2 * rope_dim), F32)],
         (
             picked[-1],
             page_table,
@@ -573,8 +590,11 @@
             new_lat,
             new_rope,
         ),
-        in_specs=[SMEM] + [HBM] * 9,
+        in_specs=[HBM] * 10,
         scratch=[
+            pltpu.SMEM((slots,), F32),
+            pltpu.VMEM((rows, latent), BF16),
+            pltpu.VMEM((2 * rows, 2 * rope_dim), BF16),
             pltpu.SMEM(page_table.shape, jnp.int32),
             pltpu.SMEM(lengths.shape, jnp.int32),
             pltpu.SMEM(move_list.shape, jnp.int32),
@@ -588,26 +608,20 @@
             pltpu.SMEM((rollouts * view,), jnp.int32),
             pltpu.VMEM((16, latent), F32),
             pltpu.VMEM((16, 2 * rope_dim), F32),
-            pltpu.SemaphoreType.DMA((8,)),
+            pltpu.SemaphoreType.DMA((9,)),
             pltpu.SemaphoreType.DMA((slots // GROUP,)),
         ],
         vmem=60,
         cost=(2 * slots * page_len * rows * (2 * latent + 2 * rope_dim), 4 * MIB),
     )
-    operands = (*got_lat, *got_rope, *local)
     blocks = call(
         functools.partial(merge_kernel, partners),
         [shape((expert_count, tokens * per_device, latent), BF16)],
-        operands,
-        in_specs=[HBM] * len(operands),
-        scratch=[pltpu.VMEM(x.shape, x.dtype) for x in operands]
-        + [
-            pltpu.VMEM((rows // LANES, partners * moves * page_len, LANES), F32),
-            pltpu.SemaphoreType.DMA((len(operands),)),
-        ],
-        vmem=60,
+        (*got_lat, *got_rope, *local),
+        scratch=[pltpu.VMEM((rows // LANES, partners * moves * page_len, LANES), F32)],
         cost=(2 * moves * page_len * rows * 2 * latent, MIB),
     )[0]
+
     blocks = deal(blocks, EXPERT)
 
     half_rows = expert_count // 2 * tokens
@@ -624,9 +638,14 @@
     )[0]
     parts = deal(parts, ("far", "side"))
     far_count = total_devices // 8
+    masks = [2 * side_bit * k for k in range(far_count)]
+    direct = far_count <= 4
     attn_out, own_rows = call(
         norm_kernel,
-        [shape((tokens, width), BF16), shape((far_count, tokens, width + LANES), BF16)],
+        [
+            shape((tokens, width), BF16),
+            shape((1 if direct else far_count, tokens, width + LANES), BF16),
+        ],
         (parts, residual, norm_gain, routes),
     )
 
@@ -641,10 +660,18 @@
             cost=(0, 2 * sum(w.size for w in sources)),
         )
 
-    piece = deal(own_rows, FAR)
+    if direct:
+        others = [swap(own_rows, mask) for mask in masks[1:]]
+        piece = call(
+            stack_kernel,
+            [shape((far_count, tokens, width + LANES), BF16)],
+            (own_rows, *others),
+        )[0]
+    else:
+        piece = deal(own_rows, FAR)
     pieces = [piece, swap(piece, top_bit, side_bit)]
     pieces = pieces + [swap(p, side_bit, top_bit) for p in pieces]
-    side_piece, *weights = load(pieces[1], (w_gate, w_up, w_down), LOAD_MIB)
+    side_piece, gate_here, up_here = load(pieces[1], (w_gate, w_up), LOAD_MIB)
     pieces = [piece, side_piece] + pieces[2:]
     pieces = pieces + [swap(p, 1) for p in pieces]
 
@@ -654,12 +681,15 @@
     kept, away = call(
         functools.partial(expert_kernel, routes.shape[1], len(pieces)),
         [shape((half, width), F32), shape((half, width), BF16)],
-        (*pieces, w_router.T, *weights),
+        (*pieces, w_router.T, gate_here, up_here, w_down),
+        in_specs=[VMEM] * (len(pieces) + 3) + [HBM],
         scratch=[
             pltpu.VMEM((all_rows, width), BF16),
             pltpu.VMEM((all_rows, hidden_units), BF16),
+            pltpu.VMEM(w_down.shape[1:], BF16),
+            pltpu.SemaphoreType.DMA((16,)),
         ],
-        vmem=16 if all_rows <= 256 else 56,
+        vmem=EXPERT_MIB if all_rows <= 256 else 56,
         cost=(6 * all_rows * width * hidden_units, 6 * width * hidden_units),
     )
 
@@ -676,8 +706,16 @@
         (kept, got),
     )
     got = swap(away, top_bit, side_bit)
-    parts = call(split_kernel, [shape((far_count, tokens, width), BF16)], (kept, got))[0]
-    moe_out = call(sum_kernel, [shape((tokens, width), BF16)], (deal(parts, FAR),))[0]
+    moe_shape = [shape((tokens, width), BF16)]
+    if direct:
+        parts = call(
+            parts_kernel, [shape((tokens, width), F32)] + moe_shape * (far_count - 1), (kept, got)
+        )
+        got = [swap(part, mask) for part, mask in zip(parts[1:], masks[1:])]
+        moe_out = call(add_kernel, moe_shape, (parts[0], *got))[0]
+    else:
+        parts = call(split_kernel, [shape((far_count, tokens, width), BF16)], (kept, got))[0]
+        moe_out = call(sum_kernel, moe_shape, (deal(parts, FAR),))[0]
     return (attn_out, moe_out)
 
 

time: 96.9 us -> 93.1 us (0.961)
  blocking collectives: 42.3 us -> 25.5 us
  starting transfers between devices: 11.1 us -> 19.9 us
  waiting for transfers between devices: 14.7 us -> 21.4 us
  Pallas kernels: 26.9 us -> 24.1 us
    all_to_all x4 -> x2, blocking collectives: 42.3 us -> 25.5 us  [deal(): return lax.all_to_all(x, names, split_axis=0, concat_axis=0, tiled=True)]
    ppermute x13 -> x19, starting transfers between devices: 11.1 us -> 19.9 us  [swap(): return lax.ppermute(x, ROWS, pairs)]
    ppermute x13 -> x19, waiting for transfers between devices: 14.7 us -> 21.4 us  [swap(): return lax.ppermute(x, ROWS, pairs)]
    pallas_call x12 -> x13, Pallas kernels: 26.9 us -> 24.1 us  [call(): pl.pallas_call(kernel, out_shape=outs, in_specs=in_specs or [VMEM] * len(...]
  transfers between devices with their start and end apart: 13 -> 19, of which waited for: 7 -> 13; matrix products, arithmetic and copies ran while one was open for 0% -> 0% of each run, Pallas kernels for 16% -> 13%
where the time goes in v2:
time: 93.1 us; the launch traced here: 92.8 us
  blocking collectives  25.5 us (27%)
  Pallas kernels  24.1 us (26%)
  waiting for transfers between devices  21.4 us (23%)
  starting transfers between devices  19.9 us (21%)
  local copies, waits for them, and re-layouts  1.12 us (1%)
    all_to_all x2, blocking collectives, deal(): return lax.all_to_all(x, names, split_axis=0, concat_axis=0, tiled=True)  25.5 us
    pallas_call x13, Pallas kernels, call(): pl.pallas_call(kernel, out_shape=outs, in_specs=in_specs or [VMEM] * len(...  24.1 us
    ppermute x19, waiting for transfers between devices, swap(): return lax.ppermute(x, ROWS, pairs)  21.4 us
    ppermute x19, starting transfers between devices, swap(): return lax.ppermute(x, ROWS, pairs)  19.9 us
  transfers between devices with their start and end apart: 19, of which 13 were waited for; matrix products, arithmetic and copies ran while one was open for 0% of the time, Pallas kernels for 13%

profile of v2, /device:TPU:0, one launch (start us, length us, event | category | flops | bytes accessed | tf_op | source)
XLA Modules:
  0.0 92.8 jit_solution(16890129799355219788)
XLA Ops:
  0.7 2.6 %shard_map.194 = (bf16[4,64,512]{2,1,0:T(8,128)(2,1)}, bf16[8,2176]{1,0:T(8,128)(2,1)}, f32[48]{0:T(128)}) custom-call(s32[1,2,4]{2,1,0:T(2,128)} %move_hbm.3, bf16[48]{0:T(256)(128)(2,1)} %scale_hbm.1, bf16[48,64,512]{2,1,0:T(8,128)(2,1)} %lat_hbm.1, bf16[48,4096]{1,0:T(8,128)(2,1)} %rope_hbm.3), custom_call_target="tpu_custom_call" | custom-call | tf_op jit(solution)/shard_map/pallas_call | solution.py:44
  3.3 3.0 %collective-permute-start = (bf16[4,64,512]{2,1,0:T(8,128)(2,1)}, bf16[4,64,512]{2,1,0:T(8,128)(2,1)S(1)}, u32[]{:S(2)}, u32[]{:S(2)}) collective-permute-start(bf16[4,64,512]{2,1,0:T(8,128)(2,1)} %get-tuple-element.22), channel_id=1, source_target_pairs={{0,16},{1,17},{2,18},{3,19},{4,20},{5,21},{6,22},{7,23},{8,24},{9,... | collective-permute-start | bytes 786440 | tf_op jit(solution)/shard_map/ppermute | solution.py:540
  6.4 7.1 %shard_map.195.refs_2_ = f32[264,640]{1,0:T(8,128)} custom-call(f32[48]{0:T(128)} %get-tuple-element.24.scale_hbm, s32[2,32]{1,0:T(2,128)} %table_hbm.1, s32[2]{0:T(128)} %lengths_hbm.1, s32[1,2,4]{2,1,0:T(2,128)} %move_hbm.3, bf16[48,64,512]{2,1,0:T(8,128)(2,1)} %lat_hbm.1, bf16[48,4096]{1,0:T(8,128)(2,1)} %rope_hbm.3, bf16[2,2,32,512]{3,2,1,0:T(8,128)(2,1)} %q_hbm.1, ...), custom_call_target="tpu_custom_call" | custom-call | flops 905969664 | bytes 4194304 | tf_op jit(solution)/shard_map/pallas_call | solution.py:44
  15.2 14.0 %all_to_all.10.blocks = bf16[16,8,512]{2,1,0:T(8,128)(2,1)S(1)} all-to-all(bf16[16,8,512]{2,1,0:T(8,128)(2,1)S(1)} %shard_map.196), channel_id=1, replica_groups=mesh['top'=2,'low'=1,'far'=4,'side'=2,'core'=2] {'far','side','core'}, dimensions={0} | all-to-all | bytes 262144 | tf_op jit(solution)/shard_map/all_to_all | solution.py:543
  30.1 1.5 %collective-permute-done.2.got = bf16[32,3584]{1,0:T(8,128)(2,1)S(1)} collective-permute-done((bf16[32,3584]{1,0:T(8,128)(2,1)S(1)}, bf16[32,3584]{1,0:T(8,128)(2,1)S(1)}, u32[]{:S(2)}, u32[]{:S(2)}) %collective-permute-start.2) | collective-permute-done | bytes 229408 | tf_op jit(solution)/shard_map/ppermute | solution.py:540
  31.6 11.4 %all_to_all.11.got = bf16[8,4,3584]{2,1,0:T(4,128)(2,1)S(1)} all-to-all(bf16[8,4,3584]{2,1,0:T(4,128)(2,1)S(1)} %shard_map.198), channel_id=1, replica_groups=mesh['top'=2,'low'=1,'far'=4,'side'=2,'core'=2] {'far','side'}, dimensions={0} | all-to-all | bytes 458752 | tf_op jit(solution)/shard_map/all_to_all | solution.py:543
  44.7 1.4 %collective-permute-start.4 = (bf16[1,4,3712]{2,1,0:T(4,128)(2,1)S(1)}, bf16[1,4,3712]{2,1,0:T(4,128)(2,1)S(1)}, u32[]{:S(2)}, u32[]{:S(2)}) collective-permute-start(bf16[1,4,3712]{2,1,0:T(4,128)(2,1)S(1)} %get-tuple-element.28.refs_0_), channel_id=1, source_target_pairs={{0,8},{1,9},{2,10},{3,11},{4,12},{5,13},{6,14},{7,15},{8,0},{9,1},... | collective-permute-start | bytes 89096 | tf_op jit(solution)/shard_map/ppermute | solution.py:540
  46.1 2.0 %collective-permute-start.3 = (bf16[1,4,3712]{2,1,0:T(4,128)(2,1)S(1)}, bf16[1,4,3712]{2,1,0:T(4,128)(2,1)S(1)}, u32[]{:S(2)}, u32[]{:S(2)}) collective-permute-start(bf16[1,4,3712]{2,1,0:T(4,128)(2,1)S(1)} %get-tuple-element.28.refs_0_), channel_id=1, source_target_pairs={{0,4},{1,5},{2,6},{3,7},{4,0},{5,1},{6,2},{7,3},{8,12},{9,13},{10,... | collective-permute-start | bytes 89096 | tf_op jit(solution)/shard_map/ppermute | solution.py:540
  48.2 1.3 %collective-permute-done.5.refs_3_ = bf16[1,4,3712]{2,1,0:T(4,128)(2,1)S(1)} collective-permute-done((bf16[1,4,3712]{2,1,0:T(4,128)(2,1)S(1)}, bf16[1,4,3712]{2,1,0:T(4,128)(2,1)S(1)}, u32[]{:S(2)}, u32[]{:S(2)}) %collective-permute-start.5) | collective-permute-done | bytes 29728 | tf_op jit(solution)/shard_map/ppermute | solution.py:540
  50.3 1.6 %collective-permute-start.6 = (bf16[4,4,3712]{2,1,0:T(4,128)(2,1)S(1)}, bf16[4,4,3712]{2,1,0:T(4,128)(2,1)S(1)}, u32[]{:S(2)}, u32[]{:S(2)}) collective-permute-start(bf16[4,4,3712]{2,1,0:T(4,128)(2,1)S(1)} %shard_map.200.refs_0_), channel_id=1, source_target_pairs={{0,16},{1,3},{2,18},{3,1},{4,20},{5,7},{6,22},{7,5},{8,24},{9,11},... | collective-permute-start | bytes 356360 | tf_op jit(solution)/shard_map/ppermute | solution.py:540
  51.9 1.2 %collective-permute-start.7 = (bf16[4,4,3712]{2,1,0:T(4,128)(2,1)S(1)}, bf16[4,4,3712]{2,1,0:T(4,128)(2,1)S(1)}, u32[]{:S(2)}, u32[]{:S(2)}) collective-permute-start(bf16[4,4,3712]{2,1,0:T(4,128)(2,1)S(1)} %shard_map.200.refs_0_), channel_id=1, source_target_pairs={{0,2},{1,17},{2,0},{3,19},{4,6},{5,21},{6,4},{7,23},{8,10},{9,25},... | collective-permute-start | bytes 356360 | tf_op jit(solution)/shard_map/ppermute | solution.py:540
  53.1 3.0 %collective-permute-done.6.passed = bf16[4,4,3712]{2,1,0:T(4,128)(2,1)S(1)} collective-permute-done((bf16[4,4,3712]{2,1,0:T(4,128)(2,1)S(1)}, bf16[4,4,3712]{2,1,0:T(4,128)(2,1)S(1)}, u32[]{:S(2)}, u32[]{:S(2)}) %collective-permute-start.6) | collective-permute-done | bytes 118816 | tf_op jit(solution)/shard_map/ppermute | solution.py:540
  56.9 5.3 %shard_map.201 = (bf16[4,4,3712]{2,1,0:T(4,128)(2,1)S(1)}, bf16[3584,1024]{1,0:T(8,128)(2,1)S(1)}, bf16[3584,1024]{1,0:T(8,128)(2,1)S(1)}) custom-call(bf16[4,4,3712]{2,1,0:T(4,128)(2,1)S(1)} %collective-permute-done.6.passed, bf16[1,3584,1024]{2,1,0:T(8,128)(2,1)} %refs_0_.1, bf16[1,3584,1024]{2,1,0:T(8,128)(2,1)} %refs_1_.1), custom_call_target="tpu_custom_call" | custom-call | bytes 14680064 | tf_op jit(solution)/shard_map/pallas_call | solution.py:44
  64.3 6.2 %shard_map.202 = (f32[64,3584]{1,0:T(8,128)S(1)}, bf16[64,3584]{1,0:T(8,128)(2,1)S(1)}) custom-call(bf16[4,4,3712]{2,1,0:T(4,128)(2,1)S(1)} %shard_map.200.refs_0_, bf16[4,4,3712]{2,1,0:T(4,128)(2,1)S(1)} %get-tuple-element.29.refs_1_, bf16[4,4,3712]{2,1,0:T(4,128)(2,1)S(1)} %collective-permute-done.7.refs_2_, ...), custom_call_target="tpu_custom_call" | custom-call | flops 2818572288 | bytes 22020096 | tf_op jit(solution)/shard_map/pallas_call | solution.py:44
  71.0 1.5 %collective-permute-done.13.got = bf16[64,3584]{1,0:T(8,128)(2,1)S(1)} collective-permute-done((bf16[64,3584]{1,0:T(8,128)(2,1)S(1)}, bf16[64,3584]{1,0:T(8,128)(2,1)S(1)}, u32[]{:S(2)}, u32[]{:S(2)}) %collective-permute-start.13) | collective-permute-done | bytes 458784 | tf_op jit(solution)/shard_map/ppermute | solution.py:540
  72.5 1.3 %collective-permute-start.14 = (bf16[32,3584]{1,0:T(8,128)(2,1)S(1)}, bf16[32,3584]{1,0:T(8,128)(2,1)S(1)}, u32[]{:S(2)}, u32[]{:S(2)}) collective-permute-start(bf16[32,3584]{1,0:T(8,128)(2,1)S(1)} %get-tuple-element.35), channel_id=1, source_target_pairs={{0,2},{1,17},{2,0},{3,19},{4,6},{5,21},{6,4},{7,23},{8,10},{9,25},... | collective-permute-start | bytes 688136 | tf_op jit(solution)/shard_map/ppermute | solution.py:540
  73.8 4.7 %collective-permute-done.14.got = bf16[32,3584]{1,0:T(8,128)(2,1)S(1)} collective-permute-done((bf16[32,3584]{1,0:T(8,128)(2,1)S(1)}, bf16[32,3584]{1,0:T(8,128)(2,1)S(1)}, u32[]{:S(2)}, u32[]{:S(2)}) %collective-permute-start.14) | collective-permute-done | bytes 229408 | tf_op jit(solution)/shard_map/ppermute | solution.py:540
  78.6 1.6 %collective-permute-start.15 = (bf16[16,3584]{1,0:T(8,128)(2,1)S(1)}, bf16[16,3584]{1,0:T(8,128)(2,1)S(1)}, u32[]{:S(2)}, u32[]{:S(2)}) collective-permute-start(bf16[16,3584]{1,0:T(8,128)(2,1)S(1)} %get-tuple-element.37), channel_id=1, source_target_pairs={{0,16},{1,3},{2,18},{3,1},{4,20},{5,7},{6,22},{7,5},{8,24},{9,11},... | collective-permute-start | bytes 344072 | tf_op jit(solution)/shard_map/ppermute | solution.py:540
  80.2 3.3 %collective-permute-done.15.got = bf16[16,3584]{1,0:T(8,128)(2,1)S(1)} collective-permute-done((bf16[16,3584]{1,0:T(8,128)(2,1)S(1)}, bf16[16,3584]{1,0:T(8,128)(2,1)S(1)}, u32[]{:S(2)}, u32[]{:S(2)}) %collective-permute-start.15) | collective-permute-done | bytes 114720 | tf_op jit(solution)/shard_map/ppermute | solution.py:540
  83.5 1.8 %collective-permute-start.16 = (bf16[4,3584]{1,0:T(4,128)(2,1)S(1)}, bf16[4,3584]{1,0:T(4,128)(2,1)S(1)}, u32[]{:S(2)}, u32[]{:S(2)}) collective-permute-start(bf16[4,3584]{1,0:T(4,128)(2,1)S(1)} %get-tuple-element.39), channel_id=1, source_target_pairs={{0,4},{1,5},{2,6},{3,7},{4,0},{5,1},{6,2},{7,3},{8,12},{9,13},{10,... | collective-permute-start | bytes 86024 | tf_op jit(solution)/shard_map/ppermute | solution.py:540
  85.3 1.2 %collective-permute-start.17 = (bf16[4,3584]{1,0:T(4,128)(2,1)S(1)}, bf16[4,3584]{1,0:T(4,128)(2,1)S(1)}, u32[]{:S(2)}, u32[]{:S(2)}) collective-permute-start(bf16[4,3584]{1,0:T(4,128)(2,1)S(1)} %get-tuple-element.40), channel_id=1, source_target_pairs={{0,8},{1,9},{2,10},{3,11},{4,12},{5,13},{6,14},{7,15},{8,0},{9,1},... | collective-permute-start | bytes 86024 | tf_op jit(solution)/shard_map/ppermute | solution.py:540
  86.5 1.5 %collective-permute-start.18 = (bf16[4,3584]{1,0:T(4,128)(2,1)S(1)}, bf16[4,3584]{1,0:T(4,128)(2,1)S(1)}, u32[]{:S(2)}, u32[]{:S(2)}) collective-permute-start(bf16[4,3584]{1,0:T(4,128)(2,1)S(1)} %get-tuple-element.41), channel_id=1, source_target_pairs={{0,12},{1,13},{2,14},{3,15},{4,8},{5,9},{6,10},{7,11},{8,4},{9,5},... | collective-permute-start | bytes 86024 | tf_op jit(solution)/shard_map/ppermute | solution.py:540
  88.0 2.1 %collective-permute-done.17.refs_2_ = bf16[4,3584]{1,0:T(4,128)(2,1)S(1)} collective-permute-done((bf16[4,3584]{1,0:T(4,128)(2,1)S(1)}, bf16[4,3584]{1,0:T(4,128)(2,1)S(1)}, u32[]{:S(2)}, u32[]{:S(2)}) %collective-permute-start.17) | collective-permute-done | bytes 28704 | tf_op jit(solution)/shard_map/ppermute | solution.py:540
  90.1 2.1 %collective-permute-done.18.refs_3_ = bf16[4,3584]{1,0:T(4,128)(2,1)S(1)} collective-permute-done((bf16[4,3584]{1,0:T(4,128)(2,1)S(1)}, bf16[4,3584]{1,0:T(4,128)(2,1)S(1)}, u32[]{:S(2)}, u32[]{:S(2)}) %collective-permute-start.18) | collective-permute-done | bytes 28704 | tf_op jit(solution)/shard_map/ppermute | solution.py:540
  (43 shorter events, 9.3 us)
Async XLA Ops:
  0.6 28.6 %copy-start.1 = (bf16[256,3584]{1,0:T(8,128)(2,1)S(1)}, bf16[256,3584]{1,0:T(8,128)(2,1)}, u32[]{:S(2)}) copy-start(bf16[256,3584]{1,0:T(8,128)(2,1)} %w_out.1) | copy-start | bytes 5505028
  0.6 28.6 %copy-start.2 = (bf16[2,512,128]{2,1,0:T(8,128)(2,1)S(1)}, bf16[2,512,128]{2,1,0:T(8,128)(2,1)}, u32[]{:S(2)}) copy-start(bf16[2,512,128]{2,1,0:T(8,128)(2,1)} %w_uv.1) | copy-start | bytes 786436
  0.7 42.4 %copy-start.6 = (s32[4,8]{1,0:T(4,128)S(1)}, s32[4,8]{1,0:T(4,128)}, u32[]{:S(2)}) copy-start(s32[4,8]{1,0:T(4,128)} %routes.1) | copy-start | bytes 388
  0.7 42.4 %copy-start.5 = (f32[3584]{0:T(1024)S(1)}, f32[3584]{0:T(1024)}, u32[]{:S(2)}) copy-start(f32[3584]{0:T(1024)} %gain.1) | copy-start | bytes 43012
  0.7 42.4 %copy-start.4 = (bf16[4,3584]{1,0:T(4,128)(2,1)S(1)}, bf16[4,3584]{1,0:T(4,128)(2,1)}, u32[]{:S(2)}) copy-start(bf16[4,3584]{1,0:T(4,128)(2,1)} %residual.1) | copy-start | bytes 86020
  3.3 10.3 %collective-permute-start = (bf16[4,64,512]{2,1,0:T(8,128)(2,1)}, bf16[4,64,512]{2,1,0:T(8,128)(2,1)S(1)}, u32[]{:S(2)}, u32[]{:S(2)}) collective-permute-start(bf16[4,64,512]{2,1,0:T(8,128)(2,1)} %get-tuple-element.22), channel_id=1, source_target_pairs={{0,16},{1,17},{2,18},{3,19},{4,20},{5,21},{6,22},{7,23},{8,24},{9,... | collective-permute-start | bytes 786440 | tf_op jit(solution)/shard_map/ppermute | solution.py:540
  6.3 7.3 %collective-permute-start.1 = (bf16[8,2176]{1,0:T(8,128)(2,1)}, bf16[8,2176]{1,0:T(8,128)(2,1)S(1)}, u32[]{:S(2)}, u32[]{:S(2)}) collective-permute-start(bf16[8,2176]{1,0:T(8,128)(2,1)} %get-tuple-element.23), channel_id=1, source_target_pairs={{0,16},{1,17},{2,18},{3,19},{4,20},{5,21},{6,22},{7,23},{8,24},{9,... | collective-permute-start | bytes 104456 | tf_op jit(solution)/shard_map/ppermute | solution.py:540
  30.0 1.6 %collective-permute-start.2 = (bf16[32,3584]{1,0:T(8,128)(2,1)S(1)}, bf16[32,3584]{1,0:T(8,128)(2,1)S(1)}, u32[]{:S(2)}, u32[]{:S(2)}) collective-permute-start(bf16[32,3584]{1,0:T(8,128)(2,1)S(1)} %get-tuple-element.26), channel_id=1, source_target_pairs={{0,1},{1,0},{2,3},{3,2},{4,5},{5,4},{6,7},{7,6},{8,9},{9,8},{10,11... | collective-permute-start | bytes 688136 | tf_op jit(solution)/shard_map/ppermute | solution.py:540
  43.8 5.7 %collective-permute-start.5 = (bf16[1,4,3712]{2,1,0:T(4,128)(2,1)S(1)}, bf16[1,4,3712]{2,1,0:T(4,128)(2,1)S(1)}, u32[]{:S(2)}, u32[]{:S(2)}) collective-permute-start(bf16[1,4,3712]{2,1,0:T(4,128)(2,1)S(1)} %get-tuple-element.28.refs_0_), channel_id=1, source_target_pairs={{0,12},{1,13},{2,14},{3,15},{4,8},{5,9},{6,10},{7,11},{8,4},{9,5},... | collective-permute-start | bytes 89096 | tf_op jit(solution)/shard_map/ppermute | solution.py:540
  44.7 5.5 %collective-permute-start.4 = (bf16[1,4,3712]{2,1,0:T(4,128)(2,1)S(1)}, bf16[1,4,3712]{2,1,0:T(4,128)(2,1)S(1)}, u32[]{:S(2)}, u32[]{:S(2)}) collective-permute-start(bf16[1,4,3712]{2,1,0:T(4,128)(2,1)S(1)} %get-tuple-element.28.refs_0_), channel_id=1, source_target_pairs={{0,8},{1,9},{2,10},{3,11},{4,12},{5,13},{6,14},{7,15},{8,0},{9,1},... | collective-permute-start | bytes 89096 | tf_op jit(solution)/shard_map/ppermute | solution.py:540
  46.1 4.2 %collective-permute-start.3 = (bf16[1,4,3712]{2,1,0:T(4,128)(2,1)S(1)}, bf16[1,4,3712]{2,1,0:T(4,128)(2,1)S(1)}, u32[]{:S(2)}, u32[]{:S(2)}) collective-permute-start(bf16[1,4,3712]{2,1,0:T(4,128)(2,1)S(1)} %get-tuple-element.28.refs_0_), channel_id=1, source_target_pairs={{0,4},{1,5},{2,6},{3,7},{4,0},{5,1},{6,2},{7,3},{8,12},{9,13},{10,... | collective-permute-start | bytes 89096 | tf_op jit(solution)/shard_map/ppermute | solution.py:540
  50.3 5.8 %collective-permute-start.6 = (bf16[4,4,3712]{2,1,0:T(4,128)(2,1)S(1)}, bf16[4,4,3712]{2,1,0:T(4,128)(2,1)S(1)}, u32[]{:S(2)}, u32[]{:S(2)}) collective-permute-start(bf16[4,4,3712]{2,1,0:T(4,128)(2,1)S(1)} %shard_map.200.refs_0_), channel_id=1, source_target_pairs={{0,16},{1,3},{2,18},{3,1},{4,20},{5,7},{6,22},{7,5},{8,24},{9,11},... | collective-permute-start | bytes 356360 | tf_op jit(solution)/shard_map/ppermute | solution.py:540
  51.9 10.9 %collective-permute-start.7 = (bf16[4,4,3712]{2,1,0:T(4,128)(2,1)S(1)}, bf16[4,4,3712]{2,1,0:T(4,128)(2,1)S(1)}, u32[]{:S(2)}, u32[]{:S(2)}) collective-permute-start(bf16[4,4,3712]{2,1,0:T(4,128)(2,1)S(1)} %shard_map.200.refs_0_), channel_id=1, source_target_pairs={{0,2},{1,17},{2,0},{3,19},{4,6},{5,21},{6,4},{7,23},{8,10},{9,25},... | collective-permute-start | bytes 356360 | tf_op jit(solution)/shard_map/ppermute | solution.py:540
  56.1 6.8 %collective-permute-start.8 = (bf16[4,4,3712]{2,1,0:T(4,128)(2,1)S(1)}, bf16[4,4,3712]{2,1,0:T(4,128)(2,1)S(1)}, u32[]{:S(2)}, u32[]{:S(2)}) collective-permute-start(bf16[4,4,3712]{2,1,0:T(4,128)(2,1)S(1)} %collective-permute-done.6.passed), channel_id=1, source_target_pairs={{0,2},{1,17},{2,0},{3,19},{4,6},{5,21},{6,4},{7,23},{8,10},{9,25},... | collective-permute-start | bytes 356360 | tf_op jit(solution)/shard_map/ppermute | solution.py:540
  56.9 6.4 %collective-permute-start.9 = (bf16[4,4,3712]{2,1,0:T(4,128)(2,1)S(1)}, bf16[4,4,3712]{2,1,0:T(4,128)(2,1)S(1)}, u32[]{:S(2)}, u32[]{:S(2)}) collective-permute-start(bf16[4,4,3712]{2,1,0:T(4,128)(2,1)S(1)} %shard_map.200.refs_0_), channel_id=1, source_target_pairs={{0,1},{1,0},{2,3},{3,2},{4,5},{5,4},{6,7},{7,6},{8,9},{9,8},{10,11... | collective-permute-start | bytes 356360 | tf_op jit(solution)/shard_map/ppermute | solution.py:540
  62.2 1.9 %collective-permute-start.10 = (bf16[4,4,3712]{2,1,0:T(4,128)(2,1)S(1)}, bf16[4,4,3712]{2,1,0:T(4,128)(2,1)S(1)}, u32[]{:S(2)}, u32[]{:S(2)}) collective-permute-start(bf16[4,4,3712]{2,1,0:T(4,128)(2,1)S(1)} %get-tuple-element.29.refs_1_), channel_id=1, source_target_pairs={{0,1},{1,0},{2,3},{3,2},{4,5},{5,4},{6,7},{7,6},{8,9},{9,8},{10,11... | collective-permute-start | bytes 356360 | tf_op jit(solution)/shard_map/ppermute | solution.py:540
  62.8 1.3 %collective-permute-start.11 = (bf16[4,4,3712]{2,1,0:T(4,128)(2,1)S(1)}, bf16[4,4,3712]{2,1,0:T(4,128)(2,1)S(1)}, u32[]{:S(2)}, u32[]{:S(2)}) collective-permute-start(bf16[4,4,3712]{2,1,0:T(4,128)(2,1)S(1)} %collective-permute-done.7.refs_2_), channel_id=1, source_target_pairs={{0,1},{1,0},{2,3},{3,2},{4,5},{5,4},{6,7},{7,6},{8,9},{9,8},{10,11... | collective-permute-start | bytes 356360 | tf_op jit(solution)/shard_map/ppermute | solution.py:540
  62.9 1.4 %collective-permute-start.12 = (bf16[4,4,3712]{2,1,0:T(4,128)(2,1)S(1)}, bf16[4,4,3712]{2,1,0:T(4,128)(2,1)S(1)}, u32[]{:S(2)}, u32[]{:S(2)}) collective-permute-start(bf16[4,4,3712]{2,1,0:T(4,128)(2,1)S(1)} %collective-permute-done.8.refs_3_), channel_id=1, source_target_pairs={{0,1},{1,0},{2,3},{3,2},{4,5},{5,4},{6,7},{7,6},{8,9},{9,8},{10,11... | collective-permute-start | bytes 356360 | tf_op jit(solution)/shard_map/ppermute | solution.py:540
  70.5 1.9 %collective-permute-start.13 = (bf16[64,3584]{1,0:T(8,128)(2,1)S(1)}, bf16[64,3584]{1,0:T(8,128)(2,1)S(1)}, u32[]{:S(2)}, u32[]{:S(2)}) collective-permute-start(bf16[64,3584]{1,0:T(8,128)(2,1)S(1)} %get-tuple-element.33), channel_id=1, source_target_pairs={{0,1},{1,0},{2,3},{3,2},{4,5},{5,4},{6,7},{7,6},{8,9},{9,8},{10,11... | collective-permute-start | bytes 1376264 | tf_op jit(solution)/shard_map/ppermute | solution.py:540
  72.5 6.1 %collective-permute-start.14 = (bf16[32,3584]{1,0:T(8,128)(2,1)S(1)}, bf16[32,3584]{1,0:T(8,128)(2,1)S(1)}, u32[]{:S(2)}, u32[]{:S(2)}) collective-permute-start(bf16[32,3584]{1,0:T(8,128)(2,1)S(1)} %get-tuple-element.35), channel_id=1, source_target_pairs={{0,2},{1,17},{2,0},{3,19},{4,6},{5,21},{6,4},{7,23},{8,10},{9,25},... | collective-permute-start | bytes 688136 | tf_op jit(solution)/shard_map/ppermute | solution.py:540
  78.6 4.9 %collective-permute-start.15 = (bf16[16,3584]{1,0:T(8,128)(2,1)S(1)}, bf16[16,3584]{1,0:T(8,128)(2,1)S(1)}, u32[]{:S(2)}, u32[]{:S(2)}) collective-permute-start(bf16[16,3584]{1,0:T(8,128)(2,1)S(1)} %get-tuple-element.37), channel_id=1, source_target_pairs={{0,16},{1,3},{2,18},{3,1},{4,20},{5,7},{6,22},{7,5},{8,24},{9,11},... | collective-permute-start | bytes 344072 | tf_op jit(solution)/shard_map/ppermute | solution.py:540
  83.5 4.5 %collective-permute-start.16 = (bf16[4,3584]{1,0:T(4,128)(2,1)S(1)}, bf16[4,3584]{1,0:T(4,128)(2,1)S(1)}, u32[]{:S(2)}, u32[]{:S(2)}) collective-permute-start(bf16[4,3584]{1,0:T(4,128)(2,1)S(1)} %get-tuple-element.39), channel_id=1, source_target_pairs={{0,4},{1,5},{2,6},{3,7},{4,0},{5,1},{6,2},{7,3},{8,12},{9,13},{10,... | collective-permute-start | bytes 86024 | tf_op jit(solution)/shard_map/ppermute | solution.py:540
  85.3 4.8 %collective-permute-start.17 = (bf16[4,3584]{1,0:T(4,128)(2,1)S(1)}, bf16[4,3584]{1,0:T(4,128)(2,1)S(1)}, u32[]{:S(2)}, u32[]{:S(2)}) collective-permute-start(bf16[4,3584]{1,0:T(4,128)(2,1)S(1)} %get-tuple-element.40), channel_id=1, source_target_pairs={{0,8},{1,9},{2,10},{3,11},{4,12},{5,13},{6,14},{7,15},{8,0},{9,1},... | collective-permute-start | bytes 86024 | tf_op jit(solution)/shard_map/ppermute | solution.py:540
  86.5 5.7 %collective-permute-start.18 = (bf16[4,3584]{1,0:T(4,128)(2,1)S(1)}, bf16[4,3584]{1,0:T(4,128)(2,1)S(1)}, u32[]{:S(2)}, u32[]{:S(2)}) collective-permute-start(bf16[4,3584]{1,0:T(4,128)(2,1)S(1)} %get-tuple-element.41), channel_id=1, source_target_pairs={{0,12},{1,13},{2,14},{3,15},{4,8},{5,9},{6,10},{7,11},{8,4},{9,5},... | collective-permute-start | bytes 86024 | tf_op jit(solution)/shard_map/ppermute | solution.py:540
  (2 other events, 15.1 us)

commit v3 on v2

--- a/solution.py
+++ b/solution.py
@@ -23,6 +23,7 @@
 EXPERT = ("far", "side", "core")
 ROWS = DP + EXPERT
 FAR = ("low", "far")
+CHIP = ("far", "side")
 LOAD_MIB = 36
 EXPERT_MIB = 36
 
@@ -368,30 +369,30 @@
     out[...] = result.reshape(out.shape).astype(BF16)
 
 
-def project_kernel(tokens, blocks, w_uv, w_out, away, kept):
-    devices = blocks.shape[0]
+def project_kernel(tokens, blocks, w_uv, other_uv, w_out, other_out, out):
+    chips = blocks.shape[0]
     per_device = w_uv.shape[0]
     core = lax.axis_index("core")
     stacked = blocks[...].astype(F32).reshape(-1, blocks.shape[2]).astype(BF16)
     rows = stacked.shape[0]
-    row_head = (iota((rows, 1), 0) // tokens) % per_device
+    row_head = (iota((rows, 1), 0) // tokens) % (2 * per_device)
     values = []
-    for head in range(per_device):
-        part = dot_nn(stacked, w_uv[head])
-        values.append(jnp.where(row_head == head, part, 0.0).astype(BF16))
+    for first, uv in ((core * per_device, w_uv), ((1 - core) * per_device, other_uv)):
+        for head in range(per_device):
+            part = dot_nn(stacked, uv[head])
+            values.append(jnp.where(row_head == first + head, part, 0.0).astype(BF16))
     values = jnp.concatenate(values, axis=1)
-    half = devices // 2 * tokens
-    out_row = iota((2 * half, rows), 0)
-    in_row = iota((2 * half, rows), 1)
-    out_device = (out_row % half) // tokens * 2 + jnp.where(out_row < half, 1 - core, core)
-    same = (in_row // (tokens * per_device) == out_device) & (in_row % tokens == out_row % tokens)
+    out_row = iota((chips * tokens, rows), 0)
+    in_row = iota((chips * tokens, rows), 1)
+    same_chip = in_row // (tokens * 2 * per_device) == out_row // tokens
+    same = same_chip & (in_row % tokens == out_row % tokens)
     joined = dot_nn(jnp.where(same, 1.0, 0.0).astype(BF16), values).astype(BF16)
-    width = w_out.shape[1]
+    depth, width = w_out.shape
     step = 512 if width % 512 == 0 else width
     for at in range(0, width, step):
-        part = dot_nn(joined, w_out[:, at : at + step])
-        away[:, at : at + step] = part[:half].astype(BF16)
-        kept[:, at : at + step] = part[half:]
+        part = dot_nn(joined[:, :depth], w_out[:, at : at + step])
+        part = part + dot_nn(joined[:, depth:], other_out[:, at : at + step])
+        out[:, :, at : at + step] = part.reshape(chips, tokens, step).astype(BF16)
 
 
 def split_kernel(kept, got, out):
@@ -452,7 +453,7 @@
 def expert_kernel(top, count, *refs):
     pieces = refs[:count]
     w_router, w_gate, w_up, down_hbm = refs[count : count + 4]
-    kept, away, rows_ref, hidden_ref, w_down, sems = refs[count + 4 :]
+    kept, away, rows_ref, hidden_ref, acc, w_down, sems = refs[count + 4 :]
     expert = lax.axis_index(EXPERT)
     width, units = w_gate.shape
     in_step = 256 if units % 256 == 0 else units
@@ -460,9 +461,9 @@
     down_copies = fetch(
         [
             pltpu.make_async_copy(
-                down_hbm.at[0, :, pl.ds(at, out_step)], w_down.at[:, pl.ds(at, out_step)], sems.at[i]
+                down_hbm.at[0, pl.ds(at, in_step)], w_down.at[pl.ds(at, in_step)], sems.at[i]
             )
-            for i, at in enumerate(range(0, width, out_step))
+            for i, at in enumerate(range(0, units, in_step))
         ]
     )
     piece_rows = rows_ref.shape[0] // count
@@ -486,13 +487,22 @@
         gate = dot_nn(rows, w_gate[:, at : at + in_step])
         up = dot_nn(rows, w_up[:, at : at + in_step])
         hidden_ref[:, at : at + in_step] = (gate / (1.0 + jnp.exp(-gate)) * up).astype(BF16)
-    hidden = hidden_ref[...]
     half = rows_ref.shape[0] // 2
-    for i, at in enumerate(range(0, width, out_step)):
-        down_copies[i].wait()
-        part = dot_nn(hidden, w_down[:, at : at + out_step]) * gates
-        kept[:, at : at + out_step] = part[:half]
-        away[:, at : at + out_step] = part[half:].astype(BF16)
+    steps = units // in_step
+    for i, down_copy in enumerate(down_copies):
+        down_copy.wait()
+        span = slice(i * in_step, (i + 1) * in_step)
+        hidden = hidden_ref[:, span]
+        for at in range(0, width, out_step):
+            part = dot_nn(hidden, w_down[span, at : at + out_step])
+            if i:
+                part = part + acc[:, at : at + out_step]
+            if i < steps - 1:
+                acc[:, at : at + out_step] = part
+            else:
+                part = part * gates
+                kept[:, at : at + out_step] = part[:half]
+                away[:, at : at + out_step] = part[half:].astype(BF16)
 
 
 def halve_kernel(kept, got, keep, away):
@@ -552,6 +562,8 @@
     partners = dp_count - 1
     rows = tokens * heads
     sizes = (heads, per_device, rollouts, following, view)
+    chips = expert_count // 2
+    other_uv, other_out = swap(w_uv, 1), swap(w_out, 1)
 
     picked = call(
         functools.partial(pick_kernel, partners, moves),
@@ -569,7 +581,7 @@
             pltpu.SemaphoreType.DMA((partners, moves)),
             pltpu.SemaphoreType.DMA((4,)),
         ],
-        vmem=60,
+        vmem=57,
     )
     got_lat = [swap(picked[k], (k + 1) * expert_count) for k in range(partners)]
     got_rope = [swap(picked[partners + k], (k + 1) * expert_count) for k in range(partners)]
@@ -611,32 +623,26 @@
             pltpu.SemaphoreType.DMA((9,)),
             pltpu.SemaphoreType.DMA((slots // GROUP,)),
         ],
-        vmem=60,
+        vmem=57,
         cost=(2 * slots * page_len * rows * (2 * latent + 2 * rope_dim), 4 * MIB),
     )
     blocks = call(
         functools.partial(merge_kernel, partners),
-        [shape((expert_count, tokens * per_device, latent), BF16)],
+        [shape((chips, 2 * tokens * per_device, latent), BF16)],
         (*got_lat, *got_rope, *local),
         scratch=[pltpu.VMEM((rows // LANES, partners * moves * page_len, LANES), F32)],
         cost=(2 * moves * page_len * rows * 2 * latent, MIB),
     )[0]
 
-    blocks = deal(blocks, EXPERT)
-
-    half_rows = expert_count // 2 * tokens
-    away, kept = call(
+    blocks = deal(blocks, CHIP)
+
+    parts = call(
         functools.partial(project_kernel, tokens),
-        [shape((half_rows, width), BF16), shape((half_rows, width), F32)],
-        (blocks, w_uv, w_out),
-        cost=(4 * half_rows * width * w_out.shape[0], 4 * MIB),
-    )
-    parts = call(
-        split_kernel,
-        [shape((expert_count // 2, tokens, width), BF16)],
-        (kept, swap(away, 1)),
+        [shape((chips, tokens, width), BF16)],
+        (blocks, w_uv, other_uv, w_out, other_out),
+        cost=(4 * chips * tokens * width * w_out.shape[0], 8 * MIB),
     )[0]
-    parts = deal(parts, ("far", "side"))
+    parts = deal(parts, CHIP)
     far_count = total_devices // 8
     masks = [2 * side_bit * k for k in range(far_count)]
     direct = far_count <= 4
@@ -686,6 +692,7 @@
         scratch=[
             pltpu.VMEM((all_rows, width), BF16),
             pltpu.VMEM((all_rows, hidden_units), BF16),
+            pltpu.VMEM((all_rows, width), F32),
             pltpu.VMEM(w_down.shape[1:], BF16),
             pltpu.SemaphoreType.DMA((16,)),
         ],

time: 93.1 us -> 93 us (level)
  blocking collectives: 25.5 us -> 10.4 us
  starting transfers between devices: 19.9 us -> 26.3 us
  waiting for transfers between devices: 21.4 us -> 26.5 us
  Pallas kernels: 24.1 us -> 27.5 us
    all_to_all x2 -> x1, blocking collectives: 25.5 us -> 10.4 us  [deal(): return lax.all_to_all(x, names, split_axis=0, concat_axis=0, tiled=True)]
    all_to_all x0 -> x1, waiting for transfers between devices: none -> 7.34 us  [deal(): return lax.all_to_all(x, names, split_axis=0, concat_axis=0, tiled=True)]
    all_to_all x0 -> x1, starting transfers between devices: none -> 6.08 us  [deal(): return lax.all_to_all(x, names, split_axis=0, concat_axis=0, tiled=True)]
    pallas_call x13 -> x12, Pallas kernels: 24.1 us -> 27.5 us  [call(): pl.pallas_call(kernel, out_shape=outs, in_specs=in_specs or [VMEM] * len(...]
    ppermute x19 -> x20, waiting for transfers between devices: 21.4 us -> 19.1 us  [swap(): return lax.ppermute(x, ROWS, pairs)]
    ppermute x19 -> x20, starting transfers between devices: 19.9 us -> 20.2 us  [swap(): return lax.ppermute(x, ROWS, pairs)]
  transfers between devices with their start and end apart: 19 -> 21, of which waited for: 13 -> 12; matrix products, arithmetic and copies ran while one was open for 0% -> 0% of each run, Pallas kernels for 13% -> 17%
where the time goes in v3:
time: 93 us; the launch traced here: 92.6 us
  Pallas kernels  27.5 us (30%)
  waiting for transfers between devices  26.5 us (28%)
  starting transfers between devices  26.3 us (28%)
  blocking collectives  10.4 us (11%)
  local copies, waits for them, and re-layouts  1.12 us (1%)
    pallas_call x12, Pallas kernels, call(): pl.pallas_call(kernel, out_shape=outs, in_specs=in_specs or [VMEM] * len(...  27.5 us
    ppermute x20, starting transfers between devices, swap(): return lax.ppermute(x, ROWS, pairs)  20.2 us
    ppermute x20, waiting for transfers between devices, swap(): return lax.ppermute(x, ROWS, pairs)  19.1 us
    all_to_all x1, blocking collectives, deal(): return lax.all_to_all(x, names, split_axis=0, concat_axis=0, tiled=True)  10.4 us
    all_to_all x1, waiting for transfers between devices, deal(): return lax.all_to_all(x, names, split_axis=0, concat_axis=0, tiled=True)  7.34 us
    all_to_all x1, starting transfers between devices, deal(): return lax.all_to_all(x, names, split_axis=0, concat_axis=0, tiled=True)  6.08 us
  transfers between devices with their start and end apart: 21, of which 12 were waited for; matrix products, arithmetic and copies ran while one was open for 0% of the time, Pallas kernels for 17%

profile of v3, /device:TPU:0, one launch (start us, length us, event | category | flops | bytes accessed | tf_op | source)
XLA Modules:
  0.0 92.6 jit_solution(15993240384065318759)
XLA Ops:
  1.2 2.6 %shard_map.194 = (bf16[4,64,512]{2,1,0:T(8,128)(2,1)}, bf16[8,2176]{1,0:T(8,128)(2,1)}, f32[48]{0:T(128)}) custom-call(s32[1,2,4]{2,1,0:T(2,128)} %move_hbm.3, bf16[48]{0:T(256)(128)(2,1)} %scale_hbm.1, bf16[48,64,512]{2,1,0:T(8,128)(2,1)} %lat_hbm.1, bf16[48,4096]{1,0:T(8,128)(2,1)} %rope_hbm.3), custom_call_target="tpu_custom_call" | custom-call | tf_op jit(solution)/shard_map/pallas_call | solution.py:45
  3.8 2.6 %collective-permute-start = (bf16[4,64,512]{2,1,0:T(8,128)(2,1)}, bf16[4,64,512]{2,1,0:T(8,128)(2,1)S(1)}, u32[]{:S(2)}, u32[]{:S(2)}) collective-permute-start(bf16[4,64,512]{2,1,0:T(8,128)(2,1)} %get-tuple-element.20), channel_id=1, source_target_pairs={{0,16},{1,17},{2,18},{3,19},{4,20},{5,21},{6,22},{7,23},{8,24},{9,... | collective-permute-start | bytes 786440 | tf_op jit(solution)/shard_map/ppermute | solution.py:550
  6.8 7.1 %shard_map.195.refs_2_ = f32[264,640]{1,0:T(8,128)} custom-call(f32[48]{0:T(128)} %get-tuple-element.22.scale_hbm, s32[2,32]{1,0:T(2,128)} %table_hbm.1, s32[2]{0:T(128)} %lengths_hbm.1, s32[1,2,4]{2,1,0:T(2,128)} %move_hbm.3, bf16[48,64,512]{2,1,0:T(8,128)(2,1)} %lat_hbm.1, bf16[48,4096]{1,0:T(8,128)(2,1)} %rope_hbm.3, bf16[2,2,32,512]{3,2,1,0:T(8,128)(2,1)} %q_hbm.1, ...), custom_call_target="tpu_custom_call" | custom-call | flops 905969664 | bytes 4194304 | tf_op jit(solution)/shard_map/pallas_call | solution.py:45
  15.3 1.2 %shard_map.196 = bf16[8,16,512]{2,1,0:T(8,128)(2,1)} custom-call(bf16[4,64,512]{2,1,0:T(8,128)(2,1)S(1)} %collective-permute-done.refs_0_, bf16[8,2176]{1,0:T(8,128)(2,1)S(1)} %collective-permute-done.1.refs_1_, f32[264,640]{1,0:T(8,128)S(1)} %copy-done), custom_call_target="tpu_custom_call" | custom-call | flops 67108864 | bytes 1048576 | tf_op jit(solution)/shard_map/pallas_call | solution.py:45
  16.4 6.1 %all-to-all-start = ((bf16[8,16,512]{2,1,0:T(8,128)(2,1)}), bf16[8,16,512]{2,1,0:T(8,128)(2,1)S(1)}, u32[]{:S(2)}, u32[]{:S(2)}) async-start(bf16[8,16,512]{2,1,0:T(8,128)(2,1)} %shard_map.196), calls=%async_computation | async-start | bytes 262144 | tf_op jit(solution)/shard_map/all_to_all | solution.py:553
  22.5 7.3 %all-to-all-done.blocks = bf16[8,16,512]{2,1,0:T(8,128)(2,1)S(1)} async-done(((bf16[8,16,512]{2,1,0:T(8,128)(2,1)}), bf16[8,16,512]{2,1,0:T(8,128)(2,1)S(1)}, u32[]{:S(2)}, u32[]{:S(2)}) %all-to-all-start) | async-done | bytes 131104 | tf_op jit(solution)/shard_map/all_to_all | solution.py:553
  29.9 2.6 %shard_map.197 = bf16[8,4,3584]{2,1,0:T(4,128)(2,1)S(1)} custom-call(bf16[8,16,512]{2,1,0:T(8,128)(2,1)S(1)} %all-to-all-done.blocks, bf16[2,512,128]{2,1,0:T(8,128)(2,1)S(1)} %copy-done.2, bf16[2,512,128]{2,1,0:T(8,128)(2,1)S(1)} %collective-permute-done.2.other_uv, bf16[256,3584]{1,0:T(8,128)(2,1)S(1)} %copy-done.1, ...), custom_call_target="tpu_custom_call" | custom-call | flops 117440512 | bytes 8388608 | tf_op jit(solution)/shard_map/pallas_call | solution.py:45
  32.5 10.4 %all_to_all.10.got = bf16[8,4,3584]{2,1,0:T(4,128)(2,1)S(1)} all-to-all(bf16[8,4,3584]{2,1,0:T(4,128)(2,1)S(1)} %shard_map.197), channel_id=1, replica_groups=mesh['top'=2,'low'=1,'far'=4,'side'=2,'core'=2] {'far','side'}, dimensions={0} | all-to-all | bytes 458752 | tf_op jit(solution)/shard_map/all_to_all | solution.py:553
  45.1 3.0 %collective-permute-start.4 = (bf16[1,4,3712]{2,1,0:T(4,128)(2,1)S(1)}, bf16[1,4,3712]{2,1,0:T(4,128)(2,1)S(1)}, u32[]{:S(2)}, u32[]{:S(2)}) collective-permute-start(bf16[1,4,3712]{2,1,0:T(4,128)(2,1)S(1)} %get-tuple-element.24.refs_0_), channel_id=1, source_target_pairs={{0,4},{1,5},{2,6},{3,7},{4,0},{5,1},{6,2},{7,3},{8,12},{9,13},{10,... | collective-permute-start | bytes 89096 | tf_op jit(solution)/shard_map/ppermute | solution.py:550
  48.0 1.3 %collective-permute-done.6.refs_3_ = bf16[1,4,3712]{2,1,0:T(4,128)(2,1)S(1)} collective-permute-done((bf16[1,4,3712]{2,1,0:T(4,128)(2,1)S(1)}, bf16[1,4,3712]{2,1,0:T(4,128)(2,1)S(1)}, u32[]{:S(2)}, u32[]{:S(2)}) %collective-permute-start.6) | collective-permute-done | bytes 29728 | tf_op jit(solution)/shard_map/ppermute | solution.py:550
  49.9 1.6 %collective-permute-start.7 = (bf16[4,4,3712]{2,1,0:T(4,128)(2,1)S(1)}, bf16[4,4,3712]{2,1,0:T(4,128)(2,1)S(1)}, u32[]{:S(2)}, u32[]{:S(2)}) collective-permute-start(bf16[4,4,3712]{2,1,0:T(4,128)(2,1)S(1)} %shard_map.199.refs_0_), channel_id=1, source_target_pairs={{0,16},{1,3},{2,18},{3,1},{4,20},{5,7},{6,22},{7,5},{8,24},{9,11},... | collective-permute-start | bytes 356360 | tf_op jit(solution)/shard_map/ppermute | solution.py:550
  51.5 1.2 %collective-permute-start.8 = (bf16[4,4,3712]{2,1,0:T(4,128)(2,1)S(1)}, bf16[4,4,3712]{2,1,0:T(4,128)(2,1)S(1)}, u32[]{:S(2)}, u32[]{:S(2)}) collective-permute-start(bf16[4,4,3712]{2,1,0:T(4,128)(2,1)S(1)} %shard_map.199.refs_0_), channel_id=1, source_target_pairs={{0,2},{1,17},{2,0},{3,19},{4,6},{5,21},{6,4},{7,23},{8,10},{9,25},... | collective-permute-start | bytes 356360 | tf_op jit(solution)/shard_map/ppermute | solution.py:550
  52.7 2.5 %collective-permute-done.7.passed = bf16[4,4,3712]{2,1,0:T(4,128)(2,1)S(1)} collective-permute-done((bf16[4,4,3712]{2,1,0:T(4,128)(2,1)S(1)}, bf16[4,4,3712]{2,1,0:T(4,128)(2,1)S(1)}, u32[]{:S(2)}, u32[]{:S(2)}) %collective-permute-start.7) | collective-permute-done | bytes 118816 | tf_op jit(solution)/shard_map/ppermute | solution.py:550
  56.0 5.3 %shard_map.200 = (bf16[4,4,3712]{2,1,0:T(4,128)(2,1)S(1)}, bf16[3584,1024]{1,0:T(8,128)(2,1)S(1)}, bf16[3584,1024]{1,0:T(8,128)(2,1)S(1)}) custom-call(bf16[4,4,3712]{2,1,0:T(4,128)(2,1)S(1)} %collective-permute-done.7.passed, bf16[1,3584,1024]{2,1,0:T(8,128)(2,1)} %refs_0_.1, bf16[1,3584,1024]{2,1,0:T(8,128)(2,1)} %refs_1_.1), custom_call_target="tpu_custom_call" | custom-call | bytes 14680064 | tf_op jit(solution)/shard_map/pallas_call | solution.py:45
  63.4 7.2 %shard_map.201 = (f32[64,3584]{1,0:T(8,128)S(1)}, bf16[64,3584]{1,0:T(8,128)(2,1)S(1)}) custom-call(bf16[4,4,3712]{2,1,0:T(4,128)(2,1)S(1)} %shard_map.199.refs_0_, bf16[4,4,3712]{2,1,0:T(4,128)(2,1)S(1)} %get-tuple-element.25.refs_1_, bf16[4,4,3712]{2,1,0:T(4,128)(2,1)S(1)} %collective-permute-done.8.refs_2_, ...), custom_call_target="tpu_custom_call" | custom-call | flops 2818572288 | bytes 22020096 | tf_op jit(solution)/shard_map/pallas_call | solution.py:45
  71.0 1.5 %collective-permute-done.14.got = bf16[64,3584]{1,0:T(8,128)(2,1)S(1)} collective-permute-done((bf16[64,3584]{1,0:T(8,128)(2,1)S(1)}, bf16[64,3584]{1,0:T(8,128)(2,1)S(1)}, u32[]{:S(2)}, u32[]{:S(2)}) %collective-permute-start.14) | collective-permute-done | bytes 458784 | tf_op jit(solution)/shard_map/ppermute | solution.py:550
  72.6 1.2 %collective-permute-start.15 = (bf16[32,3584]{1,0:T(8,128)(2,1)S(1)}, bf16[32,3584]{1,0:T(8,128)(2,1)S(1)}, u32[]{:S(2)}, u32[]{:S(2)}) collective-permute-start(bf16[32,3584]{1,0:T(8,128)(2,1)S(1)} %get-tuple-element.31), channel_id=1, source_target_pairs={{0,2},{1,17},{2,0},{3,19},{4,6},{5,21},{6,4},{7,23},{8,10},{9,25},... | collective-permute-start | bytes 688136 | tf_op jit(solution)/shard_map/ppermute | solution.py:550
  73.8 4.8 %collective-permute-done.15.got = bf16[32,3584]{1,0:T(8,128)(2,1)S(1)} collective-permute-done((bf16[32,3584]{1,0:T(8,128)(2,1)S(1)}, bf16[32,3584]{1,0:T(8,128)(2,1)S(1)}, u32[]{:S(2)}, u32[]{:S(2)}) %collective-permute-start.15) | collective-permute-done | bytes 229408 | tf_op jit(solution)/shard_map/ppermute | solution.py:550
  78.7 1.6 %collective-permute-start.16 = (bf16[16,3584]{1,0:T(8,128)(2,1)S(1)}, bf16[16,3584]{1,0:T(8,128)(2,1)S(1)}, u32[]{:S(2)}, u32[]{:S(2)}) collective-permute-start(bf16[16,3584]{1,0:T(8,128)(2,1)S(1)} %get-tuple-element.33), channel_id=1, source_target_pairs={{0,16},{1,3},{2,18},{3,1},{4,20},{5,7},{6,22},{7,5},{8,24},{9,11},... | collective-permute-start | bytes 344072 | tf_op jit(solution)/shard_map/ppermute | solution.py:550
  80.3 3.3 %collective-permute-done.16.got = bf16[16,3584]{1,0:T(8,128)(2,1)S(1)} collective-permute-done((bf16[16,3584]{1,0:T(8,128)(2,1)S(1)}, bf16[16,3584]{1,0:T(8,128)(2,1)S(1)}, u32[]{:S(2)}, u32[]{:S(2)}) %collective-permute-start.16) | collective-permute-done | bytes 114720 | tf_op jit(solution)/shard_map/ppermute | solution.py:550
  83.6 1.8 %collective-permute-start.17 = (bf16[4,3584]{1,0:T(4,128)(2,1)S(1)}, bf16[4,3584]{1,0:T(4,128)(2,1)S(1)}, u32[]{:S(2)}, u32[]{:S(2)}) collective-permute-start(bf16[4,3584]{1,0:T(4,128)(2,1)S(1)} %get-tuple-element.35), channel_id=1, source_target_pairs={{0,4},{1,5},{2,6},{3,7},{4,0},{5,1},{6,2},{7,3},{8,12},{9,13},{10,... | collective-permute-start | bytes 86024 | tf_op jit(solution)/shard_map/ppermute | solution.py:550
  86.3 1.8 %collective-permute-start.19 = (bf16[4,3584]{1,0:T(4,128)(2,1)S(1)}, bf16[4,3584]{1,0:T(4,128)(2,1)S(1)}, u32[]{:S(2)}, u32[]{:S(2)}) collective-permute-start(bf16[4,3584]{1,0:T(4,128)(2,1)S(1)} %get-tuple-element.37), channel_id=1, source_target_pairs={{0,12},{1,13},{2,14},{3,15},{4,8},{5,9},{6,10},{7,11},{8,4},{9,5},... | collective-permute-start | bytes 86024 | tf_op jit(solution)/shard_map/ppermute | solution.py:550
  88.1 2.1 %collective-permute-done.18.refs_2_ = bf16[4,3584]{1,0:T(4,128)(2,1)S(1)} collective-permute-done((bf16[4,3584]{1,0:T(4,128)(2,1)S(1)}, bf16[4,3584]{1,0:T(4,128)(2,1)S(1)}, u32[]{:S(2)}, u32[]{:S(2)}) %collective-permute-start.18) | collective-permute-done | bytes 28704 | tf_op jit(solution)/shard_map/ppermute | solution.py:550
  90.2 1.8 %collective-permute-done.19.refs_3_ = bf16[4,3584]{1,0:T(4,128)(2,1)S(1)} collective-permute-done((bf16[4,3584]{1,0:T(4,128)(2,1)S(1)}, bf16[4,3584]{1,0:T(4,128)(2,1)S(1)}, u32[]{:S(2)}, u32[]{:S(2)}) %collective-permute-start.19) | collective-permute-done | bytes 28704 | tf_op jit(solution)/shard_map/ppermute | solution.py:550
  (45 shorter events, 10.1 us)
Async XLA Ops:
  0.7 42.3 %copy-start.6 = (s32[4,8]{1,0:T(4,128)S(1)}, s32[4,8]{1,0:T(4,128)}, u32[]{:S(2)}) copy-start(s32[4,8]{1,0:T(4,128)} %routes.1) | copy-start | bytes 388
  0.7 42.3 %copy-start.5 = (f32[3584]{0:T(1024)S(1)}, f32[3584]{0:T(1024)}, u32[]{:S(2)}) copy-start(f32[3584]{0:T(1024)} %gain.1) | copy-start | bytes 43012
  0.7 42.2 %copy-start.4 = (bf16[4,3584]{1,0:T(4,128)(2,1)S(1)}, bf16[4,3584]{1,0:T(4,128)(2,1)}, u32[]{:S(2)}) copy-start(bf16[4,3584]{1,0:T(4,128)(2,1)} %residual.1) | copy-start | bytes 86020
  0.7 29.2 %collective-permute-start.3 = (bf16[256,3584]{1,0:T(8,128)(2,1)}, bf16[256,3584]{1,0:T(8,128)(2,1)}, u32[]{:S(2)}, u32[]{:S(2)}) collective-permute-start(bf16[256,3584]{1,0:T(8,128)(2,1)} %w_out.1), channel_id=1, source_target_pairs={{0,1},{1,0},{2,3},{3,2},{4,5},{5,4},{6,7},{7,6},{8,9},{9,8},{10,11... | collective-permute-start | bytes 5505032 | tf_op jit(solution)/shard_map/ppermute | solution.py:550
  3.8 10.4 %collective-permute-start = (bf16[4,64,512]{2,1,0:T(8,128)(2,1)}, bf16[4,64,512]{2,1,0:T(8,128)(2,1)S(1)}, u32[]{:S(2)}, u32[]{:S(2)}) collective-permute-start(bf16[4,64,512]{2,1,0:T(8,128)(2,1)} %get-tuple-element.20), channel_id=1, source_target_pairs={{0,16},{1,17},{2,18},{3,19},{4,20},{5,21},{6,22},{7,23},{8,24},{9,... | collective-permute-start | bytes 786440 | tf_op jit(solution)/shard_map/ppermute | solution.py:550
  6.4 16.1 %collective-permute-start.2 = (bf16[2,512,128]{2,1,0:T(8,128)(2,1)}, bf16[2,512,128]{2,1,0:T(8,128)(2,1)S(1)}, u32[]{:S(2)}, u32[]{:S(2)}) collective-permute-start(bf16[2,512,128]{2,1,0:T(8,128)(2,1)} %w_uv.1), channel_id=1, source_target_pairs={{0,1},{1,0},{2,3},{3,2},{4,5},{5,4},{6,7},{7,6},{8,9},{9,8},{10,11... | collective-permute-start | bytes 786440 | tf_op jit(solution)/shard_map/ppermute | solution.py:550
  6.4 7.7 %collective-permute-start.1 = (bf16[8,2176]{1,0:T(8,128)(2,1)}, bf16[8,2176]{1,0:T(8,128)(2,1)S(1)}, u32[]{:S(2)}, u32[]{:S(2)}) collective-permute-start(bf16[8,2176]{1,0:T(8,128)(2,1)} %get-tuple-element.21), channel_id=1, source_target_pairs={{0,16},{1,17},{2,18},{3,19},{4,20},{5,21},{6,22},{7,23},{8,24},{9,... | collective-permute-start | bytes 104456 | tf_op jit(solution)/shard_map/ppermute | solution.py:550
  16.4 13.4 %all-to-all-start = ((bf16[8,16,512]{2,1,0:T(8,128)(2,1)}), bf16[8,16,512]{2,1,0:T(8,128)(2,1)S(1)}, u32[]{:S(2)}, u32[]{:S(2)}) async-start(bf16[8,16,512]{2,1,0:T(8,128)(2,1)} %shard_map.196), calls=%async_computation | async-start | bytes 262144 | tf_op jit(solution)/shard_map/all_to_all | solution.py:553
  43.6 5.7 %collective-permute-start.6 = (bf16[1,4,3712]{2,1,0:T(4,128)(2,1)S(1)}, bf16[1,4,3712]{2,1,0:T(4,128)(2,1)S(1)}, u32[]{:S(2)}, u32[]{:S(2)}) collective-permute-start(bf16[1,4,3712]{2,1,0:T(4,128)(2,1)S(1)} %get-tuple-element.24.refs_0_), channel_id=1, source_target_pairs={{0,12},{1,13},{2,14},{3,15},{4,8},{5,9},{6,10},{7,11},{8,4},{9,5},... | collective-permute-start | bytes 89096 | tf_op jit(solution)/shard_map/ppermute | solution.py:550
  44.2 5.1 %collective-permute-start.5 = (bf16[1,4,3712]{2,1,0:T(4,128)(2,1)S(1)}, bf16[1,4,3712]{2,1,0:T(4,128)(2,1)S(1)}, u32[]{:S(2)}, u32[]{:S(2)}) collective-permute-start(bf16[1,4,3712]{2,1,0:T(4,128)(2,1)S(1)} %get-tuple-element.24.refs_0_), channel_id=1, source_target_pairs={{0,8},{1,9},{2,10},{3,11},{4,12},{5,13},{6,14},{7,15},{8,0},{9,1},... | collective-permute-start | bytes 89096 | tf_op jit(solution)/shard_map/ppermute | solution.py:550
  45.1 4.8 %collective-permute-start.4 = (bf16[1,4,3712]{2,1,0:T(4,128)(2,1)S(1)}, bf16[1,4,3712]{2,1,0:T(4,128)(2,1)S(1)}, u32[]{:S(2)}, u32[]{:S(2)}) collective-permute-start(bf16[1,4,3712]{2,1,0:T(4,128)(2,1)S(1)} %get-tuple-element.24.refs_0_), channel_id=1, source_target_pairs={{0,4},{1,5},{2,6},{3,7},{4,0},{5,1},{6,2},{7,3},{8,12},{9,13},{10,... | collective-permute-start | bytes 89096 | tf_op jit(solution)/shard_map/ppermute | solution.py:550
  49.9 5.2 %collective-permute-start.7 = (bf16[4,4,3712]{2,1,0:T(4,128)(2,1)S(1)}, bf16[4,4,3712]{2,1,0:T(4,128)(2,1)S(1)}, u32[]{:S(2)}, u32[]{:S(2)}) collective-permute-start(bf16[4,4,3712]{2,1,0:T(4,128)(2,1)S(1)} %shard_map.199.refs_0_), channel_id=1, source_target_pairs={{0,16},{1,3},{2,18},{3,1},{4,20},{5,7},{6,22},{7,5},{8,24},{9,11},... | collective-permute-start | bytes 356360 | tf_op jit(solution)/shard_map/ppermute | solution.py:550
  51.5 10.4 %collective-permute-start.8 = (bf16[4,4,3712]{2,1,0:T(4,128)(2,1)S(1)}, bf16[4,4,3712]{2,1,0:T(4,128)(2,1)S(1)}, u32[]{:S(2)}, u32[]{:S(2)}) collective-permute-start(bf16[4,4,3712]{2,1,0:T(4,128)(2,1)S(1)} %shard_map.199.refs_0_), channel_id=1, source_target_pairs={{0,2},{1,17},{2,0},{3,19},{4,6},{5,21},{6,4},{7,23},{8,10},{9,25},... | collective-permute-start | bytes 356360 | tf_op jit(solution)/shard_map/ppermute | solution.py:550
  55.1 6.9 %collective-permute-start.9 = (bf16[4,4,3712]{2,1,0:T(4,128)(2,1)S(1)}, bf16[4,4,3712]{2,1,0:T(4,128)(2,1)S(1)}, u32[]{:S(2)}, u32[]{:S(2)}) collective-permute-start(bf16[4,4,3712]{2,1,0:T(4,128)(2,1)S(1)} %collective-permute-done.7.passed), channel_id=1, source_target_pairs={{0,2},{1,17},{2,0},{3,19},{4,6},{5,21},{6,4},{7,23},{8,10},{9,25},... | collective-permute-start | bytes 356360 | tf_op jit(solution)/shard_map/ppermute | solution.py:550
  56.0 6.4 %collective-permute-start.10 = (bf16[4,4,3712]{2,1,0:T(4,128)(2,1)S(1)}, bf16[4,4,3712]{2,1,0:T(4,128)(2,1)S(1)}, u32[]{:S(2)}, u32[]{:S(2)}) collective-permute-start(bf16[4,4,3712]{2,1,0:T(4,128)(2,1)S(1)} %shard_map.199.refs_0_), channel_id=1, source_target_pairs={{0,1},{1,0},{2,3},{3,2},{4,5},{5,4},{6,7},{7,6},{8,9},{9,8},{10,11... | collective-permute-start | bytes 356360 | tf_op jit(solution)/shard_map/ppermute | solution.py:550
  61.3 1.9 %collective-permute-start.11 = (bf16[4,4,3712]{2,1,0:T(4,128)(2,1)S(1)}, bf16[4,4,3712]{2,1,0:T(4,128)(2,1)S(1)}, u32[]{:S(2)}, u32[]{:S(2)}) collective-permute-start(bf16[4,4,3712]{2,1,0:T(4,128)(2,1)S(1)} %get-tuple-element.25.refs_1_), channel_id=1, source_target_pairs={{0,1},{1,0},{2,3},{3,2},{4,5},{5,4},{6,7},{7,6},{8,9},{9,8},{10,11... | collective-permute-start | bytes 356360 | tf_op jit(solution)/shard_map/ppermute | solution.py:550
  61.9 1.3 %collective-permute-start.12 = (bf16[4,4,3712]{2,1,0:T(4,128)(2,1)S(1)}, bf16[4,4,3712]{2,1,0:T(4,128)(2,1)S(1)}, u32[]{:S(2)}, u32[]{:S(2)}) collective-permute-start(bf16[4,4,3712]{2,1,0:T(4,128)(2,1)S(1)} %collective-permute-done.8.refs_2_), channel_id=1, source_target_pairs={{0,1},{1,0},{2,3},{3,2},{4,5},{5,4},{6,7},{7,6},{8,9},{9,8},{10,11... | collective-permute-start | bytes 356360 | tf_op jit(solution)/shard_map/ppermute | solution.py:550
  62.0 1.4 %collective-permute-start.13 = (bf16[4,4,3712]{2,1,0:T(4,128)(2,1)S(1)}, bf16[4,4,3712]{2,1,0:T(4,128)(2,1)S(1)}, u32[]{:S(2)}, u32[]{:S(2)}) collective-permute-start(bf16[4,4,3712]{2,1,0:T(4,128)(2,1)S(1)} %collective-permute-done.9.refs_3_), channel_id=1, source_target_pairs={{0,1},{1,0},{2,3},{3,2},{4,5},{5,4},{6,7},{7,6},{8,9},{9,8},{10,11... | collective-permute-start | bytes 356360 | tf_op jit(solution)/shard_map/ppermute | solution.py:550
  70.6 1.9 %collective-permute-start.14 = (bf16[64,3584]{1,0:T(8,128)(2,1)S(1)}, bf16[64,3584]{1,0:T(8,128)(2,1)S(1)}, u32[]{:S(2)}, u32[]{:S(2)}) collective-permute-start(bf16[64,3584]{1,0:T(8,128)(2,1)S(1)} %get-tuple-element.29), channel_id=1, source_target_pairs={{0,1},{1,0},{2,3},{3,2},{4,5},{5,4},{6,7},{7,6},{8,9},{9,8},{10,11... | collective-permute-start | bytes 1376264 | tf_op jit(solution)/shard_map/ppermute | solution.py:550
  72.6 6.1 %collective-permute-start.15 = (bf16[32,3584]{1,0:T(8,128)(2,1)S(1)}, bf16[32,3584]{1,0:T(8,128)(2,1)S(1)}, u32[]{:S(2)}, u32[]{:S(2)}) collective-permute-start(bf16[32,3584]{1,0:T(8,128)(2,1)S(1)} %get-tuple-element.31), channel_id=1, source_target_pairs={{0,2},{1,17},{2,0},{3,19},{4,6},{5,21},{6,4},{7,23},{8,10},{9,25},... | collective-permute-start | bytes 688136 | tf_op jit(solution)/shard_map/ppermute | solution.py:550
  78.7 4.9 %collective-permute-start.16 = (bf16[16,3584]{1,0:T(8,128)(2,1)S(1)}, bf16[16,3584]{1,0:T(8,128)(2,1)S(1)}, u32[]{:S(2)}, u32[]{:S(2)}) collective-permute-start(bf16[16,3584]{1,0:T(8,128)(2,1)S(1)} %get-tuple-element.33), channel_id=1, source_target_pairs={{0,16},{1,3},{2,18},{3,1},{4,20},{5,7},{6,22},{7,5},{8,24},{9,11},... | collective-permute-start | bytes 344072 | tf_op jit(solution)/shard_map/ppermute | solution.py:550
  83.6 4.5 %collective-permute-start.17 = (bf16[4,3584]{1,0:T(4,128)(2,1)S(1)}, bf16[4,3584]{1,0:T(4,128)(2,1)S(1)}, u32[]{:S(2)}, u32[]{:S(2)}) collective-permute-start(bf16[4,3584]{1,0:T(4,128)(2,1)S(1)} %get-tuple-element.35), channel_id=1, source_target_pairs={{0,4},{1,5},{2,6},{3,7},{4,0},{5,1},{6,2},{7,3},{8,12},{9,13},{10,... | collective-permute-start | bytes 86024 | tf_op jit(solution)/shard_map/ppermute | solution.py:550
  85.4 4.8 %collective-permute-start.18 = (bf16[4,3584]{1,0:T(4,128)(2,1)S(1)}, bf16[4,3584]{1,0:T(4,128)(2,1)S(1)}, u32[]{:S(2)}, u32[]{:S(2)}) collective-permute-start(bf16[4,3584]{1,0:T(4,128)(2,1)S(1)} %get-tuple-element.36), channel_id=1, source_target_pairs={{0,8},{1,9},{2,10},{3,11},{4,12},{5,13},{6,14},{7,15},{8,0},{9,1},... | collective-permute-start | bytes 86024 | tf_op jit(solution)/shard_map/ppermute | solution.py:550
  86.3 5.7 %collective-permute-start.19 = (bf16[4,3584]{1,0:T(4,128)(2,1)S(1)}, bf16[4,3584]{1,0:T(4,128)(2,1)S(1)}, u32[]{:S(2)}, u32[]{:S(2)}) collective-permute-start(bf16[4,3584]{1,0:T(4,128)(2,1)S(1)} %get-tuple-element.37), channel_id=1, source_target_pairs={{0,12},{1,13},{2,14},{3,15},{4,8},{5,9},{6,10},{7,11},{8,4},{9,5},... | collective-permute-start | bytes 86024 | tf_op jit(solution)/shard_map/ppermute | solution.py:550
  (4 other events, 73.1 us)

commit v4 on v3

--- a/solution.py
+++ b/solution.py
@@ -453,7 +453,7 @@
 def expert_kernel(top, count, *refs):
     pieces = refs[:count]
     w_router, w_gate, w_up, down_hbm = refs[count : count + 4]
-    kept, away, rows_ref, hidden_ref, acc, w_down, sems = refs[count + 4 :]
+    kept, away, rows_ref, hidden_ref, w_down, sems = refs[count + 4 :]
     expert = lax.axis_index(EXPERT)
     width, units = w_gate.shape
     in_step = 256 if units % 256 == 0 else units
@@ -488,21 +488,13 @@
         up = dot_nn(rows, w_up[:, at : at + in_step])
         hidden_ref[:, at : at + in_step] = (gate / (1.0 + jnp.exp(-gate)) * up).astype(BF16)
     half = rows_ref.shape[0] // 2
-    steps = units // in_step
-    for i, down_copy in enumerate(down_copies):
-        down_copy.wait()
-        span = slice(i * in_step, (i + 1) * in_step)
-        hidden = hidden_ref[:, span]
-        for at in range(0, width, out_step):
-            part = dot_nn(hidden, w_down[span, at : at + out_step])
-            if i:
-                part = part + acc[:, at : at + out_step]
-            if i < steps - 1:
-                acc[:, at : at + out_step] = part
-            else:
-                part = part * gates
-                kept[:, at : at + out_step] = part[:half]
-                away[:, at : at + out_step] = part[half:].astype(BF16)
+    for copy in down_copies:
+        copy.wait()
+    hidden = hidden_ref[...]
+    for at in range(0, width, out_step):
+        part = dot_nn(hidden, w_down[:, at : at + out_step]) * gates
+        kept[:, at : at + out_step] = part[:half]
+        away[:, at : at + out_step] = part[half:].astype(BF16)
 
 
 def halve_kernel(kept, got, keep, away):
@@ -563,8 +555,6 @@
     rows = tokens * heads
     sizes = (heads, per_device, rollouts, following, view)
     chips = expert_count // 2
-    other_uv, other_out = swap(w_uv, 1), swap(w_out, 1)
-
     picked = call(
         functools.partial(pick_kernel, partners, moves),
         [shape((moves, page_len, latent), BF16)] * partners
@@ -581,7 +571,7 @@
             pltpu.SemaphoreType.DMA((partners, moves)),
             pltpu.SemaphoreType.DMA((4,)),
         ],
-        vmem=57,
+        vmem=60,
     )
     got_lat = [swap(picked[k], (k + 1) * expert_count) for k in range(partners)]
     got_rope = [swap(picked[partners + k], (k + 1) * expert_count) for k in range(partners)]
@@ -623,7 +613,7 @@
             pltpu.SemaphoreType.DMA((9,)),
             pltpu.SemaphoreType.DMA((slots // GROUP,)),
         ],
-        vmem=57,
+        vmem=60,
         cost=(2 * slots * page_len * rows * (2 * latent + 2 * rope_dim), 4 * MIB),
     )
     blocks = call(
@@ -634,6 +624,8 @@
         cost=(2 * moves * page_len * rows * 2 * latent, MIB),
     )[0]
 
+    away_uv, away_out, blocks = lax.optimization_barrier((w_uv, w_out, blocks))
+    other_uv, other_out = swap(away_uv, 1), swap(away_out, 1)
     blocks = deal(blocks, CHIP)
 
     parts = call(
@@ -692,7 +684,6 @@
         scratch=[
             pltpu.VMEM((all_rows, width), BF16),
             pltpu.VMEM((all_rows, hidden_units), BF16),
-            pltpu.VMEM((all_rows, width), F32),
             pltpu.VMEM(w_down.shape[1:], BF16),
             pltpu.SemaphoreType.DMA((16,)),
         ],

time: 93 us -> 92.2 us (level)
  blocking collectives: 10.4 us -> 24 us
  waiting for transfers between devices: 26.5 us -> 20.4 us
  starting transfers between devices: 26.3 us -> 20.4 us
  Pallas kernels: 27.5 us -> 25.3 us
    all_to_all x1 -> x2, blocking collectives: 10.4 us -> 24 us  [deal(): return lax.all_to_all(x, names, split_axis=0, concat_axis=0, tiled=True)]
    all_to_all x1 -> x0, waiting for transfers between devices: 7.34 us -> none  [deal(): return lax.all_to_all(x, names, split_axis=0, concat_axis=0, tiled=True)]
    all_to_all x1 -> x0, starting transfers between devices: 6.08 us -> none  [deal(): return lax.all_to_all(x, names, split_axis=0, concat_axis=0, tiled=True)]
    pallas_call x12, Pallas kernels: 27.5 us -> 25.3 us  [call(): pl.pallas_call(kernel, out_shape=outs, in_specs=in_specs or [VMEM] * len(...]
    ppermute x20, waiting for transfers between devices: 19.1 us -> 20.4 us  [swap(): return lax.ppermute(x, ROWS, pairs)]
  transfers between devices with their start and end apart: 21 -> 20, of which waited for: 12 -> 12; matrix products, arithmetic and copies ran while one was open for 0% -> 0% of each run, Pallas kernels for 17% -> 13%
where the time goes in v4:
time: 92.2 us; the launch traced here: 91.9 us
  Pallas kernels  25.3 us (27%)
  blocking collectives  24 us (26%)
  starting transfers between devices  20.4 us (22%)
  waiting for transfers between devices  20.4 us (22%)
  local copies, waits for them, and re-layouts  1.12 us (1%)
    pallas_call x12, Pallas kernels, call(): pl.pallas_call(kernel, out_shape=outs, in_specs=in_specs or [VMEM] * len(...  25.3 us
    all_to_all x2, blocking collectives, deal(): return lax.all_to_all(x, names, split_axis=0, concat_axis=0, tiled=True)  24 us
    ppermute x20, starting transfers between devices, swap(): return lax.ppermute(x, ROWS, pairs)  20.4 us
    ppermute x20, waiting for transfers between devices, swap(): return lax.ppermute(x, ROWS, pairs)  20.4 us
  transfers between devices with their start and end apart: 20, of which 12 were waited for; matrix products, arithmetic and copies ran while one was open for 0% of the time, Pallas kernels for 13%

profile of v4, /device:TPU:0, one launch (start us, length us, event | category | flops | bytes accessed | tf_op | source)
XLA Modules:
  0.0 91.9 jit_solution(1474431484534199795)
XLA Ops:
  0.7 2.6 %shard_map.194 = (bf16[4,64,512]{2,1,0:T(8,128)(2,1)}, bf16[8,2176]{1,0:T(8,128)(2,1)}, f32[48]{0:T(128)}) custom-call(s32[1,2,4]{2,1,0:T(2,128)} %move_hbm.3, bf16[48]{0:T(256)(128)(2,1)} %scale_hbm.1, bf16[48,64,512]{2,1,0:T(8,128)(2,1)} %lat_hbm.1, bf16[48,4096]{1,0:T(8,128)(2,1)} %rope_hbm.3), custom_call_target="tpu_custom_call" | custom-call | tf_op jit(solution)/shard_map/pallas_call | solution.py:45
  3.3 3.0 %collective-permute-start = (bf16[4,64,512]{2,1,0:T(8,128)(2,1)}, bf16[4,64,512]{2,1,0:T(8,128)(2,1)S(1)}, u32[]{:S(2)}, u32[]{:S(2)}) collective-permute-start(bf16[4,64,512]{2,1,0:T(8,128)(2,1)} %get-tuple-element.23), channel_id=1, source_target_pairs={{0,16},{1,17},{2,18},{3,19},{4,20},{5,21},{6,22},{7,23},{8,24},{9,... | collective-permute-start | bytes 786440 | tf_op jit(solution)/shard_map/ppermute | solution.py:542
  6.4 7.1 %shard_map.195.refs_2_ = f32[264,640]{1,0:T(8,128)} custom-call(f32[48]{0:T(128)} %get-tuple-element.25.scale_hbm, s32[2,32]{1,0:T(2,128)} %table_hbm.1, s32[2]{0:T(128)} %lengths_hbm.1, s32[1,2,4]{2,1,0:T(2,128)} %move_hbm.3, bf16[48,64,512]{2,1,0:T(8,128)(2,1)} %lat_hbm.1, bf16[48,4096]{1,0:T(8,128)(2,1)} %rope_hbm.3, bf16[2,2,32,512]{3,2,1,0:T(8,128)(2,1)} %q_hbm.1, ...), custom_call_target="tpu_custom_call" | custom-call | flops 905969664 | bytes 4194304 | tf_op jit(solution)/shard_map/pallas_call | solution.py:45
  13.5 1.1 %copy-done = f32[264,640]{1,0:T(8,128)S(1)} copy-done((f32[264,640]{1,0:T(8,128)S(1)}, f32[264,640]{1,0:T(8,128)}, u32[]{:S(2)}) %copy-start) | copy-done | bytes 675864
  15.8 13.3 %all_to_all.10.blocks = bf16[8,16,512]{2,1,0:T(8,128)(2,1)S(1)} all-to-all(bf16[8,16,512]{2,1,0:T(8,128)(2,1)S(1)} %shard_map.196), channel_id=1, replica_groups=mesh['top'=2,'low'=1,'far'=4,'side'=2,'core'=2] {'far','side'}, dimensions={0} | all-to-all | bytes 262144 | tf_op jit(solution)/shard_map/all_to_all | solution.py:545
  29.1 1.1 %shard_map.197 = bf16[8,4,3584]{2,1,0:T(4,128)(2,1)S(1)} custom-call(bf16[8,16,512]{2,1,0:T(8,128)(2,1)S(1)} %all_to_all.10.blocks, bf16[2,512,128]{2,1,0:T(8,128)(2,1)S(1)} %copy-done.2, bf16[2,512,128]{2,1,0:T(8,128)(2,1)S(1)} %collective-permute-done.2.other_uv, bf16[256,3584]{1,0:T(8,128)(2,1)S(1)} %copy-done.1, ...), custom_call_target="tpu_custom_call" | custom-call | flops 117440512 | bytes 8388608 | tf_op jit(solution)/shard_map/pallas_call | solution.py:45
  30.2 10.6 %all_to_all.11.got = bf16[8,4,3584]{2,1,0:T(4,128)(2,1)S(1)} all-to-all(bf16[8,4,3584]{2,1,0:T(4,128)(2,1)S(1)} %shard_map.197), channel_id=1, replica_groups=mesh['top'=2,'low'=1,'far'=4,'side'=2,'core'=2] {'far','side'}, dimensions={0} | all-to-all | bytes 458752 | tf_op jit(solution)/shard_map/all_to_all | solution.py:545
  42.5 1.4 %collective-permute-start.5 = (bf16[1,4,3712]{2,1,0:T(4,128)(2,1)S(1)}, bf16[1,4,3712]{2,1,0:T(4,128)(2,1)S(1)}, u32[]{:S(2)}, u32[]{:S(2)}) collective-permute-start(bf16[1,4,3712]{2,1,0:T(4,128)(2,1)S(1)} %get-tuple-element.30.refs_0_), channel_id=1, source_target_pairs={{0,8},{1,9},{2,10},{3,11},{4,12},{5,13},{6,14},{7,15},{8,0},{9,1},... | collective-permute-start | bytes 89096 | tf_op jit(solution)/shard_map/ppermute | solution.py:542
  43.9 2.0 %collective-permute-start.4 = (bf16[1,4,3712]{2,1,0:T(4,128)(2,1)S(1)}, bf16[1,4,3712]{2,1,0:T(4,128)(2,1)S(1)}, u32[]{:S(2)}, u32[]{:S(2)}) collective-permute-start(bf16[1,4,3712]{2,1,0:T(4,128)(2,1)S(1)} %get-tuple-element.30.refs_0_), channel_id=1, source_target_pairs={{0,4},{1,5},{2,6},{3,7},{4,0},{5,1},{6,2},{7,3},{8,12},{9,13},{10,... | collective-permute-start | bytes 89096 | tf_op jit(solution)/shard_map/ppermute | solution.py:542
  46.0 1.3 %collective-permute-done.6.refs_3_ = bf16[1,4,3712]{2,1,0:T(4,128)(2,1)S(1)} collective-permute-done((bf16[1,4,3712]{2,1,0:T(4,128)(2,1)S(1)}, bf16[1,4,3712]{2,1,0:T(4,128)(2,1)S(1)}, u32[]{:S(2)}, u32[]{:S(2)}) %collective-permute-start.6) | collective-permute-done | bytes 29728 | tf_op jit(solution)/shard_map/ppermute | solution.py:542
  48.1 1.6 %collective-permute-start.7 = (bf16[4,4,3712]{2,1,0:T(4,128)(2,1)S(1)}, bf16[4,4,3712]{2,1,0:T(4,128)(2,1)S(1)}, u32[]{:S(2)}, u32[]{:S(2)}) collective-permute-start(bf16[4,4,3712]{2,1,0:T(4,128)(2,1)S(1)} %shard_map.199.refs_0_), channel_id=1, source_target_pairs={{0,16},{1,3},{2,18},{3,1},{4,20},{5,7},{6,22},{7,5},{8,24},{9,11},... | collective-permute-start | bytes 356360 | tf_op jit(solution)/shard_map/ppermute | solution.py:542
  49.7 1.2 %collective-permute-start.8 = (bf16[4,4,3712]{2,1,0:T(4,128)(2,1)S(1)}, bf16[4,4,3712]{2,1,0:T(4,128)(2,1)S(1)}, u32[]{:S(2)}, u32[]{:S(2)}) collective-permute-start(bf16[4,4,3712]{2,1,0:T(4,128)(2,1)S(1)} %shard_map.199.refs_0_), channel_id=1, source_target_pairs={{0,2},{1,17},{2,0},{3,19},{4,6},{5,21},{6,4},{7,23},{8,10},{9,25},... | collective-permute-start | bytes 356360 | tf_op jit(solution)/shard_map/ppermute | solution.py:542
  50.9 3.3 %collective-permute-done.7.passed = bf16[4,4,3712]{2,1,0:T(4,128)(2,1)S(1)} collective-permute-done((bf16[4,4,3712]{2,1,0:T(4,128)(2,1)S(1)}, bf16[4,4,3712]{2,1,0:T(4,128)(2,1)S(1)}, u32[]{:S(2)}, u32[]{:S(2)}) %collective-permute-start.7) | collective-permute-done | bytes 118816 | tf_op jit(solution)/shard_map/ppermute | solution.py:542
  55.2 5.3 %shard_map.200 = (bf16[4,4,3712]{2,1,0:T(4,128)(2,1)S(1)}, bf16[3584,1024]{1,0:T(8,128)(2,1)S(1)}, bf16[3584,1024]{1,0:T(8,128)(2,1)S(1)}) custom-call(bf16[4,4,3712]{2,1,0:T(4,128)(2,1)S(1)} %collective-permute-done.7.passed, bf16[1,3584,1024]{2,1,0:T(8,128)(2,1)} %refs_0_.1, bf16[1,3584,1024]{2,1,0:T(8,128)(2,1)} %refs_1_.1), custom_call_target="tpu_custom_call" | custom-call | bytes 14680064 | tf_op jit(solution)/shard_map/pallas_call | solution.py:45
  62.7 7.1 %shard_map.201 = (f32[64,3584]{1,0:T(8,128)S(1)}, bf16[64,3584]{1,0:T(8,128)(2,1)S(1)}) custom-call(bf16[4,4,3712]{2,1,0:T(4,128)(2,1)S(1)} %shard_map.199.refs_0_, bf16[4,4,3712]{2,1,0:T(4,128)(2,1)S(1)} %get-tuple-element.31.refs_1_, bf16[4,4,3712]{2,1,0:T(4,128)(2,1)S(1)} %collective-permute-done.8.refs_2_, ...), custom_call_target="tpu_custom_call" | custom-call | flops 2818572288 | bytes 22020096 | tf_op jit(solution)/shard_map/pallas_call | solution.py:45
  70.2 1.5 %collective-permute-done.14.got = bf16[64,3584]{1,0:T(8,128)(2,1)S(1)} collective-permute-done((bf16[64,3584]{1,0:T(8,128)(2,1)S(1)}, bf16[64,3584]{1,0:T(8,128)(2,1)S(1)}, u32[]{:S(2)}, u32[]{:S(2)}) %collective-permute-start.14) | collective-permute-done | bytes 458784 | tf_op jit(solution)/shard_map/ppermute | solution.py:542
  72.8 5.0 %collective-permute-done.15.got = bf16[32,3584]{1,0:T(8,128)(2,1)S(1)} collective-permute-done((bf16[32,3584]{1,0:T(8,128)(2,1)S(1)}, bf16[32,3584]{1,0:T(8,128)(2,1)S(1)}, u32[]{:S(2)}, u32[]{:S(2)}) %collective-permute-start.15) | collective-permute-done | bytes 229408 | tf_op jit(solution)/shard_map/ppermute | solution.py:542
  77.9 1.6 %collective-permute-start.16 = (bf16[16,3584]{1,0:T(8,128)(2,1)S(1)}, bf16[16,3584]{1,0:T(8,128)(2,1)S(1)}, u32[]{:S(2)}, u32[]{:S(2)}) collective-permute-start(bf16[16,3584]{1,0:T(8,128)(2,1)S(1)} %get-tuple-element.39), channel_id=1, source_target_pairs={{0,16},{1,3},{2,18},{3,1},{4,20},{5,7},{6,22},{7,5},{8,24},{9,11},... | collective-permute-start | bytes 344072 | tf_op jit(solution)/shard_map/ppermute | solution.py:542
  79.4 3.3 %collective-permute-done.16.got = bf16[16,3584]{1,0:T(8,128)(2,1)S(1)} collective-permute-done((bf16[16,3584]{1,0:T(8,128)(2,1)S(1)}, bf16[16,3584]{1,0:T(8,128)(2,1)S(1)}, u32[]{:S(2)}, u32[]{:S(2)}) %collective-permute-start.16) | collective-permute-done | bytes 114720 | tf_op jit(solution)/shard_map/ppermute | solution.py:542
  82.8 1.1 %collective-permute-start.17 = (bf16[4,3584]{1,0:T(4,128)(2,1)S(1)}, bf16[4,3584]{1,0:T(4,128)(2,1)S(1)}, u32[]{:S(2)}, u32[]{:S(2)}) collective-permute-start(bf16[4,3584]{1,0:T(4,128)(2,1)S(1)} %get-tuple-element.41), channel_id=1, source_target_pairs={{0,4},{1,5},{2,6},{3,7},{4,0},{5,1},{6,2},{7,3},{8,12},{9,13},{10,... | collective-permute-start | bytes 86024 | tf_op jit(solution)/shard_map/ppermute | solution.py:542
  83.8 1.7 %collective-permute-start.18 = (bf16[4,3584]{1,0:T(4,128)(2,1)S(1)}, bf16[4,3584]{1,0:T(4,128)(2,1)S(1)}, u32[]{:S(2)}, u32[]{:S(2)}) collective-permute-start(bf16[4,3584]{1,0:T(4,128)(2,1)S(1)} %get-tuple-element.42), channel_id=1, source_target_pairs={{0,8},{1,9},{2,10},{3,11},{4,12},{5,13},{6,14},{7,15},{8,0},{9,1},... | collective-permute-start | bytes 86024 | tf_op jit(solution)/shard_map/ppermute | solution.py:542
  85.6 1.6 %collective-permute-start.19 = (bf16[4,3584]{1,0:T(4,128)(2,1)S(1)}, bf16[4,3584]{1,0:T(4,128)(2,1)S(1)}, u32[]{:S(2)}, u32[]{:S(2)}) collective-permute-start(bf16[4,3584]{1,0:T(4,128)(2,1)S(1)} %get-tuple-element.43), channel_id=1, source_target_pairs={{0,12},{1,13},{2,14},{3,15},{4,8},{5,9},{6,10},{7,11},{8,4},{9,5},... | collective-permute-start | bytes 86024 | tf_op jit(solution)/shard_map/ppermute | solution.py:542
  87.2 1.4 %collective-permute-done.18.refs_2_ = bf16[4,3584]{1,0:T(4,128)(2,1)S(1)} collective-permute-done((bf16[4,3584]{1,0:T(4,128)(2,1)S(1)}, bf16[4,3584]{1,0:T(4,128)(2,1)S(1)}, u32[]{:S(2)}, u32[]{:S(2)}) %collective-permute-start.18) | collective-permute-done | bytes 28704 | tf_op jit(solution)/shard_map/ppermute | solution.py:542
  88.6 2.6 %collective-permute-done.19.refs_3_ = bf16[4,3584]{1,0:T(4,128)(2,1)S(1)} collective-permute-done((bf16[4,3584]{1,0:T(4,128)(2,1)S(1)}, bf16[4,3584]{1,0:T(4,128)(2,1)S(1)}, u32[]{:S(2)}, u32[]{:S(2)}) %collective-permute-start.19) | collective-permute-done | bytes 28704 | tf_op jit(solution)/shard_map/ppermute | solution.py:542
  (44 shorter events, 9.1 us)
Async XLA Ops:
  0.6 14.6 %copy-start.2 = (bf16[2,512,128]{2,1,0:T(8,128)(2,1)S(1)}, bf16[2,512,128]{2,1,0:T(8,128)(2,1)}, u32[]{:S(2)}) copy-start(bf16[2,512,128]{2,1,0:T(8,128)(2,1)} %w_uv.1) | copy-start | bytes 786436
  0.7 40.2 %copy-start.6 = (s32[4,8]{1,0:T(4,128)S(1)}, s32[4,8]{1,0:T(4,128)}, u32[]{:S(2)}) copy-start(s32[4,8]{1,0:T(4,128)} %routes.1) | copy-start | bytes 388
  0.7 40.2 %copy-start.5 = (f32[3584]{0:T(1024)S(1)}, f32[3584]{0:T(1024)}, u32[]{:S(2)}) copy-start(f32[3584]{0:T(1024)} %gain.1) | copy-start | bytes 43012
  0.7 40.2 %copy-start.4 = (bf16[4,3584]{1,0:T(4,128)(2,1)S(1)}, bf16[4,3584]{1,0:T(4,128)(2,1)}, u32[]{:S(2)}) copy-start(bf16[4,3584]{1,0:T(4,128)(2,1)} %residual.1) | copy-start | bytes 86020
  3.3 10.3 %collective-permute-start = (bf16[4,64,512]{2,1,0:T(8,128)(2,1)}, bf16[4,64,512]{2,1,0:T(8,128)(2,1)S(1)}, u32[]{:S(2)}, u32[]{:S(2)}) collective-permute-start(bf16[4,64,512]{2,1,0:T(8,128)(2,1)} %get-tuple-element.23), channel_id=1, source_target_pairs={{0,16},{1,17},{2,18},{3,19},{4,20},{5,21},{6,22},{7,23},{8,24},{9,... | collective-permute-start | bytes 786440 | tf_op jit(solution)/shard_map/ppermute | solution.py:542
  6.3 7.3 %collective-permute-start.1 = (bf16[8,2176]{1,0:T(8,128)(2,1)}, bf16[8,2176]{1,0:T(8,128)(2,1)S(1)}, u32[]{:S(2)}, u32[]{:S(2)}) collective-permute-start(bf16[8,2176]{1,0:T(8,128)(2,1)} %get-tuple-element.24), channel_id=1, source_target_pairs={{0,16},{1,17},{2,18},{3,19},{4,20},{5,21},{6,22},{7,23},{8,24},{9,... | collective-permute-start | bytes 104456 | tf_op jit(solution)/shard_map/ppermute | solution.py:542
  15.2 13.9 %collective-permute-start.3 = (bf16[256,3584]{1,0:T(8,128)(2,1)S(1)}, bf16[256,3584]{1,0:T(8,128)(2,1)S(1)}, u32[]{:S(2)}, u32[]{:S(2)}) collective-permute-start(bf16[256,3584]{1,0:T(8,128)(2,1)S(1)} %copy-done.1), channel_id=1, source_target_pairs={{0,1},{1,0},{2,3},{3,2},{4,5},{5,4},{6,7},{7,6},{8,9},{9,8},{10,11... | collective-permute-start | bytes 5505032 | tf_op jit(solution)/shard_map/ppermute | solution.py:542
  15.3 13.8 %collective-permute-start.2 = (bf16[2,512,128]{2,1,0:T(8,128)(2,1)S(1)}, bf16[2,512,128]{2,1,0:T(8,128)(2,1)S(1)}, u32[]{:S(2)}, u32[]{:S(2)}) collective-permute-start(bf16[2,512,128]{2,1,0:T(8,128)(2,1)S(1)} %copy-done.2), channel_id=1, source_target_pairs={{0,1},{1,0},{2,3},{3,2},{4,5},{5,4},{6,7},{7,6},{8,9},{9,8},{10,11... | collective-permute-start | bytes 786440 | tf_op jit(solution)/shard_map/ppermute | solution.py:542
  41.6 5.7 %collective-permute-start.6 = (bf16[1,4,3712]{2,1,0:T(4,128)(2,1)S(1)}, bf16[1,4,3712]{2,1,0:T(4,128)(2,1)S(1)}, u32[]{:S(2)}, u32[]{:S(2)}) collective-permute-start(bf16[1,4,3712]{2,1,0:T(4,128)(2,1)S(1)} %get-tuple-element.30.refs_0_), channel_id=1, source_target_pairs={{0,12},{1,13},{2,14},{3,15},{4,8},{5,9},{6,10},{7,11},{8,4},{9,5},... | collective-permute-start | bytes 89096 | tf_op jit(solution)/shard_map/ppermute | solution.py:542
  42.5 5.5 %collective-permute-start.5 = (bf16[1,4,3712]{2,1,0:T(4,128)(2,1)S(1)}, bf16[1,4,3712]{2,1,0:T(4,128)(2,1)S(1)}, u32[]{:S(2)}, u32[]{:S(2)}) collective-permute-start(bf16[1,4,3712]{2,1,0:T(4,128)(2,1)S(1)} %get-tuple-element.30.refs_0_), channel_id=1, source_target_pairs={{0,8},{1,9},{2,10},{3,11},{4,12},{5,13},{6,14},{7,15},{8,0},{9,1},... | collective-permute-start | bytes 89096 | tf_op jit(solution)/shard_map/ppermute | solution.py:542
  43.9 4.2 %collective-permute-start.4 = (bf16[1,4,3712]{2,1,0:T(4,128)(2,1)S(1)}, bf16[1,4,3712]{2,1,0:T(4,128)(2,1)S(1)}, u32[]{:S(2)}, u32[]{:S(2)}) collective-permute-start(bf16[1,4,3712]{2,1,0:T(4,128)(2,1)S(1)} %get-tuple-element.30.refs_0_), channel_id=1, source_target_pairs={{0,4},{1,5},{2,6},{3,7},{4,0},{5,1},{6,2},{7,3},{8,12},{9,13},{10,... | collective-permute-start | bytes 89096 | tf_op jit(solution)/shard_map/ppermute | solution.py:542
  48.1 6.1 %collective-permute-start.7 = (bf16[4,4,3712]{2,1,0:T(4,128)(2,1)S(1)}, bf16[4,4,3712]{2,1,0:T(4,128)(2,1)S(1)}, u32[]{:S(2)}, u32[]{:S(2)}) collective-permute-start(bf16[4,4,3712]{2,1,0:T(4,128)(2,1)S(1)} %shard_map.199.refs_0_), channel_id=1, source_target_pairs={{0,16},{1,3},{2,18},{3,1},{4,20},{5,7},{6,22},{7,5},{8,24},{9,11},... | collective-permute-start | bytes 356360 | tf_op jit(solution)/shard_map/ppermute | solution.py:542
  49.7 11.5 %collective-permute-start.8 = (bf16[4,4,3712]{2,1,0:T(4,128)(2,1)S(1)}, bf16[4,4,3712]{2,1,0:T(4,128)(2,1)S(1)}, u32[]{:S(2)}, u32[]{:S(2)}) collective-permute-start(bf16[4,4,3712]{2,1,0:T(4,128)(2,1)S(1)} %shard_map.199.refs_0_), channel_id=1, source_target_pairs={{0,2},{1,17},{2,0},{3,19},{4,6},{5,21},{6,4},{7,23},{8,10},{9,25},... | collective-permute-start | bytes 356360 | tf_op jit(solution)/shard_map/ppermute | solution.py:542
  54.2 7.0 %collective-permute-start.9 = (bf16[4,4,3712]{2,1,0:T(4,128)(2,1)S(1)}, bf16[4,4,3712]{2,1,0:T(4,128)(2,1)S(1)}, u32[]{:S(2)}, u32[]{:S(2)}) collective-permute-start(bf16[4,4,3712]{2,1,0:T(4,128)(2,1)S(1)} %collective-permute-done.7.passed), channel_id=1, source_target_pairs={{0,2},{1,17},{2,0},{3,19},{4,6},{5,21},{6,4},{7,23},{8,10},{9,25},... | collective-permute-start | bytes 356360 | tf_op jit(solution)/shard_map/ppermute | solution.py:542
  55.2 6.4 %collective-permute-start.10 = (bf16[4,4,3712]{2,1,0:T(4,128)(2,1)S(1)}, bf16[4,4,3712]{2,1,0:T(4,128)(2,1)S(1)}, u32[]{:S(2)}, u32[]{:S(2)}) collective-permute-start(bf16[4,4,3712]{2,1,0:T(4,128)(2,1)S(1)} %shard_map.199.refs_0_), channel_id=1, source_target_pairs={{0,1},{1,0},{2,3},{3,2},{4,5},{5,4},{6,7},{7,6},{8,9},{9,8},{10,11... | collective-permute-start | bytes 356360 | tf_op jit(solution)/shard_map/ppermute | solution.py:542
  60.6 1.9 %collective-permute-start.11 = (bf16[4,4,3712]{2,1,0:T(4,128)(2,1)S(1)}, bf16[4,4,3712]{2,1,0:T(4,128)(2,1)S(1)}, u32[]{:S(2)}, u32[]{:S(2)}) collective-permute-start(bf16[4,4,3712]{2,1,0:T(4,128)(2,1)S(1)} %get-tuple-element.31.refs_1_), channel_id=1, source_target_pairs={{0,1},{1,0},{2,3},{3,2},{4,5},{5,4},{6,7},{7,6},{8,9},{9,8},{10,11... | collective-permute-start | bytes 356360 | tf_op jit(solution)/shard_map/ppermute | solution.py:542
  61.1 1.3 %collective-permute-start.12 = (bf16[4,4,3712]{2,1,0:T(4,128)(2,1)S(1)}, bf16[4,4,3712]{2,1,0:T(4,128)(2,1)S(1)}, u32[]{:S(2)}, u32[]{:S(2)}) collective-permute-start(bf16[4,4,3712]{2,1,0:T(4,128)(2,1)S(1)} %collective-permute-done.8.refs_2_), channel_id=1, source_target_pairs={{0,1},{1,0},{2,3},{3,2},{4,5},{5,4},{6,7},{7,6},{8,9},{9,8},{10,11... | collective-permute-start | bytes 356360 | tf_op jit(solution)/shard_map/ppermute | solution.py:542
  61.2 1.4 %collective-permute-start.13 = (bf16[4,4,3712]{2,1,0:T(4,128)(2,1)S(1)}, bf16[4,4,3712]{2,1,0:T(4,128)(2,1)S(1)}, u32[]{:S(2)}, u32[]{:S(2)}) collective-permute-start(bf16[4,4,3712]{2,1,0:T(4,128)(2,1)S(1)} %collective-permute-done.9.refs_3_), channel_id=1, source_target_pairs={{0,1},{1,0},{2,3},{3,2},{4,5},{5,4},{6,7},{7,6},{8,9},{9,8},{10,11... | collective-permute-start | bytes 356360 | tf_op jit(solution)/shard_map/ppermute | solution.py:542
  69.8 1.9 %collective-permute-start.14 = (bf16[64,3584]{1,0:T(8,128)(2,1)S(1)}, bf16[64,3584]{1,0:T(8,128)(2,1)S(1)}, u32[]{:S(2)}, u32[]{:S(2)}) collective-permute-start(bf16[64,3584]{1,0:T(8,128)(2,1)S(1)} %get-tuple-element.35), channel_id=1, source_target_pairs={{0,1},{1,0},{2,3},{3,2},{4,5},{5,4},{6,7},{7,6},{8,9},{9,8},{10,11... | collective-permute-start | bytes 1376264 | tf_op jit(solution)/shard_map/ppermute | solution.py:542
  71.7 6.1 %collective-permute-start.15 = (bf16[32,3584]{1,0:T(8,128)(2,1)S(1)}, bf16[32,3584]{1,0:T(8,128)(2,1)S(1)}, u32[]{:S(2)}, u32[]{:S(2)}) collective-permute-start(bf16[32,3584]{1,0:T(8,128)(2,1)S(1)} %get-tuple-element.37), channel_id=1, source_target_pairs={{0,2},{1,17},{2,0},{3,19},{4,6},{5,21},{6,4},{7,23},{8,10},{9,25},... | collective-permute-start | bytes 688136 | tf_op jit(solution)/shard_map/ppermute | solution.py:542
  77.9 4.9 %collective-permute-start.16 = (bf16[16,3584]{1,0:T(8,128)(2,1)S(1)}, bf16[16,3584]{1,0:T(8,128)(2,1)S(1)}, u32[]{:S(2)}, u32[]{:S(2)}) collective-permute-start(bf16[16,3584]{1,0:T(8,128)(2,1)S(1)} %get-tuple-element.39), channel_id=1, source_target_pairs={{0,16},{1,3},{2,18},{3,1},{4,20},{5,7},{6,22},{7,5},{8,24},{9,11},... | collective-permute-start | bytes 344072 | tf_op jit(solution)/shard_map/ppermute | solution.py:542
  82.8 4.5 %collective-permute-start.17 = (bf16[4,3584]{1,0:T(4,128)(2,1)S(1)}, bf16[4,3584]{1,0:T(4,128)(2,1)S(1)}, u32[]{:S(2)}, u32[]{:S(2)}) collective-permute-start(bf16[4,3584]{1,0:T(4,128)(2,1)S(1)} %get-tuple-element.41), channel_id=1, source_target_pairs={{0,4},{1,5},{2,6},{3,7},{4,0},{5,1},{6,2},{7,3},{8,12},{9,13},{10,... | collective-permute-start | bytes 86024 | tf_op jit(solution)/shard_map/ppermute | solution.py:542
  83.8 4.8 %collective-permute-start.18 = (bf16[4,3584]{1,0:T(4,128)(2,1)S(1)}, bf16[4,3584]{1,0:T(4,128)(2,1)S(1)}, u32[]{:S(2)}, u32[]{:S(2)}) collective-permute-start(bf16[4,3584]{1,0:T(4,128)(2,1)S(1)} %get-tuple-element.42), channel_id=1, source_target_pairs={{0,8},{1,9},{2,10},{3,11},{4,12},{5,13},{6,14},{7,15},{8,0},{9,1},... | collective-permute-start | bytes 86024 | tf_op jit(solution)/shard_map/ppermute | solution.py:542
  85.6 5.7 %collective-permute-start.19 = (bf16[4,3584]{1,0:T(4,128)(2,1)S(1)}, bf16[4,3584]{1,0:T(4,128)(2,1)S(1)}, u32[]{:S(2)}, u32[]{:S(2)}) collective-permute-start(bf16[4,3584]{1,0:T(4,128)(2,1)S(1)} %get-tuple-element.43), channel_id=1, source_target_pairs={{0,12},{1,13},{2,14},{3,15},{4,8},{5,9},{6,10},{7,11},{8,4},{9,5},... | collective-permute-start | bytes 86024 | tf_op jit(solution)/shard_map/ppermute | solution.py:542
  (3 other events, 30.2 us)

commit v5 on v4

--- a/solution.py
+++ b/solution.py
@@ -24,8 +24,10 @@
 ROWS = DP + EXPERT
 FAR = ("low", "far")
 CHIP = ("far", "side")
-LOAD_MIB = 36
-EXPERT_MIB = 36
+ROPE_ROWS = 16
+LOAD_MIB = 40
+SIDE_MIB = 28
+EXPERT_MIB = 16
 
 
 def dot_nt(a, b):
@@ -67,18 +69,27 @@
     return copies
 
 
+def row_copies(source, target, sems, first):
+    return [
+        pltpu.make_async_copy(
+            source.at[pl.ds(at, ROPE_ROWS)], target.at[pl.ds(at, ROPE_ROWS)], sems.at[first + i]
+        )
+        for i, at in enumerate(range(0, source.shape[0], ROPE_ROWS))
+    ]
+
+
 def pick_kernel(partners, moves, move_hbm, scale_hbm, lat, rope_hbm, *rest):
     lat_outs, rope_outs = rest[:partners], rest[partners : 2 * partners]
     scale_out, move, rope, scale_ref, wide_scale, lat_sems, sems = rest[2 * partners :]
     slots, width = rope.shape
     half = width // 2
     me = lax.axis_index(DP)
-    get_move, get_scale, get_rope = fetch(
+    get_move, get_scale, *get_rope = fetch(
         [
             pltpu.make_async_copy(move_hbm, move, sems.at[0]),
             pltpu.make_async_copy(scale_hbm, scale_ref, sems.at[1]),
-            pltpu.make_async_copy(rope_hbm, rope, sems.at[2]),
         ]
+        + row_copies(rope_hbm, rope, sems, 3)
     )
     get_move.wait()
     copies = []
@@ -92,9 +103,10 @@
     fetch(copies)
     get_scale.wait()
     wide_scale[...] = scale_ref[...].astype(F32)
-    (put_scale,) = fetch([pltpu.make_async_copy(wide_scale, scale_out, sems.at[3])])
+    (put_scale,) = fetch([pltpu.make_async_copy(wide_scale, scale_out, sems.at[2])])
     put_scale.wait()
-    get_rope.wait()
+    for copy in get_rope:
+        copy.wait()
     row = iota((2 * moves, 1), 0)
     column = iota((2 * moves, slots), 1)
     for k in range(partners):
@@ -131,6 +143,8 @@
 
 
 GROUP = 8
+HALF = 4
+OUT_ROWS = 32
 
 
 def local_kernel(
@@ -146,6 +160,7 @@
     turn_hbm,
     new_lat_hbm,
     new_rope_hbm,
+    out_hbm,
     out,
     scale,
     qrel_out,
@@ -165,6 +180,7 @@
     new_turns,
     sems,
     lat_sems,
+    out_sems,
 ):
     heads, per_device, rollouts, following, view = sizes
     slots, page_len, latent = lat.shape
@@ -177,7 +193,6 @@
         (lengths_hbm, lengths),
         (move_hbm, move),
         (scale_hbm, scale),
-        (rope_hbm, rope),
         (turn_hbm, q_rope),
         (q_hbm, q_lat),
         (new_lat_hbm, new_lat),
@@ -185,13 +200,14 @@
     )
     small = fetch(
         [pltpu.make_async_copy(src, dst, sems.at[i]) for i, (src, dst) in enumerate(pairs)]
+        + row_copies(rope_hbm, rope, sems, len(pairs))
     )
     chunks = fetch(
         [
             pltpu.make_async_copy(
-                lat_hbm.at[pl.ds(at, GROUP)], lat.at[pl.ds(at, GROUP)], lat_sems.at[at // GROUP]
+                lat_hbm.at[pl.ds(at, HALF)], lat.at[pl.ds(at, HALF)], lat_sems.at[at // HALF]
             )
-            for at in range(0, slots, GROUP)
+            for at in range(0, slots, HALF)
         ]
     )
     place = iota((rows, rows), 0)
@@ -241,6 +257,15 @@
             limit = limit_row(slots + (me ^ (k + 1)) * moves + m)
             out[at : at + 1, :rows] = limit.astype(F32)
     queries = qrel_out[...]
+    out[rows : 2 * rows, :latent] = queries.astype(F32)
+    out[: 2 * rows, latent:] = q2_out[...].astype(F32)
+
+    def send(first, count, sem):
+        return fetch(
+            [pltpu.make_async_copy(out.at[pl.ds(first, count)], out_hbm.at[pl.ds(first, count)], sem)]
+        )[0]
+
+    sent = [send(rows, rows, out_sems.at[0])]
     fresh_rows = rollouts * following
     new_keys[...] = jnp.zeros(new_keys.shape, F32)
     new_turns[...] = jnp.zeros(new_turns.shape, F32)
@@ -258,7 +283,8 @@
 
     best = jnp.full((page_len, rows), LOW, F32)
     for first in range(0, slots, GROUP):
-        chunks[first // GROUP].wait()
+        for copy in chunks[first // HALF : (first + GROUP) // HALF]:
+            copy.wait()
         keys = lat[first : first + GROUP].reshape(GROUP * page_len, latent)
         fresh = dot_nt(keys, queries)
         for g in range(GROUP):
@@ -302,10 +328,13 @@
     acc = acc + dot_tn(jnp.concatenate(weights, axis=0), jnp.concatenate(keys, axis=0))
     whole = jnp.sum(total, axis=0, keepdims=True) + jnp.sum(new_exp, axis=0, keepdims=True)
     out[:rows, :latent] = acc
-    out[rows : 2 * rows, :latent] = qrel_out[...].astype(F32)
     out[2 * rows : 2 * rows + 1, :rows] = peak
     out[2 * rows + 1 : 2 * rows + 2, :rows] = whole
-    out[: 2 * rows, latent:] = q2_out[...].astype(F32)
+    sent.append(send(2 * rows, out.shape[0] - 2 * rows, out_sems.at[1]))
+    for i in range(rows // OUT_ROWS):
+        sent.append(send(i * OUT_ROWS, OUT_ROWS, out_sems.at[2 + i]))
+    for copy in sent:
+        copy.wait()
 
 
 def merge_kernel(partners, *refs):
@@ -433,8 +462,9 @@
     refs[-1][...] = total.astype(BF16)
 
 
-def load_kernel(count, passed, *refs):
-    sources, passed_out, outs, sems = refs[:count], refs[count], refs[count + 1 : -1], refs[-1]
+def load_kernel(count, held, passed, *refs):
+    sources, passed_out = refs[held : held + count], refs[held + count]
+    outs, sems = refs[2 * held + count + 1 : -1], refs[-1]
     split = sems.shape[1]
     copies = []
     for k, (source, out) in enumerate(zip(sources, outs)):
@@ -452,20 +482,12 @@
 
 def expert_kernel(top, count, *refs):
     pieces = refs[:count]
-    w_router, w_gate, w_up, down_hbm = refs[count : count + 4]
-    kept, away, rows_ref, hidden_ref, w_down, sems = refs[count + 4 :]
+    w_router, w_gate, w_up, w_down = refs[count : count + 4]
+    kept, away, rows_ref, hidden_ref = refs[count + 4 :]
     expert = lax.axis_index(EXPERT)
     width, units = w_gate.shape
     in_step = 256 if units % 256 == 0 else units
     out_step = 512 if width % 512 == 0 else width
-    down_copies = fetch(
-        [
-            pltpu.make_async_copy(
-                down_hbm.at[0, pl.ds(at, in_step)], w_down.at[pl.ds(at, in_step)], sems.at[i]
-            )
-            for i, at in enumerate(range(0, units, in_step))
-        ]
-    )
     piece_rows = rows_ref.shape[0] // count
     named = []
     for k, piece in enumerate(pieces):
@@ -488,8 +510,6 @@
         up = dot_nn(rows, w_up[:, at : at + in_step])
         hidden_ref[:, at : at + in_step] = (gate / (1.0 + jnp.exp(-gate)) * up).astype(BF16)
     half = rows_ref.shape[0] // 2
-    for copy in down_copies:
-        copy.wait()
     hidden = hidden_ref[...]
     for at in range(0, width, out_step):
         part = dot_nn(hidden, w_down[:, at : at + out_step]) * gates
@@ -569,7 +589,7 @@
             pltpu.VMEM(page_scale.shape, BF16),
             pltpu.VMEM((slots,), F32),
             pltpu.SemaphoreType.DMA((partners, moves)),
-            pltpu.SemaphoreType.DMA((4,)),
+            pltpu.SemaphoreType.DMA((3 + slots // ROPE_ROWS,)),
         ],
         vmem=60,
     )
@@ -593,7 +613,9 @@
             new_rope,
         ),
         in_specs=[HBM] * 10,
+        out_specs=[HBM],
         scratch=[
+            pltpu.VMEM((2 * rows + extra, latent + 2 * rope_dim), F32),
             pltpu.SMEM((slots,), F32),
             pltpu.VMEM((rows, latent), BF16),
             pltpu.VMEM((2 * rows, 2 * rope_dim), BF16),
@@ -610,8 +632,9 @@
             pltpu.SMEM((rollouts * view,), jnp.int32),
             pltpu.VMEM((16, latent), F32),
             pltpu.VMEM((16, 2 * rope_dim), F32),
-            pltpu.SemaphoreType.DMA((9,)),
-            pltpu.SemaphoreType.DMA((slots // GROUP,)),
+            pltpu.SemaphoreType.DMA((8 + slots // ROPE_ROWS,)),
+            pltpu.SemaphoreType.DMA((slots // HALF,)),
+            pltpu.SemaphoreType.DMA((2 + rows // OUT_ROWS,)),
         ],
         vmem=60,
         cost=(2 * slots * page_len * rows * (2 * latent + 2 * rope_dim), 4 * MIB),
@@ -647,29 +670,37 @@
         (parts, residual, norm_gain, routes),
     )
 
-    def load(passed, sources, vmem):
-        return call(
-            functools.partial(load_kernel, len(sources)),
-            [shape(passed.shape, BF16)] + [shape(w.shape[1:], BF16) for w in sources],
-            (passed, *sources),
-            in_specs=[VMEM] + [HBM] * len(sources),
-            scratch=[pltpu.SemaphoreType.DMA((len(sources), 8))],
-            vmem=vmem,
-            cost=(0, 2 * sum(w.size for w in sources)),
-        )
+    def load(passed, sources, vmem, held=()):
+        outs = [shape(passed.shape, BF16)] + [shape(x.shape, BF16) for x in held]
+        return pl.pallas_call(
+            functools.partial(load_kernel, len(sources), len(held)),
+            out_shape=outs + [shape(w.shape[1:], BF16) for w in sources],
+            in_specs=[VMEM] + [ANY] * len(held) + [HBM] * len(sources),
+            out_specs=[VMEM] + [ANY] * len(held) + [VMEM] * len(sources),
+            input_output_aliases={1 + i: 1 + i for i in range(len(held))},
+            scratch_shapes=[pltpu.SemaphoreType.DMA((len(sources), 8))],
+            compiler_params=pltpu.CompilerParams(vmem_limit_bytes=vmem * MIB),
+            cost_estimate=pl.CostEstimate(
+                flops=0, bytes_accessed=2 * sum(w.size for w in sources), transcendentals=0
+            ),
+        )(passed, *held, *sources)
 
     if direct:
         others = [swap(own_rows, mask) for mask in masks[1:]]
+        own_rows, down_here = load(own_rows, (w_down,), LOAD_MIB)
         piece = call(
             stack_kernel,
             [shape((far_count, tokens, width + LANES), BF16)],
             (own_rows, *others),
         )[0]
     else:
+        own_rows, down_here = load(own_rows, (w_down,), LOAD_MIB)
         piece = deal(own_rows, FAR)
     pieces = [piece, swap(piece, top_bit, side_bit)]
     pieces = pieces + [swap(p, side_bit, top_bit) for p in pieces]
-    side_piece, gate_here, up_here = load(pieces[1], (w_gate, w_up), LOAD_MIB)
+    side_piece, down_here, gate_here, up_here = load(
+        pieces[1], (w_gate, w_up), SIDE_MIB, (down_here,)
+    )
     pieces = [piece, side_piece] + pieces[2:]
     pieces = pieces + [swap(p, 1) for p in pieces]
 
@@ -679,13 +710,10 @@
     kept, away = call(
         functools.partial(expert_kernel, routes.shape[1], len(pieces)),
         [shape((half, width), F32), shape((half, width), BF16)],
-        (*pieces, w_router.T, gate_here, up_here, w_down),
-        in_specs=[VMEM] * (len(pieces) + 3) + [HBM],
+        (*pieces, w_router.T, gate_here, up_here, down_here),
         scratch=[
             pltpu.VMEM((all_rows, width), BF16),
             pltpu.VMEM((all_rows, hidden_units), BF16),
-            pltpu.VMEM(w_down.shape[1:], BF16),
-            pltpu.SemaphoreType.DMA((16,)),
         ],
         vmem=EXPERT_MIB if all_rows <= 256 else 56,
         cost=(6 * all_rows * width * hidden_units, 6 * width * hidden_units),

time: 92.2 us -> 90.6 us (0.983)
  waiting for transfers between devices: 20.4 us -> 18.3 us
    pallas_call x0 -> x2, Pallas kernels: none -> 8.53 us  [load(): pl.pallas_call(functools.partial(load_kernel, len(sources), len(held)), o...]
    pallas_call x12 -> x11, Pallas kernels: 25.3 us -> 17 us  [call(): pl.pallas_call(kernel, out_shape=outs, in_specs=in_specs or [VMEM] * len(...]
    ppermute x20, waiting for transfers between devices: 20.4 us -> 18.3 us  [swap(): return lax.ppermute(x, ROWS, pairs)]
  transfers between devices with their start and end apart: 20 -> 20, of which waited for: 12 -> 9; matrix products, arithmetic and copies ran while one was open for 0% -> 0% of each run, Pallas kernels for 13% -> 18%
where the time goes in v5:
time: 90.6 us; the launch traced here: 90.3 us
  Pallas kernels  25.5 us (28%)
  blocking collectives  24 us (26%)
  starting transfers between devices  20.5 us (23%)
  waiting for transfers between devices  18.3 us (20%)
  local copies, waits for them, and re-layouts  1.11 us (1%)
    all_to_all x2, blocking collectives, deal(): return lax.all_to_all(x, names, split_axis=0, concat_axis=0, tiled=True)  24 us
    ppermute x20, starting transfers between devices, swap(): return lax.ppermute(x, ROWS, pairs)  20.5 us
    ppermute x20, waiting for transfers between devices, swap(): return lax.ppermute(x, ROWS, pairs)  18.3 us
    pallas_call x11, Pallas kernels, call(): pl.pallas_call(kernel, out_shape=outs, in_specs=in_specs or [VMEM] * len(...  17 us
    pallas_call x2, Pallas kernels, load(): pl.pallas_call(functools.partial(load_kernel, len(sources), len(held)), o...  8.53 us
  transfers between devices with their start and end apart: 20, of which 9 were waited for; matrix products, arithmetic and copies ran while one was open for 0% of the time, Pallas kernels for 18%

profile of v5, /device:TPU:0, one launch (start us, length us, event | category | flops | bytes accessed | tf_op | source)
XLA Modules:
  0.0 90.3 jit_solution(6328246031763595010)
XLA Ops:
  0.7 2.6 %shard_map.194 = (bf16[4,64,512]{2,1,0:T(8,128)(2,1)}, bf16[8,2176]{1,0:T(8,128)(2,1)}, f32[48]{0:T(128)}) custom-call(s32[1,2,4]{2,1,0:T(2,128)} %move_hbm.3, bf16[48]{0:T(256)(128)(2,1)} %scale_hbm.1, bf16[48,64,512]{2,1,0:T(8,128)(2,1)} %lat_hbm.1, bf16[48,4096]{1,0:T(8,128)(2,1)} %rope_hbm.3), custom_call_target="tpu_custom_call" | custom-call | tf_op jit(solution)/shard_map/pallas_call | solution.py:47
  3.3 3.0 %collective-permute-start = (bf16[4,64,512]{2,1,0:T(8,128)(2,1)}, bf16[4,64,512]{2,1,0:T(8,128)(2,1)S(1)}, u32[]{:S(2)}, u32[]{:S(2)}) collective-permute-start(bf16[4,64,512]{2,1,0:T(8,128)(2,1)} %get-tuple-element.26), channel_id=1, source_target_pairs={{0,16},{1,17},{2,18},{3,19},{4,20},{5,21},{6,22},{7,23},{8,24},{9,... | collective-permute-start | bytes 786440 | tf_op jit(solution)/shard_map/ppermute | solution.py:562
  6.4 7.4 %shard_map.195.refs_2_ = f32[264,640]{1,0:T(8,128)} custom-call(f32[48]{0:T(128)} %get-tuple-element.28.scale_hbm, s32[2,32]{1,0:T(2,128)} %table_hbm.1, s32[2]{0:T(128)} %lengths_hbm.1, s32[1,2,4]{2,1,0:T(2,128)} %move_hbm.3, bf16[48,64,512]{2,1,0:T(8,128)(2,1)} %lat_hbm.1, bf16[48,4096]{1,0:T(8,128)(2,1)} %rope_hbm.3, bf16[2,2,32,512]{3,2,1,0:T(8,128)(2,1)} %q_hbm.1, ...), custom_call_target="tpu_custom_call" | custom-call | flops 905969664 | bytes 4194304 | tf_op jit(solution)/shard_map/pallas_call | solution.py:47
  13.8 1.1 %copy-done = f32[264,640]{1,0:T(8,128)S(1)} copy-done((f32[264,640]{1,0:T(8,128)S(1)}, f32[264,640]{1,0:T(8,128)}, u32[]{:S(2)}) %copy-start) | copy-done | bytes 675864
  16.0 13.4 %all_to_all.10.blocks = bf16[8,16,512]{2,1,0:T(8,128)(2,1)S(1)} all-to-all(bf16[8,16,512]{2,1,0:T(8,128)(2,1)S(1)} %shard_map.196), channel_id=1, replica_groups=mesh['top'=2,'low'=1,'far'=4,'side'=2,'core'=2] {'far','side'}, dimensions={0} | all-to-all | bytes 262144 | tf_op jit(solution)/shard_map/all_to_all | solution.py:565
  29.4 1.1 %shard_map.197 = bf16[8,4,3584]{2,1,0:T(4,128)(2,1)S(1)} custom-call(bf16[8,16,512]{2,1,0:T(8,128)(2,1)S(1)} %all_to_all.10.blocks, bf16[2,512,128]{2,1,0:T(8,128)(2,1)S(1)} %copy-done.2, bf16[2,512,128]{2,1,0:T(8,128)(2,1)S(1)} %collective-permute-done.2.other_uv, bf16[256,3584]{1,0:T(8,128)(2,1)S(1)} %copy-done.1, ...), custom_call_target="tpu_custom_call" | custom-call | flops 117440512 | bytes 8388608 | tf_op jit(solution)/shard_map/pallas_call | solution.py:47
  30.6 10.6 %all_to_all.11.got = bf16[8,4,3584]{2,1,0:T(4,128)(2,1)S(1)} all-to-all(bf16[8,4,3584]{2,1,0:T(4,128)(2,1)S(1)} %shard_map.197), channel_id=1, replica_groups=mesh['top'=2,'low'=1,'far'=4,'side'=2,'core'=2] {'far','side'}, dimensions={0} | all-to-all | bytes 458752 | tf_op jit(solution)/shard_map/all_to_all | solution.py:565
  41.9 0.9 collective-permute-start.4
  43.4 2.9 %collective-permute-start.6 = (bf16[1,4,3712]{2,1,0:T(4,128)(2,1)S(1)}, bf16[1,4,3712]{2,1,0:T(4,128)(2,1)S(1)}, u32[]{:S(2)}, u32[]{:S(2)}) collective-permute-start(bf16[1,4,3712]{2,1,0:T(4,128)(2,1)S(1)} %get-tuple-element.33.passed), channel_id=1, source_target_pairs={{0,12},{1,13},{2,14},{3,15},{4,8},{5,9},{6,10},{7,11},{8,4},{9,5},... | collective-permute-start | bytes 89096 | tf_op jit(solution)/shard_map/ppermute | solution.py:562
  46.3 3.2 %shard_map.199 = (bf16[1,4,3712]{2,1,0:T(4,128)(2,1)S(1)}, bf16[1024,3584]{1,0:T(8,128)(2,1)S(1)}) custom-call(bf16[1,4,3712]{2,1,0:T(4,128)(2,1)S(1)} %get-tuple-element.33.passed, bf16[1,1024,3584]{2,1,0:T(8,128)(2,1)} %refs_0_.1), custom_call_target="tpu_custom_call" | custom-call | bytes 7340032 | tf_op jit(solution)/shard_map/pallas_call | solution.py:675
  49.6 1.6 %collective-permute-start.7 = (bf16[4,4,3712]{2,1,0:T(4,128)(2,1)S(1)}, bf16[4,4,3712]{2,1,0:T(4,128)(2,1)S(1)}, u32[]{:S(2)}, u32[]{:S(2)}) collective-permute-start(bf16[4,4,3712]{2,1,0:T(4,128)(2,1)S(1)} %shard_map.200.refs_0_), channel_id=1, source_target_pairs={{0,16},{1,3},{2,18},{3,1},{4,20},{5,7},{6,22},{7,5},{8,24},{9,11},... | collective-permute-start | bytes 356360 | tf_op jit(solution)/shard_map/ppermute | solution.py:562
  51.1 1.3 %collective-permute-start.8 = (bf16[4,4,3712]{2,1,0:T(4,128)(2,1)S(1)}, bf16[4,4,3712]{2,1,0:T(4,128)(2,1)S(1)}, u32[]{:S(2)}, u32[]{:S(2)}) collective-permute-start(bf16[4,4,3712]{2,1,0:T(4,128)(2,1)S(1)} %shard_map.200.refs_0_), channel_id=1, source_target_pairs={{0,2},{1,17},{2,0},{3,19},{4,6},{5,21},{6,4},{7,23},{8,10},{9,25},... | collective-permute-start | bytes 356360 | tf_op jit(solution)/shard_map/ppermute | solution.py:562
  52.4 3.3 %collective-permute-done.7.passed = bf16[4,4,3712]{2,1,0:T(4,128)(2,1)S(1)} collective-permute-done((bf16[4,4,3712]{2,1,0:T(4,128)(2,1)S(1)}, bf16[4,4,3712]{2,1,0:T(4,128)(2,1)S(1)}, u32[]{:S(2)}, u32[]{:S(2)}) %collective-permute-start.7) | collective-permute-done | bytes 118816 | tf_op jit(solution)/shard_map/ppermute | solution.py:562
  55.7 0.9 %collective-permute-start.9 = (bf16[4,4,3712]{2,1,0:T(4,128)(2,1)S(1)}, bf16[4,4,3712]{2,1,0:T(4,128)(2,1)S(1)}, u32[]{:S(2)}, u32[]{:S(2)}) collective-permute-start(bf16[4,4,3712]{2,1,0:T(4,128)(2,1)S(1)} %collective-permute-done.7.passed), channel_id=1, source_target_pairs={{0,2},{1,17},{2,0},{3,19},{4,6},{5,21},{6,4},{7,23},{8,10},{9,25},... | collective-permute-start | bytes 356360 | tf_op jit(solution)/shard_map/ppermute | solution.py:562
  56.6 5.4 %shard_map.201 = (bf16[4,4,3712]{2,1,0:T(4,128)(2,1)S(1)}, bf16[1024,3584]{1,0:T(8,128)(2,1)S(1)}, bf16[3584,1024]{1,0:T(8,128)(2,1)S(1)}, bf16[3584,1024]{1,0:T(8,128)(2,1)S(1)}) custom-call(bf16[4,4,3712]{2,1,0:T(4,128)(2,1)S(1)} %collective-permute-done.7.passed, ...), custom_call_target="tpu_custom_call", output_to_operand_aliasing={{1}: (1, {})} | custom-call | bytes 14680064 | tf_op jit(solution)/shard_map/pallas_call | solution.py:675
  64.0 3.8 %shard_map.202 = (f32[64,3584]{1,0:T(8,128)S(1)}, bf16[64,3584]{1,0:T(8,128)(2,1)S(1)}) custom-call(bf16[4,4,3712]{2,1,0:T(4,128)(2,1)S(1)} %shard_map.200.refs_0_, bf16[4,4,3712]{2,1,0:T(4,128)(2,1)S(1)} %get-tuple-element.36.refs_1_, bf16[4,4,3712]{2,1,0:T(4,128)(2,1)S(1)} %collective-permute-done.8.refs_2_, ...), custom_call_target="tpu_custom_call" | custom-call | flops 2818572288 | bytes 22020096 | tf_op jit(solution)/shard_map/pallas_call | solution.py:47
  68.3 1.5 %collective-permute-done.14.got = bf16[64,3584]{1,0:T(8,128)(2,1)S(1)} collective-permute-done((bf16[64,3584]{1,0:T(8,128)(2,1)S(1)}, bf16[64,3584]{1,0:T(8,128)(2,1)S(1)}, u32[]{:S(2)}, u32[]{:S(2)}) %collective-permute-start.14) | collective-permute-done | bytes 458784 | tf_op jit(solution)/shard_map/ppermute | solution.py:562
  69.8 1.2 %collective-permute-start.15 = (bf16[32,3584]{1,0:T(8,128)(2,1)S(1)}, bf16[32,3584]{1,0:T(8,128)(2,1)S(1)}, u32[]{:S(2)}, u32[]{:S(2)}) collective-permute-start(bf16[32,3584]{1,0:T(8,128)(2,1)S(1)} %get-tuple-element.43), channel_id=1, source_target_pairs={{0,2},{1,17},{2,0},{3,19},{4,6},{5,21},{6,4},{7,23},{8,10},{9,25},... | collective-permute-start | bytes 688136 | tf_op jit(solution)/shard_map/ppermute | solution.py:562
  71.0 4.9 %collective-permute-done.15.got = bf16[32,3584]{1,0:T(8,128)(2,1)S(1)} collective-permute-done((bf16[32,3584]{1,0:T(8,128)(2,1)S(1)}, bf16[32,3584]{1,0:T(8,128)(2,1)S(1)}, u32[]{:S(2)}, u32[]{:S(2)}) %collective-permute-start.15) | collective-permute-done | bytes 229408 | tf_op jit(solution)/shard_map/ppermute | solution.py:562
  76.0 1.6 %collective-permute-start.16 = (bf16[16,3584]{1,0:T(8,128)(2,1)S(1)}, bf16[16,3584]{1,0:T(8,128)(2,1)S(1)}, u32[]{:S(2)}, u32[]{:S(2)}) collective-permute-start(bf16[16,3584]{1,0:T(8,128)(2,1)S(1)} %get-tuple-element.45), channel_id=1, source_target_pairs={{0,16},{1,3},{2,18},{3,1},{4,20},{5,7},{6,22},{7,5},{8,24},{9,11},... | collective-permute-start | bytes 344072 | tf_op jit(solution)/shard_map/ppermute | solution.py:562
  77.5 3.3 %collective-permute-done.16.got = bf16[16,3584]{1,0:T(8,128)(2,1)S(1)} collective-permute-done((bf16[16,3584]{1,0:T(8,128)(2,1)S(1)}, bf16[16,3584]{1,0:T(8,128)(2,1)S(1)}, u32[]{:S(2)}, u32[]{:S(2)}) %collective-permute-start.16) | collective-permute-done | bytes 114720 | tf_op jit(solution)/shard_map/ppermute | solution.py:562
  80.9 3.0 %collective-permute-start.18 = (bf16[4,3584]{1,0:T(4,128)(2,1)S(1)}, bf16[4,3584]{1,0:T(4,128)(2,1)S(1)}, u32[]{:S(2)}, u32[]{:S(2)}) collective-permute-start(bf16[4,3584]{1,0:T(4,128)(2,1)S(1)} %get-tuple-element.48), channel_id=1, source_target_pairs={{0,8},{1,9},{2,10},{3,11},{4,12},{5,13},{6,14},{7,15},{8,0},{9,1},... | collective-permute-start | bytes 86024 | tf_op jit(solution)/shard_map/ppermute | solution.py:562
  84.0 1.3 %collective-permute-start.19 = (bf16[4,3584]{1,0:T(4,128)(2,1)S(1)}, bf16[4,3584]{1,0:T(4,128)(2,1)S(1)}, u32[]{:S(2)}, u32[]{:S(2)}) collective-permute-start(bf16[4,3584]{1,0:T(4,128)(2,1)S(1)} %get-tuple-element.49), channel_id=1, source_target_pairs={{0,12},{1,13},{2,14},{3,15},{4,8},{5,9},{6,10},{7,11},{8,4},{9,5},... | collective-permute-start | bytes 86024 | tf_op jit(solution)/shard_map/ppermute | solution.py:562
  85.8 3.8 %collective-permute-done.19.refs_3_ = bf16[4,3584]{1,0:T(4,128)(2,1)S(1)} collective-permute-done((bf16[4,3584]{1,0:T(4,128)(2,1)S(1)}, bf16[4,3584]{1,0:T(4,128)(2,1)S(1)}, u32[]{:S(2)}, u32[]{:S(2)}) %collective-permute-start.19) | collective-permute-done | bytes 28704 | tf_op jit(solution)/shard_map/ppermute | solution.py:562
  (45 shorter events, 6.4 us)
Async XLA Ops:
  0.6 14.9 %copy-start.2 = (bf16[2,512,128]{2,1,0:T(8,128)(2,1)S(1)}, bf16[2,512,128]{2,1,0:T(8,128)(2,1)}, u32[]{:S(2)}) copy-start(bf16[2,512,128]{2,1,0:T(8,128)(2,1)} %w_uv.1) | copy-start | bytes 786436
  0.7 40.6 %copy-start.4 = (bf16[4,3584]{1,0:T(4,128)(2,1)S(1)}, bf16[4,3584]{1,0:T(4,128)(2,1)}, u32[]{:S(2)}) copy-start(bf16[4,3584]{1,0:T(4,128)(2,1)} %residual.1) | copy-start | bytes 86020
  0.7 40.5 %copy-start.5 = (f32[3584]{0:T(1024)S(1)}, f32[3584]{0:T(1024)}, u32[]{:S(2)}) copy-start(f32[3584]{0:T(1024)} %gain.1) | copy-start | bytes 43012
  0.7 40.5 %copy-start.6 = (s32[4,8]{1,0:T(4,128)S(1)}, s32[4,8]{1,0:T(4,128)}, u32[]{:S(2)}) copy-start(s32[4,8]{1,0:T(4,128)} %routes.1) | copy-start | bytes 388
  3.3 10.5 %collective-permute-start = (bf16[4,64,512]{2,1,0:T(8,128)(2,1)}, bf16[4,64,512]{2,1,0:T(8,128)(2,1)S(1)}, u32[]{:S(2)}, u32[]{:S(2)}) collective-permute-start(bf16[4,64,512]{2,1,0:T(8,128)(2,1)} %get-tuple-element.26), channel_id=1, source_target_pairs={{0,16},{1,17},{2,18},{3,19},{4,20},{5,21},{6,22},{7,23},{8,24},{9,... | collective-permute-start | bytes 786440 | tf_op jit(solution)/shard_map/ppermute | solution.py:562
  6.3 7.4 %collective-permute-start.1 = (bf16[8,2176]{1,0:T(8,128)(2,1)}, bf16[8,2176]{1,0:T(8,128)(2,1)S(1)}, u32[]{:S(2)}, u32[]{:S(2)}) collective-permute-start(bf16[8,2176]{1,0:T(8,128)(2,1)} %get-tuple-element.27), channel_id=1, source_target_pairs={{0,16},{1,17},{2,18},{3,19},{4,20},{5,21},{6,22},{7,23},{8,24},{9,... | collective-permute-start | bytes 104456 | tf_op jit(solution)/shard_map/ppermute | solution.py:562
  15.4 14.0 %collective-permute-start.3 = (bf16[256,3584]{1,0:T(8,128)(2,1)S(1)}, bf16[256,3584]{1,0:T(8,128)(2,1)S(1)}, u32[]{:S(2)}, u32[]{:S(2)}) collective-permute-start(bf16[256,3584]{1,0:T(8,128)(2,1)S(1)} %copy-done.1), channel_id=1, source_target_pairs={{0,1},{1,0},{2,3},{3,2},{4,5},{5,4},{6,7},{7,6},{8,9},{9,8},{10,11... | collective-permute-start | bytes 5505032 | tf_op jit(solution)/shard_map/ppermute | solution.py:562
  15.5 13.9 %collective-permute-start.2 = (bf16[2,512,128]{2,1,0:T(8,128)(2,1)S(1)}, bf16[2,512,128]{2,1,0:T(8,128)(2,1)S(1)}, u32[]{:S(2)}, u32[]{:S(2)}) collective-permute-start(bf16[2,512,128]{2,1,0:T(8,128)(2,1)S(1)} %copy-done.2), channel_id=1, source_target_pairs={{0,1},{1,0},{2,3},{3,2},{4,5},{5,4},{6,7},{7,6},{8,9},{9,8},{10,11... | collective-permute-start | bytes 786440 | tf_op jit(solution)/shard_map/ppermute | solution.py:562
  41.9 7.6 %collective-permute-start.4 = (bf16[1,4,3712]{2,1,0:T(4,128)(2,1)S(1)}, bf16[1,4,3712]{2,1,0:T(4,128)(2,1)S(1)}, u32[]{:S(2)}, u32[]{:S(2)}) collective-permute-start(bf16[1,4,3712]{2,1,0:T(4,128)(2,1)S(1)} %get-tuple-element.33.passed), channel_id=1, source_target_pairs={{0,4},{1,5},{2,6},{3,7},{4,0},{5,1},{6,2},{7,3},{8,12},{9,13},{10,... | collective-permute-start | bytes 89096 | tf_op jit(solution)/shard_map/ppermute | solution.py:562
  42.8 6.7 %collective-permute-start.5 = (bf16[1,4,3712]{2,1,0:T(4,128)(2,1)S(1)}, bf16[1,4,3712]{2,1,0:T(4,128)(2,1)S(1)}, u32[]{:S(2)}, u32[]{:S(2)}) collective-permute-start(bf16[1,4,3712]{2,1,0:T(4,128)(2,1)S(1)} %get-tuple-element.33.passed), channel_id=1, source_target_pairs={{0,8},{1,9},{2,10},{3,11},{4,12},{5,13},{6,14},{7,15},{8,0},{9,1},... | collective-permute-start | bytes 89096 | tf_op jit(solution)/shard_map/ppermute | solution.py:562
  43.4 6.1 %collective-permute-start.6 = (bf16[1,4,3712]{2,1,0:T(4,128)(2,1)S(1)}, bf16[1,4,3712]{2,1,0:T(4,128)(2,1)S(1)}, u32[]{:S(2)}, u32[]{:S(2)}) collective-permute-start(bf16[1,4,3712]{2,1,0:T(4,128)(2,1)S(1)} %get-tuple-element.33.passed), channel_id=1, source_target_pairs={{0,12},{1,13},{2,14},{3,15},{4,8},{5,9},{6,10},{7,11},{8,4},{9,5},... | collective-permute-start | bytes 89096 | tf_op jit(solution)/shard_map/ppermute | solution.py:562
  49.6 6.1 %collective-permute-start.7 = (bf16[4,4,3712]{2,1,0:T(4,128)(2,1)S(1)}, bf16[4,4,3712]{2,1,0:T(4,128)(2,1)S(1)}, u32[]{:S(2)}, u32[]{:S(2)}) collective-permute-start(bf16[4,4,3712]{2,1,0:T(4,128)(2,1)S(1)} %shard_map.200.refs_0_), channel_id=1, source_target_pairs={{0,16},{1,3},{2,18},{3,1},{4,20},{5,7},{6,22},{7,5},{8,24},{9,11},... | collective-permute-start | bytes 356360 | tf_op jit(solution)/shard_map/ppermute | solution.py:562
  51.1 11.4 %collective-permute-start.8 = (bf16[4,4,3712]{2,1,0:T(4,128)(2,1)S(1)}, bf16[4,4,3712]{2,1,0:T(4,128)(2,1)S(1)}, u32[]{:S(2)}, u32[]{:S(2)}) collective-permute-start(bf16[4,4,3712]{2,1,0:T(4,128)(2,1)S(1)} %shard_map.200.refs_0_), channel_id=1, source_target_pairs={{0,2},{1,17},{2,0},{3,19},{4,6},{5,21},{6,4},{7,23},{8,10},{9,25},... | collective-permute-start | bytes 356360 | tf_op jit(solution)/shard_map/ppermute | solution.py:562
  55.7 6.9 %collective-permute-start.9 = (bf16[4,4,3712]{2,1,0:T(4,128)(2,1)S(1)}, bf16[4,4,3712]{2,1,0:T(4,128)(2,1)S(1)}, u32[]{:S(2)}, u32[]{:S(2)}) collective-permute-start(bf16[4,4,3712]{2,1,0:T(4,128)(2,1)S(1)} %collective-permute-done.7.passed), channel_id=1, source_target_pairs={{0,2},{1,17},{2,0},{3,19},{4,6},{5,21},{6,4},{7,23},{8,10},{9,25},... | collective-permute-start | bytes 356360 | tf_op jit(solution)/shard_map/ppermute | solution.py:562
  56.6 6.5 %collective-permute-start.10 = (bf16[4,4,3712]{2,1,0:T(4,128)(2,1)S(1)}, bf16[4,4,3712]{2,1,0:T(4,128)(2,1)S(1)}, u32[]{:S(2)}, u32[]{:S(2)}) collective-permute-start(bf16[4,4,3712]{2,1,0:T(4,128)(2,1)S(1)} %shard_map.200.refs_0_), channel_id=1, source_target_pairs={{0,1},{1,0},{2,3},{3,2},{4,5},{5,4},{6,7},{7,6},{8,9},{9,8},{10,11... | collective-permute-start | bytes 356360 | tf_op jit(solution)/shard_map/ppermute | solution.py:562
  61.9 1.5 %collective-permute-start.11 = (bf16[4,4,3712]{2,1,0:T(4,128)(2,1)S(1)}, bf16[4,4,3712]{2,1,0:T(4,128)(2,1)S(1)}, u32[]{:S(2)}, u32[]{:S(2)}) collective-permute-start(bf16[4,4,3712]{2,1,0:T(4,128)(2,1)S(1)} %get-tuple-element.36.refs_1_), channel_id=1, source_target_pairs={{0,1},{1,0},{2,3},{3,2},{4,5},{5,4},{6,7},{7,6},{8,9},{9,8},{10,11... | collective-permute-start | bytes 356360 | tf_op jit(solution)/shard_map/ppermute | solution.py:562
  62.5 1.3 %collective-permute-start.12 = (bf16[4,4,3712]{2,1,0:T(4,128)(2,1)S(1)}, bf16[4,4,3712]{2,1,0:T(4,128)(2,1)S(1)}, u32[]{:S(2)}, u32[]{:S(2)}) collective-permute-start(bf16[4,4,3712]{2,1,0:T(4,128)(2,1)S(1)} %collective-permute-done.8.refs_2_), channel_id=1, source_target_pairs={{0,1},{1,0},{2,3},{3,2},{4,5},{5,4},{6,7},{7,6},{8,9},{9,8},{10,11... | collective-permute-start | bytes 356360 | tf_op jit(solution)/shard_map/ppermute | solution.py:562
  62.6 1.4 %collective-permute-start.13 = (bf16[4,4,3712]{2,1,0:T(4,128)(2,1)S(1)}, bf16[4,4,3712]{2,1,0:T(4,128)(2,1)S(1)}, u32[]{:S(2)}, u32[]{:S(2)}) collective-permute-start(bf16[4,4,3712]{2,1,0:T(4,128)(2,1)S(1)} %collective-permute-done.9.refs_3_), channel_id=1, source_target_pairs={{0,1},{1,0},{2,3},{3,2},{4,5},{5,4},{6,7},{7,6},{8,9},{9,8},{10,11... | collective-permute-start | bytes 356360 | tf_op jit(solution)/shard_map/ppermute | solution.py:562
  67.9 1.9 %collective-permute-start.14 = (bf16[64,3584]{1,0:T(8,128)(2,1)S(1)}, bf16[64,3584]{1,0:T(8,128)(2,1)S(1)}, u32[]{:S(2)}, u32[]{:S(2)}) collective-permute-start(bf16[64,3584]{1,0:T(8,128)(2,1)S(1)} %get-tuple-element.41), channel_id=1, source_target_pairs={{0,1},{1,0},{2,3},{3,2},{4,5},{5,4},{6,7},{7,6},{8,9},{9,8},{10,11... | collective-permute-start | bytes 1376264 | tf_op jit(solution)/shard_map/ppermute | solution.py:562
  69.8 6.1 %collective-permute-start.15 = (bf16[32,3584]{1,0:T(8,128)(2,1)S(1)}, bf16[32,3584]{1,0:T(8,128)(2,1)S(1)}, u32[]{:S(2)}, u32[]{:S(2)}) collective-permute-start(bf16[32,3584]{1,0:T(8,128)(2,1)S(1)} %get-tuple-element.43), channel_id=1, source_target_pairs={{0,2},{1,17},{2,0},{3,19},{4,6},{5,21},{6,4},{7,23},{8,10},{9,25},... | collective-permute-start | bytes 688136 | tf_op jit(solution)/shard_map/ppermute | solution.py:562
  76.0 4.9 %collective-permute-start.16 = (bf16[16,3584]{1,0:T(8,128)(2,1)S(1)}, bf16[16,3584]{1,0:T(8,128)(2,1)S(1)}, u32[]{:S(2)}, u32[]{:S(2)}) collective-permute-start(bf16[16,3584]{1,0:T(8,128)(2,1)S(1)} %get-tuple-element.45), channel_id=1, source_target_pairs={{0,16},{1,3},{2,18},{3,1},{4,20},{5,7},{6,22},{7,5},{8,24},{9,11},... | collective-permute-start | bytes 344072 | tf_op jit(solution)/shard_map/ppermute | solution.py:562
  80.9 4.5 %collective-permute-start.17 = (bf16[4,3584]{1,0:T(4,128)(2,1)S(1)}, bf16[4,3584]{1,0:T(4,128)(2,1)S(1)}, u32[]{:S(2)}, u32[]{:S(2)}) collective-permute-start(bf16[4,3584]{1,0:T(4,128)(2,1)S(1)} %get-tuple-element.47), channel_id=1, source_target_pairs={{0,4},{1,5},{2,6},{3,7},{4,0},{5,1},{6,2},{7,3},{8,12},{9,13},{10,... | collective-permute-start | bytes 86024 | tf_op jit(solution)/shard_map/ppermute | solution.py:562
  80.9 4.9 %collective-permute-start.18 = (bf16[4,3584]{1,0:T(4,128)(2,1)S(1)}, bf16[4,3584]{1,0:T(4,128)(2,1)S(1)}, u32[]{:S(2)}, u32[]{:S(2)}) collective-permute-start(bf16[4,3584]{1,0:T(4,128)(2,1)S(1)} %get-tuple-element.48), channel_id=1, source_target_pairs={{0,8},{1,9},{2,10},{3,11},{4,12},{5,13},{6,14},{7,15},{8,0},{9,1},... | collective-permute-start | bytes 86024 | tf_op jit(solution)/shard_map/ppermute | solution.py:562
  84.0 5.7 %collective-permute-start.19 = (bf16[4,3584]{1,0:T(4,128)(2,1)S(1)}, bf16[4,3584]{1,0:T(4,128)(2,1)S(1)}, u32[]{:S(2)}, u32[]{:S(2)}) collective-permute-start(bf16[4,3584]{1,0:T(4,128)(2,1)S(1)} %get-tuple-element.49), channel_id=1, source_target_pairs={{0,12},{1,13},{2,14},{3,15},{4,8},{5,9},{6,10},{7,11},{8,4},{9,5},... | collective-permute-start | bytes 86024 | tf_op jit(solution)/shard_map/ppermute | solution.py:562
  (3 other events, 23.3 us)

commit v6 on v5

--- a/solution.py
+++ b/solution.py
@@ -25,7 +25,8 @@
 FAR = ("low", "far")
 CHIP = ("far", "side")
 ROPE_ROWS = 16
-LOAD_MIB = 40
+UP_MIB = 40
+LOAD_MIB = 34
 SIDE_MIB = 28
 EXPERT_MIB = 16
 
@@ -462,9 +463,9 @@
     refs[-1][...] = total.astype(BF16)
 
 
-def load_kernel(count, held, passed, *refs):
-    sources, passed_out = refs[held : held + count], refs[held + count]
-    outs, sems = refs[2 * held + count + 1 : -1], refs[-1]
+def load_kernel(count, held, after, passed, *refs):
+    sources, passed_out = refs[held : held + count], refs[held + count + after]
+    outs, sems = refs[2 * held + count + after + 1 : -1], refs[-1]
     split = sems.shape[1]
     copies = []
     for k, (source, out) in enumerate(zip(sources, outs)):
@@ -649,12 +650,28 @@
 
     away_uv, away_out, blocks = lax.optimization_barrier((w_uv, w_out, blocks))
     other_uv, other_out = swap(away_uv, 1), swap(away_out, 1)
+    def load(passed, sources, vmem, held=(), after=()):
+        outs = [shape(passed.shape, BF16)] + [shape(x.shape, BF16) for x in held]
+        return pl.pallas_call(
+            functools.partial(load_kernel, len(sources), len(held), len(after)),
+            out_shape=outs + [shape(w.shape[1:], BF16) for w in sources],
+            in_specs=[VMEM] + [ANY] * len(held) + [HBM] * len(sources) + [ANY] * len(after),
+            out_specs=[VMEM] + [ANY] * len(held) + [VMEM] * len(sources),
+            input_output_aliases={1 + i: 1 + i for i in range(len(held))},
+            scratch_shapes=[pltpu.SemaphoreType.DMA((len(sources), 8))],
+            compiler_params=pltpu.CompilerParams(vmem_limit_bytes=vmem * MIB),
+            cost_estimate=pl.CostEstimate(
+                flops=0, bytes_accessed=2 * sum(w.size for w in sources), transcendentals=0
+            ),
+        )(passed, *held, *sources, *after)
+
+    own_uv, up_here = load(w_uv, (w_up,), UP_MIB, after=(blocks,))
     blocks = deal(blocks, CHIP)
 
     parts = call(
         functools.partial(project_kernel, tokens),
         [shape((chips, tokens, width), BF16)],
-        (blocks, w_uv, other_uv, w_out, other_out),
+        (blocks, own_uv, other_uv, w_out, other_out),
         cost=(4 * chips * tokens * width * w_out.shape[0], 8 * MIB),
     )[0]
     parts = deal(parts, CHIP)
@@ -670,36 +687,21 @@
         (parts, residual, norm_gain, routes),
     )
 
-    def load(passed, sources, vmem, held=()):
-        outs = [shape(passed.shape, BF16)] + [shape(x.shape, BF16) for x in held]
-        return pl.pallas_call(
-            functools.partial(load_kernel, len(sources), len(held)),
-            out_shape=outs + [shape(w.shape[1:], BF16) for w in sources],
-            in_specs=[VMEM] + [ANY] * len(held) + [HBM] * len(sources),
-            out_specs=[VMEM] + [ANY] * len(held) + [VMEM] * len(sources),
-            input_output_aliases={1 + i: 1 + i for i in range(len(held))},
-            scratch_shapes=[pltpu.SemaphoreType.DMA((len(sources), 8))],
-            compiler_params=pltpu.CompilerParams(vmem_limit_bytes=vmem * MIB),
-            cost_estimate=pl.CostEstimate(
-                flops=0, bytes_accessed=2 * sum(w.size for w in sources), transcendentals=0
-            ),
-        )(passed, *held, *sources)
-
     if direct:
         others = [swap(own_rows, mask) for mask in masks[1:]]
-        own_rows, down_here = load(own_rows, (w_down,), LOAD_MIB)
+        own_rows, up_here, down_here = load(own_rows, (w_down,), LOAD_MIB, (up_here,))
         piece = call(
             stack_kernel,
             [shape((far_count, tokens, width + LANES), BF16)],
             (own_rows, *others),
         )[0]
     else:
-        own_rows, down_here = load(own_rows, (w_down,), LOAD_MIB)
+        own_rows, up_here, down_here = load(own_rows, (w_down,), LOAD_MIB, (up_here,))
         piece = deal(own_rows, FAR)
     pieces = [piece, swap(piece, top_bit, side_bit)]
     pieces = pieces + [swap(p, side_bit, top_bit) for p in pieces]
-    side_piece, down_here, gate_here, up_here = load(
-        pieces[1], (w_gate, w_up), SIDE_MIB, (down_here,)
+    side_piece, up_here, down_here, gate_here = load(
+        pieces[1], (w_gate,), SIDE_MIB, (up_here, down_here)
     )
     pieces = [piece, side_piece] + pieces[2:]
     pieces = pieces + [swap(p, 1) for p in pieces]

time: 90.6 us -> 106 us (1.17)
  local copies, waits for them, and re-layouts: 1.11 us -> 19 us
  blocking collectives: 24 us -> 12.7 us
  starting transfers between devices: 20.5 us -> 26.5 us
  Pallas kernels: 25.5 us -> 28.7 us
    unnamed x14 -> x26, local copies, waits for them, and re-layouts: 1.11 us -> 19 us
    all_to_all x2 -> x1, blocking collectives: 24 us -> 12.7 us  [deal(): return lax.all_to_all(x, names, split_axis=0, concat_axis=0, tiled=True)]
    all_to_all x0 -> x1, starting transfers between devices: none -> 6.29 us  [deal(): return lax.all_to_all(x, names, split_axis=0, concat_axis=0, tiled=True)]
    pallas_call x11, Pallas kernels: 17 us -> 19.1 us  [call(): pl.pallas_call(kernel, out_shape=outs, in_specs=in_specs or [VMEM] * len(...]
    ppermute x20, waiting for transfers between devices: 18.3 us -> 16.4 us  [swap(): return lax.ppermute(x, ROWS, pairs)]
    all_to_all x0 -> x1, waiting for transfers between devices: none -> 1.25 us  [deal(): return lax.all_to_all(x, names, split_axis=0, concat_axis=0, tiled=True)]
    pallas_call x2 -> x3, Pallas kernels: 8.53 us -> 9.54 us  [load(): pl.pallas_call(functools.partial(load_kernel, len(sources), len(held), le...]
  transfers between devices with their start and end apart: 20 -> 21, of which waited for: 9 -> 10; matrix products, arithmetic and copies ran while one was open for 0% -> 0% of each run, Pallas kernels for 18% -> 16%
where the time goes in v6:
time: 106 us; the launch traced here: 105 us
  Pallas kernels  28.7 us (27%)
  starting transfers between devices  26.5 us (25%)
  local copies, waits for them, and re-layouts  19 us (18%)
  waiting for transfers between devices  17.7 us (17%)
  blocking collectives  12.7 us (12%)
    ppermute x20, starting transfers between devices, swap(): return lax.ppermute(x, ROWS, pairs)  20.3 us
    pallas_call x11, Pallas kernels, call(): pl.pallas_call(kernel, out_shape=outs, in_specs=in_specs or [VMEM] * len(...  19.1 us
    unnamed x26, local copies, waits for them, and re-layouts  19 us
    ppermute x20, waiting for transfers between devices, swap(): return lax.ppermute(x, ROWS, pairs)  16.4 us
    all_to_all x1, blocking collectives, deal(): return lax.all_to_all(x, names, split_axis=0, concat_axis=0, tiled=True)  12.7 us
    pallas_call x3, Pallas kernels, load(): pl.pallas_call(functools.partial(load_kernel, len(sources), len(held), le...  9.54 us
    all_to_all x1, starting transfers between devices, deal(): return lax.all_to_all(x, names, split_axis=0, concat_axis=0, tiled=True)  6.29 us
  transfers between devices with their start and end apart: 21, of which 10 were waited for; matrix products, arithmetic and copies ran while one was open for 0% of the time, Pallas kernels for 16%

profile of v6, /device:TPU:0, one launch (start us, length us, event | category | flops | bytes accessed | tf_op | source)
XLA Modules:
  0.0 105.4 jit_solution(8064949845274004050)
XLA Ops:
  0.7 2.6 %shard_map.194 = (bf16[4,64,512]{2,1,0:T(8,128)(2,1)}, bf16[8,2176]{1,0:T(8,128)(2,1)}, f32[48]{0:T(128)}) custom-call(s32[1,2,4]{2,1,0:T(2,128)} %move_hbm.3, bf16[48]{0:T(256)(128)(2,1)} %scale_hbm.1, bf16[48,64,512]{2,1,0:T(8,128)(2,1)} %lat_hbm.1, bf16[48,4096]{1,0:T(8,128)(2,1)} %rope_hbm.3), custom_call_target="tpu_custom_call" | custom-call | tf_op jit(solution)/shard_map/pallas_call | solution.py:48
  3.3 3.0 %collective-permute-start = (bf16[4,64,512]{2,1,0:T(8,128)(2,1)}, bf16[4,64,512]{2,1,0:T(8,128)(2,1)S(1)}, u32[]{:S(2)}, u32[]{:S(2)}) collective-permute-start(bf16[4,64,512]{2,1,0:T(8,128)(2,1)} %get-tuple-element.29), channel_id=1, source_target_pairs={{0,16},{1,17},{2,18},{3,19},{4,20},{5,21},{6,22},{7,23},{8,24},{9,... | collective-permute-start | bytes 786440 | tf_op jit(solution)/shard_map/ppermute | solution.py:563
  6.3 7.4 %shard_map.195.refs_2_ = f32[264,640]{1,0:T(8,128)} custom-call(f32[48]{0:T(128)} %get-tuple-element.31.scale_hbm, s32[2,32]{1,0:T(2,128)} %table_hbm.1, s32[2]{0:T(128)} %lengths_hbm.1, s32[1,2,4]{2,1,0:T(2,128)} %move_hbm.3, bf16[48,64,512]{2,1,0:T(8,128)(2,1)} %lat_hbm.1, bf16[48,4096]{1,0:T(8,128)(2,1)} %rope_hbm.3, bf16[2,2,32,512]{3,2,1,0:T(8,128)(2,1)} %q_hbm.1, ...), custom_call_target="tpu_custom_call" | custom-call | flops 905969664 | bytes 4194304 | tf_op jit(solution)/shard_map/pallas_call | solution.py:48
  16.5 6.3 %all-to-all-start = ((bf16[8,16,512]{2,1,0:T(8,128)(2,1)}), bf16[8,16,512]{2,1,0:T(8,128)(2,1)S(1)}, u32[]{:S(2)}, u32[]{:S(2)}) async-start(bf16[8,16,512]{2,1,0:T(8,128)(2,1)} %shard_map.196.refs_1_), calls=%async_computation | async-start | bytes 262144 | tf_op jit(solution)/shard_map/all_to_all | solution.py:566
  22.8 3.2 %shard_map.197 = (bf16[2,512,128]{2,1,0:T(8,128)(2,1)S(1)}, bf16[3584,1024]{1,0:T(8,128)(2,1)S(1)}) custom-call(bf16[2,512,128]{2,1,0:T(8,128)(2,1)S(1)} %copy-done.8, bf16[1,3584,1024]{2,1,0:T(8,128)(2,1)} %refs_0_.1, bf16[8,16,512]{2,1,0:T(8,128)(2,1)} %shard_map.196.refs_1_), custom_call_target="tpu_custom_call" | custom-call | bytes 7340032 | tf_op jit(solution)/shard_map/pallas_call | solution.py:655
  26.0 2.9 %copy-done = bf16[3584,1024]{1,0:T(8,128)(2,1)} copy-done((bf16[3584,1024]{1,0:T(8,128)(2,1)}, bf16[3584,1024]{1,0:T(8,128)(2,1)S(1)}, u32[]{:S(2)}) %copy-start) | copy-done | bytes 7340056
  30.2 2.6 %shard_map.198 = bf16[8,4,3584]{2,1,0:T(4,128)(2,1)S(1)} custom-call(bf16[8,16,512]{2,1,0:T(8,128)(2,1)S(1)} %all-to-all-done.blocks, bf16[2,512,128]{2,1,0:T(8,128)(2,1)S(1)} %get-tuple-element.33.w_uv, bf16[2,512,128]{2,1,0:T(8,128)(2,1)S(1)} %collective-permute-done.2.other_uv, bf16[256,3584]{1,0:T(8,128)(2,1)S(1)} %copy-done.7, ...), custom_call_target="tpu_custom_call" | custom-call | flops 117440512 | bytes 8388608 | tf_op jit(solution)/shard_map/pallas_call | solution.py:48
  32.8 12.7 %all_to_all.10.got = bf16[8,4,3584]{2,1,0:T(4,128)(2,1)S(1)} all-to-all(bf16[8,4,3584]{2,1,0:T(4,128)(2,1)S(1)} %shard_map.198), channel_id=1, replica_groups=mesh['top'=2,'low'=1,'far'=4,'side'=2,'core'=2] {'far','side'}, dimensions={0} | all-to-all | bytes 458752 | tf_op jit(solution)/shard_map/all_to_all | solution.py:566
  47.7 2.9 %collective-permute-start.6 = (bf16[1,4,3712]{2,1,0:T(4,128)(2,1)S(1)}, bf16[1,4,3712]{2,1,0:T(4,128)(2,1)S(1)}, u32[]{:S(2)}, u32[]{:S(2)}) collective-permute-start(bf16[1,4,3712]{2,1,0:T(4,128)(2,1)S(1)} %get-tuple-element.37.passed), channel_id=1, source_target_pairs={{0,12},{1,13},{2,14},{3,15},{4,8},{5,9},{6,10},{7,11},{8,4},{9,5},... | collective-permute-start | bytes 89096 | tf_op jit(solution)/shard_map/ppermute | solution.py:563
  50.6 3.1 %copy-done.1 = bf16[3584,1024]{1,0:T(8,128)(2,1)S(1)} copy-done((bf16[3584,1024]{1,0:T(8,128)(2,1)S(1)}, bf16[3584,1024]{1,0:T(8,128)(2,1)}, u32[]{:S(2)}) %copy-start.1) | copy-done | bytes 7340056
  53.7 3.2 %shard_map.200 = (bf16[1,4,3712]{2,1,0:T(4,128)(2,1)S(1)}, bf16[3584,1024]{1,0:T(8,128)(2,1)S(1)}, bf16[1024,3584]{1,0:T(8,128)(2,1)S(1)}) custom-call(bf16[1,4,3712]{2,1,0:T(4,128)(2,1)S(1)} %get-tuple-element.37.passed, bf16[3584,1024]{1,0:T(8,128)(2,1)S(1)} %copy-done.1, bf16[1,1024,3584]{2,1,0:T(8,128)(2,1)} %refs_1_.1), custom_call_target="tpu_custom_call", output_to_operand_aliasing={{1}: (1, {})} | custom-call | bytes 7340032 | tf_op jit(solution)/shard_map/pallas_call | solution.py:655
  56.8 2.9 %copy-done.2 = bf16[3584,1024]{1,0:T(8,128)(2,1)} copy-done((bf16[3584,1024]{1,0:T(8,128)(2,1)}, bf16[3584,1024]{1,0:T(8,128)(2,1)S(1)}, u32[]{:S(2)}) %copy-start.2) | copy-done | bytes 7340056
  59.8 1.6 %collective-permute-start.7 = (bf16[4,4,3712]{2,1,0:T(4,128)(2,1)S(1)}, bf16[4,4,3712]{2,1,0:T(4,128)(2,1)S(1)}, u32[]{:S(2)}, u32[]{:S(2)}) collective-permute-start(bf16[4,4,3712]{2,1,0:T(4,128)(2,1)S(1)} %shard_map.201.refs_0_), channel_id=1, source_target_pairs={{0,16},{1,3},{2,18},{3,1},{4,20},{5,7},{6,22},{7,5},{8,24},{9,11},... | collective-permute-start | bytes 356360 | tf_op jit(solution)/shard_map/ppermute | solution.py:563
  62.5 3.3 %collective-permute-done.7.passed = bf16[4,4,3712]{2,1,0:T(4,128)(2,1)S(1)} collective-permute-done((bf16[4,4,3712]{2,1,0:T(4,128)(2,1)S(1)}, bf16[4,4,3712]{2,1,0:T(4,128)(2,1)S(1)}, u32[]{:S(2)}, u32[]{:S(2)}) %collective-permute-start.7) | collective-permute-done | bytes 118816 | tf_op jit(solution)/shard_map/ppermute | solution.py:563
  66.4 3.1 %copy-done.3 = bf16[3584,1024]{1,0:T(8,128)(2,1)S(1)} copy-done((bf16[3584,1024]{1,0:T(8,128)(2,1)S(1)}, bf16[3584,1024]{1,0:T(8,128)(2,1)}, u32[]{:S(2)}) %copy-start.3) | copy-done | bytes 7340056
  69.5 3.2 %shard_map.202 = (bf16[4,4,3712]{2,1,0:T(4,128)(2,1)S(1)}, bf16[3584,1024]{1,0:T(8,128)(2,1)S(1)}, bf16[1024,3584]{1,0:T(8,128)(2,1)S(1)}, bf16[3584,1024]{1,0:T(8,128)(2,1)S(1)}) custom-call(bf16[4,4,3712]{2,1,0:T(4,128)(2,1)S(1)} %collective-permute-done.7.passed, bf16[3584,1024]{1,0:T(8,128)(2,1)S(1)} %copy-done.3, ...), custom_call_target="tpu_custom_call", output_to_operand_aliasing={{1}: (1, {}), {2}: (2, {})} | custom-call | bytes 7340032 | tf_op jit(solution)/shard_map/pallas_call | solution.py:655
  72.7 2.9 %copy-done.4 = bf16[3584,1024]{1,0:T(8,128)(2,1)} copy-done((bf16[3584,1024]{1,0:T(8,128)(2,1)}, bf16[3584,1024]{1,0:T(8,128)(2,1)S(1)}, u32[]{:S(2)}) %copy-start.4) | copy-done | bytes 7340056
  77.6 3.1 %copy-done.5 = bf16[3584,1024]{1,0:T(8,128)(2,1)S(1)} copy-done((bf16[3584,1024]{1,0:T(8,128)(2,1)S(1)}, bf16[3584,1024]{1,0:T(8,128)(2,1)}, u32[]{:S(2)}) %copy-start.5) | copy-done | bytes 7340056
  80.7 3.8 %shard_map.203 = (f32[64,3584]{1,0:T(8,128)S(1)}, bf16[64,3584]{1,0:T(8,128)(2,1)S(1)}) custom-call(bf16[4,4,3712]{2,1,0:T(4,128)(2,1)S(1)} %shard_map.201.refs_0_, bf16[4,4,3712]{2,1,0:T(4,128)(2,1)S(1)} %get-tuple-element.42.refs_1_, bf16[4,4,3712]{2,1,0:T(4,128)(2,1)S(1)} %collective-permute-done.8.refs_2_, ...), custom_call_target="tpu_custom_call" | custom-call | flops 2818572288 | bytes 22020096 | tf_op jit(solution)/shard_map/pallas_call | solution.py:48
  88.0 4.6 %collective-permute-done.15.got = bf16[32,3584]{1,0:T(8,128)(2,1)S(1)} collective-permute-done((bf16[32,3584]{1,0:T(8,128)(2,1)S(1)}, bf16[32,3584]{1,0:T(8,128)(2,1)S(1)}, u32[]{:S(2)}, u32[]{:S(2)}) %collective-permute-start.15) | collective-permute-done | bytes 229408 | tf_op jit(solution)/shard_map/ppermute | solution.py:563
  92.6 1.6 %collective-permute-start.16 = (bf16[16,3584]{1,0:T(8,128)(2,1)S(1)}, bf16[16,3584]{1,0:T(8,128)(2,1)S(1)}, u32[]{:S(2)}, u32[]{:S(2)}) collective-permute-start(bf16[16,3584]{1,0:T(8,128)(2,1)S(1)} %get-tuple-element.51), channel_id=1, source_target_pairs={{0,16},{1,3},{2,18},{3,1},{4,20},{5,7},{6,22},{7,5},{8,24},{9,11},... | collective-permute-start | bytes 344072 | tf_op jit(solution)/shard_map/ppermute | solution.py:563
  94.2 3.3 %collective-permute-done.16.got = bf16[16,3584]{1,0:T(8,128)(2,1)S(1)} collective-permute-done((bf16[16,3584]{1,0:T(8,128)(2,1)S(1)}, bf16[16,3584]{1,0:T(8,128)(2,1)S(1)}, u32[]{:S(2)}, u32[]{:S(2)}) %collective-permute-start.16) | collective-permute-done | bytes 114720 | tf_op jit(solution)/shard_map/ppermute | solution.py:563
  99.1 2.9 %collective-permute-start.19 = (bf16[4,3584]{1,0:T(4,128)(2,1)S(1)}, bf16[4,3584]{1,0:T(4,128)(2,1)S(1)}, u32[]{:S(2)}, u32[]{:S(2)}) collective-permute-start(bf16[4,3584]{1,0:T(4,128)(2,1)S(1)} %get-tuple-element.55), channel_id=1, source_target_pairs={{0,12},{1,13},{2,14},{3,15},{4,8},{5,9},{6,10},{7,11},{8,4},{9,5},... | collective-permute-start | bytes 86024 | tf_op jit(solution)/shard_map/ppermute | solution.py:563
  102.4 2.3 %collective-permute-done.19.refs_3_ = bf16[4,3584]{1,0:T(4,128)(2,1)S(1)} collective-permute-done((bf16[4,3584]{1,0:T(4,128)(2,1)S(1)}, bf16[4,3584]{1,0:T(4,128)(2,1)S(1)}, u32[]{:S(2)}, u32[]{:S(2)}) %collective-permute-start.19) | collective-permute-done | bytes 28704 | tf_op jit(solution)/shard_map/ppermute | solution.py:563
  (59 shorter events, 16.4 us)
Async XLA Ops:
  3.3 10.5 %collective-permute-start = (bf16[4,64,512]{2,1,0:T(8,128)(2,1)}, bf16[4,64,512]{2,1,0:T(8,128)(2,1)S(1)}, u32[]{:S(2)}, u32[]{:S(2)}) collective-permute-start(bf16[4,64,512]{2,1,0:T(8,128)(2,1)} %get-tuple-element.29), channel_id=1, source_target_pairs={{0,16},{1,17},{2,18},{3,19},{4,20},{5,21},{6,22},{7,23},{8,24},{9,... | collective-permute-start | bytes 786440 | tf_op jit(solution)/shard_map/ppermute | solution.py:563
  6.3 7.5 %collective-permute-start.1 = (bf16[8,2176]{1,0:T(8,128)(2,1)}, bf16[8,2176]{1,0:T(8,128)(2,1)S(1)}, u32[]{:S(2)}, u32[]{:S(2)}) collective-permute-start(bf16[8,2176]{1,0:T(8,128)(2,1)} %get-tuple-element.30), channel_id=1, source_target_pairs={{0,16},{1,17},{2,18},{3,19},{4,20},{5,21},{6,22},{7,23},{8,24},{9,... | collective-permute-start | bytes 104456 | tf_op jit(solution)/shard_map/ppermute | solution.py:563
  6.3 39.1 %copy-start.10 = (bf16[4,3584]{1,0:T(4,128)(2,1)S(1)}, bf16[4,3584]{1,0:T(4,128)(2,1)}, u32[]{:S(2)}) copy-start(bf16[4,3584]{1,0:T(4,128)(2,1)} %residual.1) | copy-start | bytes 86020
  6.3 39.1 %copy-start.11 = (f32[3584]{0:T(1024)S(1)}, f32[3584]{0:T(1024)}, u32[]{:S(2)}) copy-start(f32[3584]{0:T(1024)} %gain.1) | copy-start | bytes 43012
  6.3 39.1 %copy-start.12 = (s32[4,8]{1,0:T(4,128)S(1)}, s32[4,8]{1,0:T(4,128)}, u32[]{:S(2)}) copy-start(s32[4,8]{1,0:T(4,128)} %routes.1) | copy-start | bytes 388
  16.0 14.2 %collective-permute-start.3 = (bf16[256,3584]{1,0:T(8,128)(2,1)S(1)}, bf16[256,3584]{1,0:T(8,128)(2,1)}, u32[]{:S(2)}, u32[]{:S(2)}) collective-permute-start(bf16[256,3584]{1,0:T(8,128)(2,1)S(1)} %copy-done.7), channel_id=1, source_target_pairs={{0,1},{1,0},{2,3},{3,2},{4,5},{5,4},{6,7},{7,6},{8,9},{9,8},{10,11... | collective-permute-start | bytes 5505032 | tf_op jit(solution)/shard_map/ppermute | solution.py:563
  16.0 14.1 %collective-permute-start.2 = (bf16[2,512,128]{2,1,0:T(8,128)(2,1)S(1)}, bf16[2,512,128]{2,1,0:T(8,128)(2,1)S(1)}, u32[]{:S(2)}, u32[]{:S(2)}) collective-permute-start(bf16[2,512,128]{2,1,0:T(8,128)(2,1)S(1)} %copy-done.8), channel_id=1, source_target_pairs={{0,1},{1,0},{2,3},{3,2},{4,5},{5,4},{6,7},{7,6},{8,9},{9,8},{10,11... | collective-permute-start | bytes 786440 | tf_op jit(solution)/shard_map/ppermute | solution.py:563
  16.5 13.6 %all-to-all-start = ((bf16[8,16,512]{2,1,0:T(8,128)(2,1)}), bf16[8,16,512]{2,1,0:T(8,128)(2,1)S(1)}, u32[]{:S(2)}, u32[]{:S(2)}) async-start(bf16[8,16,512]{2,1,0:T(8,128)(2,1)} %shard_map.196.refs_1_), calls=%async_computation | async-start | bytes 262144 | tf_op jit(solution)/shard_map/all_to_all | solution.py:566
  46.2 13.6 %collective-permute-start.4 = (bf16[1,4,3712]{2,1,0:T(4,128)(2,1)S(1)}, bf16[1,4,3712]{2,1,0:T(4,128)(2,1)S(1)}, u32[]{:S(2)}, u32[]{:S(2)}) collective-permute-start(bf16[1,4,3712]{2,1,0:T(4,128)(2,1)S(1)} %get-tuple-element.37.passed), channel_id=1, source_target_pairs={{0,4},{1,5},{2,6},{3,7},{4,0},{5,1},{6,2},{7,3},{8,12},{9,13},{10,... | collective-permute-start | bytes 89096 | tf_op jit(solution)/shard_map/ppermute | solution.py:563
  47.1 12.7 %collective-permute-start.5 = (bf16[1,4,3712]{2,1,0:T(4,128)(2,1)S(1)}, bf16[1,4,3712]{2,1,0:T(4,128)(2,1)S(1)}, u32[]{:S(2)}, u32[]{:S(2)}) collective-permute-start(bf16[1,4,3712]{2,1,0:T(4,128)(2,1)S(1)} %get-tuple-element.37.passed), channel_id=1, source_target_pairs={{0,8},{1,9},{2,10},{3,11},{4,12},{5,13},{6,14},{7,15},{8,0},{9,1},... | collective-permute-start | bytes 89096 | tf_op jit(solution)/shard_map/ppermute | solution.py:563
  47.7 12.1 %collective-permute-start.6 = (bf16[1,4,3712]{2,1,0:T(4,128)(2,1)S(1)}, bf16[1,4,3712]{2,1,0:T(4,128)(2,1)S(1)}, u32[]{:S(2)}, u32[]{:S(2)}) collective-permute-start(bf16[1,4,3712]{2,1,0:T(4,128)(2,1)S(1)} %get-tuple-element.37.passed), channel_id=1, source_target_pairs={{0,12},{1,13},{2,14},{3,15},{4,8},{5,9},{6,10},{7,11},{8,4},{9,5},... | collective-permute-start | bytes 89096 | tf_op jit(solution)/shard_map/ppermute | solution.py:563
  59.8 6.0 %collective-permute-start.7 = (bf16[4,4,3712]{2,1,0:T(4,128)(2,1)S(1)}, bf16[4,4,3712]{2,1,0:T(4,128)(2,1)S(1)}, u32[]{:S(2)}, u32[]{:S(2)}) collective-permute-start(bf16[4,4,3712]{2,1,0:T(4,128)(2,1)S(1)} %shard_map.201.refs_0_), channel_id=1, source_target_pairs={{0,16},{1,3},{2,18},{3,1},{4,20},{5,7},{6,22},{7,5},{8,24},{9,11},... | collective-permute-start | bytes 356360 | tf_op jit(solution)/shard_map/ppermute | solution.py:563
  61.3 14.7 %collective-permute-start.8 = (bf16[4,4,3712]{2,1,0:T(4,128)(2,1)S(1)}, bf16[4,4,3712]{2,1,0:T(4,128)(2,1)S(1)}, u32[]{:S(2)}, u32[]{:S(2)}) collective-permute-start(bf16[4,4,3712]{2,1,0:T(4,128)(2,1)S(1)} %shard_map.201.refs_0_), channel_id=1, source_target_pairs={{0,2},{1,17},{2,0},{3,19},{4,6},{5,21},{6,4},{7,23},{8,10},{9,25},... | collective-permute-start | bytes 356360 | tf_op jit(solution)/shard_map/ppermute | solution.py:563
  65.8 10.3 %collective-permute-start.9 = (bf16[4,4,3712]{2,1,0:T(4,128)(2,1)S(1)}, bf16[4,4,3712]{2,1,0:T(4,128)(2,1)S(1)}, u32[]{:S(2)}, u32[]{:S(2)}) collective-permute-start(bf16[4,4,3712]{2,1,0:T(4,128)(2,1)S(1)} %collective-permute-done.7.passed), channel_id=1, source_target_pairs={{0,2},{1,17},{2,0},{3,19},{4,6},{5,21},{6,4},{7,23},{8,10},{9,25},... | collective-permute-start | bytes 356360 | tf_op jit(solution)/shard_map/ppermute | solution.py:563
  66.4 10.2 %collective-permute-start.10 = (bf16[4,4,3712]{2,1,0:T(4,128)(2,1)S(1)}, bf16[4,4,3712]{2,1,0:T(4,128)(2,1)S(1)}, u32[]{:S(2)}, u32[]{:S(2)}) collective-permute-start(bf16[4,4,3712]{2,1,0:T(4,128)(2,1)S(1)} %shard_map.201.refs_0_), channel_id=1, source_target_pairs={{0,1},{1,0},{2,3},{3,2},{4,5},{5,4},{6,7},{7,6},{8,9},{9,8},{10,11... | collective-permute-start | bytes 356360 | tf_op jit(solution)/shard_map/ppermute | solution.py:563
  75.6 1.5 %collective-permute-start.11 = (bf16[4,4,3712]{2,1,0:T(4,128)(2,1)S(1)}, bf16[4,4,3712]{2,1,0:T(4,128)(2,1)S(1)}, u32[]{:S(2)}, u32[]{:S(2)}) collective-permute-start(bf16[4,4,3712]{2,1,0:T(4,128)(2,1)S(1)} %get-tuple-element.42.refs_1_), channel_id=1, source_target_pairs={{0,1},{1,0},{2,3},{3,2},{4,5},{5,4},{6,7},{7,6},{8,9},{9,8},{10,11... | collective-permute-start | bytes 356360 | tf_op jit(solution)/shard_map/ppermute | solution.py:563
  76.1 1.3 %collective-permute-start.12 = (bf16[4,4,3712]{2,1,0:T(4,128)(2,1)S(1)}, bf16[4,4,3712]{2,1,0:T(4,128)(2,1)S(1)}, u32[]{:S(2)}, u32[]{:S(2)}) collective-permute-start(bf16[4,4,3712]{2,1,0:T(4,128)(2,1)S(1)} %collective-permute-done.8.refs_2_), channel_id=1, source_target_pairs={{0,1},{1,0},{2,3},{3,2},{4,5},{5,4},{6,7},{7,6},{8,9},{9,8},{10,11... | collective-permute-start | bytes 356360 | tf_op jit(solution)/shard_map/ppermute | solution.py:563
  76.1 1.5 %collective-permute-start.13 = (bf16[4,4,3712]{2,1,0:T(4,128)(2,1)S(1)}, bf16[4,4,3712]{2,1,0:T(4,128)(2,1)S(1)}, u32[]{:S(2)}, u32[]{:S(2)}) collective-permute-start(bf16[4,4,3712]{2,1,0:T(4,128)(2,1)S(1)} %collective-permute-done.9.refs_3_), channel_id=1, source_target_pairs={{0,1},{1,0},{2,3},{3,2},{4,5},{5,4},{6,7},{7,6},{8,9},{9,8},{10,11... | collective-permute-start | bytes 356360 | tf_op jit(solution)/shard_map/ppermute | solution.py:563
  84.5 1.9 %collective-permute-start.14 = (bf16[64,3584]{1,0:T(8,128)(2,1)S(1)}, bf16[64,3584]{1,0:T(8,128)(2,1)S(1)}, u32[]{:S(2)}, u32[]{:S(2)}) collective-permute-start(bf16[64,3584]{1,0:T(8,128)(2,1)S(1)} %get-tuple-element.47), channel_id=1, source_target_pairs={{0,1},{1,0},{2,3},{3,2},{4,5},{5,4},{6,7},{7,6},{8,9},{9,8},{10,11... | collective-permute-start | bytes 1376264 | tf_op jit(solution)/shard_map/ppermute | solution.py:563
  86.5 6.1 %collective-permute-start.15 = (bf16[32,3584]{1,0:T(8,128)(2,1)S(1)}, bf16[32,3584]{1,0:T(8,128)(2,1)S(1)}, u32[]{:S(2)}, u32[]{:S(2)}) collective-permute-start(bf16[32,3584]{1,0:T(8,128)(2,1)S(1)} %get-tuple-element.49), channel_id=1, source_target_pairs={{0,2},{1,17},{2,0},{3,19},{4,6},{5,21},{6,4},{7,23},{8,10},{9,25},... | collective-permute-start | bytes 688136 | tf_op jit(solution)/shard_map/ppermute | solution.py:563
  92.6 4.9 %collective-permute-start.16 = (bf16[16,3584]{1,0:T(8,128)(2,1)S(1)}, bf16[16,3584]{1,0:T(8,128)(2,1)S(1)}, u32[]{:S(2)}, u32[]{:S(2)}) collective-permute-start(bf16[16,3584]{1,0:T(8,128)(2,1)S(1)} %get-tuple-element.51), channel_id=1, source_target_pairs={{0,16},{1,3},{2,18},{3,1},{4,20},{5,7},{6,22},{7,5},{8,24},{9,11},... | collective-permute-start | bytes 344072 | tf_op jit(solution)/shard_map/ppermute | solution.py:563
  97.5 4.5 %collective-permute-start.17 = (bf16[4,3584]{1,0:T(4,128)(2,1)S(1)}, bf16[4,3584]{1,0:T(4,128)(2,1)S(1)}, u32[]{:S(2)}, u32[]{:S(2)}) collective-permute-start(bf16[4,3584]{1,0:T(4,128)(2,1)S(1)} %get-tuple-element.53), channel_id=1, source_target_pairs={{0,4},{1,5},{2,6},{3,7},{4,0},{5,1},{6,2},{7,3},{8,12},{9,13},{10,... | collective-permute-start | bytes 86024 | tf_op jit(solution)/shard_map/ppermute | solution.py:563
  97.6 4.8 %collective-permute-start.18 = (bf16[4,3584]{1,0:T(4,128)(2,1)S(1)}, bf16[4,3584]{1,0:T(4,128)(2,1)S(1)}, u32[]{:S(2)}, u32[]{:S(2)}) collective-permute-start(bf16[4,3584]{1,0:T(4,128)(2,1)S(1)} %get-tuple-element.54), channel_id=1, source_target_pairs={{0,8},{1,9},{2,10},{3,11},{4,12},{5,13},{6,14},{7,15},{8,0},{9,1},... | collective-permute-start | bytes 86024 | tf_op jit(solution)/shard_map/ppermute | solution.py:563
  99.1 5.7 %collective-permute-start.19 = (bf16[4,3584]{1,0:T(4,128)(2,1)S(1)}, bf16[4,3584]{1,0:T(4,128)(2,1)S(1)}, u32[]{:S(2)}, u32[]{:S(2)}) collective-permute-start(bf16[4,3584]{1,0:T(4,128)(2,1)S(1)} %get-tuple-element.55), channel_id=1, source_target_pairs={{0,12},{1,13},{2,14},{3,15},{4,8},{5,9},{6,10},{7,11},{8,4},{9,5},... | collective-permute-start | bytes 86024 | tf_op jit(solution)/shard_map/ppermute | solution.py:563
  (10 other events, 58.0 us)

commit v7 on v5

--- a/solution.py
+++ b/solution.py
@@ -25,7 +25,8 @@
 FAR = ("low", "far")
 CHIP = ("far", "side")
 ROPE_ROWS = 16
-LOAD_MIB = 40
+LOAD_MIB = 41
+UP_MIB = 34
 SIDE_MIB = 28
 EXPERT_MIB = 16
 
@@ -696,12 +697,12 @@
     else:
         own_rows, down_here = load(own_rows, (w_down,), LOAD_MIB)
         piece = deal(own_rows, FAR)
-    pieces = [piece, swap(piece, top_bit, side_bit)]
-    pieces = pieces + [swap(p, side_bit, top_bit) for p in pieces]
-    side_piece, down_here, gate_here, up_here = load(
-        pieces[1], (w_gate, w_up), SIDE_MIB, (down_here,)
-    )
-    pieces = [piece, side_piece] + pieces[2:]
+    side_piece = swap(piece, top_bit, side_bit)
+    piece, down_here, up_here = load(piece, (w_up,), UP_MIB, (down_here,))
+    pieces = [piece, side_piece, swap(piece, side_bit, top_bit), swap(side_piece, side_bit, top_bit)]
+    pieces[1], down_here, up_here, gate_here = load(
+        side_piece, (w_gate,), SIDE_MIB, (down_here, up_here)
+    )
     pieces = pieces + [swap(p, 1) for p in pieces]
 
     all_rows = total_devices * tokens

time: 90.6 us -> 88.8 us (0.980)
  waiting for transfers between devices: 18.3 us -> 15.2 us
  Pallas kernels: 25.5 us -> 26.6 us
    ppermute x20, waiting for transfers between devices: 18.3 us -> 15.2 us  [swap(): return lax.ppermute(x, ROWS, pairs)]
    pallas_call x2 -> x3, Pallas kernels: 8.53 us -> 9.54 us  [load(): pl.pallas_call(functools.partial(load_kernel, len(sources), len(held)), o...]
  transfers between devices with their start and end apart: 20 -> 20, of which waited for: 9 -> 8; matrix products, arithmetic and copies ran while one was open for 0% -> 0% of each run, Pallas kernels for 18% -> 19%
where the time goes in v7:
time: 88.8 us; the launch traced here: 88.5 us
  Pallas kernels  26.6 us (30%)
  blocking collectives  24 us (27%)
  starting transfers between devices  20.7 us (23%)
  waiting for transfers between devices  15.2 us (17%)
  local copies, waits for them, and re-layouts  1.11 us (1%)
    all_to_all x2, blocking collectives, deal(): return lax.all_to_all(x, names, split_axis=0, concat_axis=0, tiled=True)  24 us
    ppermute x20, starting transfers between devices, swap(): return lax.ppermute(x, ROWS, pairs)  20.7 us
    pallas_call x11, Pallas kernels, call(): pl.pallas_call(kernel, out_shape=outs, in_specs=in_specs or [VMEM] * len(...  17 us
    ppermute x20, waiting for transfers between devices, swap(): return lax.ppermute(x, ROWS, pairs)  15.2 us
    pallas_call x3, Pallas kernels, load(): pl.pallas_call(functools.partial(load_kernel, len(sources), len(held)), o...  9.54 us
  transfers between devices with their start and end apart: 20, of which 8 were waited for; matrix products, arithmetic and copies ran while one was open for 0% of the time, Pallas kernels for 19%

profile of v7, /device:TPU:0, one launch (start us, length us, event | category | flops | bytes accessed | tf_op | source)
XLA Modules:
  0.0 88.5 jit_solution(17227397648271823632)
XLA Ops:
  0.7 2.6 %shard_map.194 = (bf16[4,64,512]{2,1,0:T(8,128)(2,1)}, bf16[8,2176]{1,0:T(8,128)(2,1)}, f32[48]{0:T(128)}) custom-call(s32[1,2,4]{2,1,0:T(2,128)} %move_hbm.3, bf16[48]{0:T(256)(128)(2,1)} %scale_hbm.1, bf16[48,64,512]{2,1,0:T(8,128)(2,1)} %lat_hbm.1, bf16[48,4096]{1,0:T(8,128)(2,1)} %rope_hbm.3), custom_call_target="tpu_custom_call" | custom-call | tf_op jit(solution)/shard_map/pallas_call | solution.py:48
  3.3 3.0 %collective-permute-start = (bf16[4,64,512]{2,1,0:T(8,128)(2,1)}, bf16[4,64,512]{2,1,0:T(8,128)(2,1)S(1)}, u32[]{:S(2)}, u32[]{:S(2)}) collective-permute-start(bf16[4,64,512]{2,1,0:T(8,128)(2,1)} %get-tuple-element.29), channel_id=1, source_target_pairs={{0,16},{1,17},{2,18},{3,19},{4,20},{5,21},{6,22},{7,23},{8,24},{9,... | collective-permute-start | bytes 786440 | tf_op jit(solution)/shard_map/ppermute | solution.py:563
  6.4 7.4 %shard_map.195.refs_2_ = f32[264,640]{1,0:T(8,128)} custom-call(f32[48]{0:T(128)} %get-tuple-element.31.scale_hbm, s32[2,32]{1,0:T(2,128)} %table_hbm.1, s32[2]{0:T(128)} %lengths_hbm.1, s32[1,2,4]{2,1,0:T(2,128)} %move_hbm.3, bf16[48,64,512]{2,1,0:T(8,128)(2,1)} %lat_hbm.1, bf16[48,4096]{1,0:T(8,128)(2,1)} %rope_hbm.3, bf16[2,2,32,512]{3,2,1,0:T(8,128)(2,1)} %q_hbm.1, ...), custom_call_target="tpu_custom_call" | custom-call | flops 905969664 | bytes 4194304 | tf_op jit(solution)/shard_map/pallas_call | solution.py:48
  13.8 1.1 %copy-done = f32[264,640]{1,0:T(8,128)S(1)} copy-done((f32[264,640]{1,0:T(8,128)S(1)}, f32[264,640]{1,0:T(8,128)}, u32[]{:S(2)}) %copy-start) | copy-done | bytes 675864
  16.0 13.4 %all_to_all.10.blocks = bf16[8,16,512]{2,1,0:T(8,128)(2,1)S(1)} all-to-all(bf16[8,16,512]{2,1,0:T(8,128)(2,1)S(1)} %shard_map.196), channel_id=1, replica_groups=mesh['top'=2,'low'=1,'far'=4,'side'=2,'core'=2] {'far','side'}, dimensions={0} | all-to-all | bytes 262144 | tf_op jit(solution)/shard_map/all_to_all | solution.py:566
  29.4 1.1 %shard_map.197 = bf16[8,4,3584]{2,1,0:T(4,128)(2,1)S(1)} custom-call(bf16[8,16,512]{2,1,0:T(8,128)(2,1)S(1)} %all_to_all.10.blocks, bf16[2,512,128]{2,1,0:T(8,128)(2,1)S(1)} %copy-done.2, bf16[2,512,128]{2,1,0:T(8,128)(2,1)S(1)} %collective-permute-done.2.other_uv, bf16[256,3584]{1,0:T(8,128)(2,1)S(1)} %copy-done.1, ...), custom_call_target="tpu_custom_call" | custom-call | flops 117440512 | bytes 8388608 | tf_op jit(solution)/shard_map/pallas_call | solution.py:48
  30.6 10.6 %all_to_all.11.got = bf16[8,4,3584]{2,1,0:T(4,128)(2,1)S(1)} all-to-all(bf16[8,4,3584]{2,1,0:T(4,128)(2,1)S(1)} %shard_map.197), channel_id=1, replica_groups=mesh['top'=2,'low'=1,'far'=4,'side'=2,'core'=2] {'far','side'}, dimensions={0} | all-to-all | bytes 458752 | tf_op jit(solution)/shard_map/all_to_all | solution.py:566
  41.9 0.9 %collective-permute-start.4 = (bf16[1,4,3712]{2,1,0:T(4,128)(2,1)S(1)}, bf16[1,4,3712]{2,1,0:T(4,128)(2,1)S(1)}, u32[]{:S(2)}, u32[]{:S(2)}) collective-permute-start(bf16[1,4,3712]{2,1,0:T(4,128)(2,1)S(1)} %get-tuple-element.36.passed), channel_id=1, source_target_pairs={{0,4},{1,5},{2,6},{3,7},{4,0},{5,1},{6,2},{7,3},{8,12},{9,13},{10,... | collective-permute-start | bytes 89096 | tf_op jit(solution)/shard_map/ppermute | solution.py:563
  43.4 2.9 %collective-permute-start.6 = (bf16[1,4,3712]{2,1,0:T(4,128)(2,1)S(1)}, bf16[1,4,3712]{2,1,0:T(4,128)(2,1)S(1)}, u32[]{:S(2)}, u32[]{:S(2)}) collective-permute-start(bf16[1,4,3712]{2,1,0:T(4,128)(2,1)S(1)} %get-tuple-element.36.passed), channel_id=1, source_target_pairs={{0,12},{1,13},{2,14},{3,15},{4,8},{5,9},{6,10},{7,11},{8,4},{9,5},... | collective-permute-start | bytes 89096 | tf_op jit(solution)/shard_map/ppermute | solution.py:563
  46.3 3.2 %shard_map.199 = (bf16[1,4,3712]{2,1,0:T(4,128)(2,1)S(1)}, bf16[1024,3584]{1,0:T(8,128)(2,1)S(1)}) custom-call(bf16[1,4,3712]{2,1,0:T(4,128)(2,1)S(1)} %get-tuple-element.36.passed, bf16[1,1024,3584]{2,1,0:T(8,128)(2,1)} %refs_0_.1), custom_call_target="tpu_custom_call" | custom-call | bytes 7340032 | tf_op jit(solution)/shard_map/pallas_call | solution.py:676
  49.6 1.6 %collective-permute-start.7 = (bf16[4,4,3712]{2,1,0:T(4,128)(2,1)S(1)}, bf16[4,4,3712]{2,1,0:T(4,128)(2,1)S(1)}, u32[]{:S(2)}, u32[]{:S(2)}) collective-permute-start(bf16[4,4,3712]{2,1,0:T(4,128)(2,1)S(1)} %shard_map.200.passed), channel_id=1, source_target_pairs={{0,16},{1,3},{2,18},{3,1},{4,20},{5,7},{6,22},{7,5},{8,24},{9,11},... | collective-permute-start | bytes 356360 | tf_op jit(solution)/shard_map/ppermute | solution.py:563
  51.1 3.2 %shard_map.201 = (bf16[4,4,3712]{2,1,0:T(4,128)(2,1)S(1)}, bf16[1024,3584]{1,0:T(8,128)(2,1)S(1)}, bf16[3584,1024]{1,0:T(8,128)(2,1)S(1)}) custom-call(bf16[4,4,3712]{2,1,0:T(4,128)(2,1)S(1)} %shard_map.200.passed, bf16[1024,3584]{1,0:T(8,128)(2,1)S(1)} %get-tuple-element.38.refs_0_, bf16[1,3584,1024]{2,1,0:T(8,128)(2,1)} %refs_1_.1), custom_call_target="tpu_custom_call", output_to_operand_aliasing={{1}: (1, {})} | custom-call | bytes 7340032 | tf_op jit(solution)/shard_map/pallas_call | solution.py:676
  54.3 1.4 %collective-permute-start.8 = (bf16[4,4,3712]{2,1,0:T(4,128)(2,1)S(1)}, bf16[4,4,3712]{2,1,0:T(4,128)(2,1)S(1)}, u32[]{:S(2)}, u32[]{:S(2)}) collective-permute-start(bf16[4,4,3712]{2,1,0:T(4,128)(2,1)S(1)} %get-tuple-element.39.refs_0_), channel_id=1, source_target_pairs={{0,2},{1,17},{2,0},{3,19},{4,6},{5,21},{6,4},{7,23},{8,10},{9,25},... | collective-permute-start | bytes 356360 | tf_op jit(solution)/shard_map/ppermute | solution.py:563
  55.6 1.3 %collective-permute-start.9 = (bf16[4,4,3712]{2,1,0:T(4,128)(2,1)S(1)}, bf16[4,4,3712]{2,1,0:T(4,128)(2,1)S(1)}, u32[]{:S(2)}, u32[]{:S(2)}) collective-permute-start(bf16[4,4,3712]{2,1,0:T(4,128)(2,1)S(1)} %collective-permute-done.7.passed), channel_id=1, source_target_pairs={{0,2},{1,17},{2,0},{3,19},{4,6},{5,21},{6,4},{7,23},{8,10},{9,25},... | collective-permute-start | bytes 356360 | tf_op jit(solution)/shard_map/ppermute | solution.py:563
  56.9 3.2 %shard_map.202 = (bf16[4,4,3712]{2,1,0:T(4,128)(2,1)S(1)}, bf16[1024,3584]{1,0:T(8,128)(2,1)S(1)}, bf16[3584,1024]{1,0:T(8,128)(2,1)S(1)}, bf16[3584,1024]{1,0:T(8,128)(2,1)S(1)}) custom-call(bf16[4,4,3712]{2,1,0:T(4,128)(2,1)S(1)} %collective-permute-done.7.passed, ...), custom_call_target="tpu_custom_call", output_to_operand_aliasing={{1}: (1, {}), {2}: (2, {})} | custom-call | bytes 7340032 | tf_op jit(solution)/shard_map/pallas_call | solution.py:676
  62.2 3.9 %shard_map.203 = (f32[64,3584]{1,0:T(8,128)S(1)}, bf16[64,3584]{1,0:T(8,128)(2,1)S(1)}) custom-call(bf16[4,4,3712]{2,1,0:T(4,128)(2,1)S(1)} %get-tuple-element.39.refs_0_, bf16[4,4,3712]{2,1,0:T(4,128)(2,1)S(1)} %get-tuple-element.42.refs_1_, bf16[4,4,3712]{2,1,0:T(4,128)(2,1)S(1)} %collective-permute-done.8.refs_2_, ...), custom_call_target="tpu_custom_call" | custom-call | flops 2818572288 | bytes 22020096 | tf_op jit(solution)/shard_map/pallas_call | solution.py:48
  66.5 1.5 %collective-permute-done.14.got = bf16[64,3584]{1,0:T(8,128)(2,1)S(1)} collective-permute-done((bf16[64,3584]{1,0:T(8,128)(2,1)S(1)}, bf16[64,3584]{1,0:T(8,128)(2,1)S(1)}, u32[]{:S(2)}, u32[]{:S(2)}) %collective-permute-start.14) | collective-permute-done | bytes 458784 | tf_op jit(solution)/shard_map/ppermute | solution.py:563
  68.1 0.9 %collective-permute-start.15 = (bf16[32,3584]{1,0:T(8,128)(2,1)S(1)}, bf16[32,3584]{1,0:T(8,128)(2,1)S(1)}, u32[]{:S(2)}, u32[]{:S(2)}) collective-permute-start(bf16[32,3584]{1,0:T(8,128)(2,1)S(1)} %get-tuple-element.49), channel_id=1, source_target_pairs={{0,2},{1,17},{2,0},{3,19},{4,6},{5,21},{6,4},{7,23},{8,10},{9,25},... | collective-permute-start | bytes 688136 | tf_op jit(solution)/shard_map/ppermute | solution.py:563
  69.0 5.1 %collective-permute-done.15.got = bf16[32,3584]{1,0:T(8,128)(2,1)S(1)} collective-permute-done((bf16[32,3584]{1,0:T(8,128)(2,1)S(1)}, bf16[32,3584]{1,0:T(8,128)(2,1)S(1)}, u32[]{:S(2)}, u32[]{:S(2)}) %collective-permute-start.15) | collective-permute-done | bytes 229408 | tf_op jit(solution)/shard_map/ppermute | solution.py:563
  74.2 1.6 %collective-permute-start.16 = (bf16[16,3584]{1,0:T(8,128)(2,1)S(1)}, bf16[16,3584]{1,0:T(8,128)(2,1)S(1)}, u32[]{:S(2)}, u32[]{:S(2)}) collective-permute-start(bf16[16,3584]{1,0:T(8,128)(2,1)S(1)} %get-tuple-element.51), channel_id=1, source_target_pairs={{0,16},{1,3},{2,18},{3,1},{4,20},{5,7},{6,22},{7,5},{8,24},{9,11},... | collective-permute-start | bytes 344072 | tf_op jit(solution)/shard_map/ppermute | solution.py:563
  75.8 3.3 %collective-permute-done.16.got = bf16[16,3584]{1,0:T(8,128)(2,1)S(1)} collective-permute-done((bf16[16,3584]{1,0:T(8,128)(2,1)S(1)}, bf16[16,3584]{1,0:T(8,128)(2,1)S(1)}, u32[]{:S(2)}, u32[]{:S(2)}) %collective-permute-start.16) | collective-permute-done | bytes 114720 | tf_op jit(solution)/shard_map/ppermute | solution.py:563
  79.2 3.0 %collective-permute-start.18 = (bf16[4,3584]{1,0:T(4,128)(2,1)S(1)}, bf16[4,3584]{1,0:T(4,128)(2,1)S(1)}, u32[]{:S(2)}, u32[]{:S(2)}) collective-permute-start(bf16[4,3584]{1,0:T(4,128)(2,1)S(1)} %get-tuple-element.54), channel_id=1, source_target_pairs={{0,8},{1,9},{2,10},{3,11},{4,12},{5,13},{6,14},{7,15},{8,0},{9,1},... | collective-permute-start | bytes 86024 | tf_op jit(solution)/shard_map/ppermute | solution.py:563
  82.2 1.4 %collective-permute-start.19 = (bf16[4,3584]{1,0:T(4,128)(2,1)S(1)}, bf16[4,3584]{1,0:T(4,128)(2,1)S(1)}, u32[]{:S(2)}, u32[]{:S(2)}) collective-permute-start(bf16[4,3584]{1,0:T(4,128)(2,1)S(1)} %get-tuple-element.55), channel_id=1, source_target_pairs={{0,12},{1,13},{2,14},{3,15},{4,8},{5,9},{6,10},{7,11},{8,4},{9,5},... | collective-permute-start | bytes 86024 | tf_op jit(solution)/shard_map/ppermute | solution.py:563
  84.0 3.8 %collective-permute-done.19.refs_3_ = bf16[4,3584]{1,0:T(4,128)(2,1)S(1)} collective-permute-done((bf16[4,3584]{1,0:T(4,128)(2,1)S(1)}, bf16[4,3584]{1,0:T(4,128)(2,1)S(1)}, u32[]{:S(2)}, u32[]{:S(2)}) %collective-permute-start.19) | collective-permute-done | bytes 28704 | tf_op jit(solution)/shard_map/ppermute | solution.py:563
  (46 shorter events, 6.4 us)
Async XLA Ops:
  0.6 14.9 %copy-start.2 = (bf16[2,512,128]{2,1,0:T(8,128)(2,1)S(1)}, bf16[2,512,128]{2,1,0:T(8,128)(2,1)}, u32[]{:S(2)}) copy-start(bf16[2,512,128]{2,1,0:T(8,128)(2,1)} %w_uv.1) | copy-start | bytes 786436
  0.7 40.6 %copy-start.4 = (bf16[4,3584]{1,0:T(4,128)(2,1)S(1)}, bf16[4,3584]{1,0:T(4,128)(2,1)}, u32[]{:S(2)}) copy-start(bf16[4,3584]{1,0:T(4,128)(2,1)} %residual.1) | copy-start | bytes 86020
  0.7 40.5 %copy-start.5 = (f32[3584]{0:T(1024)S(1)}, f32[3584]{0:T(1024)}, u32[]{:S(2)}) copy-start(f32[3584]{0:T(1024)} %gain.1) | copy-start | bytes 43012
  0.7 40.5 %copy-start.6 = (s32[4,8]{1,0:T(4,128)S(1)}, s32[4,8]{1,0:T(4,128)}, u32[]{:S(2)}) copy-start(s32[4,8]{1,0:T(4,128)} %routes.1) | copy-start | bytes 388
  3.3 10.5 %collective-permute-start = (bf16[4,64,512]{2,1,0:T(8,128)(2,1)}, bf16[4,64,512]{2,1,0:T(8,128)(2,1)S(1)}, u32[]{:S(2)}, u32[]{:S(2)}) collective-permute-start(bf16[4,64,512]{2,1,0:T(8,128)(2,1)} %get-tuple-element.29), channel_id=1, source_target_pairs={{0,16},{1,17},{2,18},{3,19},{4,20},{5,21},{6,22},{7,23},{8,24},{9,... | collective-permute-start | bytes 786440 | tf_op jit(solution)/shard_map/ppermute | solution.py:563
  6.3 7.4 %collective-permute-start.1 = (bf16[8,2176]{1,0:T(8,128)(2,1)}, bf16[8,2176]{1,0:T(8,128)(2,1)S(1)}, u32[]{:S(2)}, u32[]{:S(2)}) collective-permute-start(bf16[8,2176]{1,0:T(8,128)(2,1)} %get-tuple-element.30), channel_id=1, source_target_pairs={{0,16},{1,17},{2,18},{3,19},{4,20},{5,21},{6,22},{7,23},{8,24},{9,... | collective-permute-start | bytes 104456 | tf_op jit(solution)/shard_map/ppermute | solution.py:563
  15.4 14.0 %collective-permute-start.3 = (bf16[256,3584]{1,0:T(8,128)(2,1)S(1)}, bf16[256,3584]{1,0:T(8,128)(2,1)S(1)}, u32[]{:S(2)}, u32[]{:S(2)}) collective-permute-start(bf16[256,3584]{1,0:T(8,128)(2,1)S(1)} %copy-done.1), channel_id=1, source_target_pairs={{0,1},{1,0},{2,3},{3,2},{4,5},{5,4},{6,7},{7,6},{8,9},{9,8},{10,11... | collective-permute-start | bytes 5505032 | tf_op jit(solution)/shard_map/ppermute | solution.py:563
  15.5 13.9 %collective-permute-start.2 = (bf16[2,512,128]{2,1,0:T(8,128)(2,1)S(1)}, bf16[2,512,128]{2,1,0:T(8,128)(2,1)S(1)}, u32[]{:S(2)}, u32[]{:S(2)}) collective-permute-start(bf16[2,512,128]{2,1,0:T(8,128)(2,1)S(1)} %copy-done.2), channel_id=1, source_target_pairs={{0,1},{1,0},{2,3},{3,2},{4,5},{5,4},{6,7},{7,6},{8,9},{9,8},{10,11... | collective-permute-start | bytes 786440 | tf_op jit(solution)/shard_map/ppermute | solution.py:563
  41.9 7.6 %collective-permute-start.4 = (bf16[1,4,3712]{2,1,0:T(4,128)(2,1)S(1)}, bf16[1,4,3712]{2,1,0:T(4,128)(2,1)S(1)}, u32[]{:S(2)}, u32[]{:S(2)}) collective-permute-start(bf16[1,4,3712]{2,1,0:T(4,128)(2,1)S(1)} %get-tuple-element.36.passed), channel_id=1, source_target_pairs={{0,4},{1,5},{2,6},{3,7},{4,0},{5,1},{6,2},{7,3},{8,12},{9,13},{10,... | collective-permute-start | bytes 89096 | tf_op jit(solution)/shard_map/ppermute | solution.py:563
  42.8 6.7 %collective-permute-start.5 = (bf16[1,4,3712]{2,1,0:T(4,128)(2,1)S(1)}, bf16[1,4,3712]{2,1,0:T(4,128)(2,1)S(1)}, u32[]{:S(2)}, u32[]{:S(2)}) collective-permute-start(bf16[1,4,3712]{2,1,0:T(4,128)(2,1)S(1)} %get-tuple-element.36.passed), channel_id=1, source_target_pairs={{0,8},{1,9},{2,10},{3,11},{4,12},{5,13},{6,14},{7,15},{8,0},{9,1},... | collective-permute-start | bytes 89096 | tf_op jit(solution)/shard_map/ppermute | solution.py:563
  43.4 6.1 %collective-permute-start.6 = (bf16[1,4,3712]{2,1,0:T(4,128)(2,1)S(1)}, bf16[1,4,3712]{2,1,0:T(4,128)(2,1)S(1)}, u32[]{:S(2)}, u32[]{:S(2)}) collective-permute-start(bf16[1,4,3712]{2,1,0:T(4,128)(2,1)S(1)} %get-tuple-element.36.passed), channel_id=1, source_target_pairs={{0,12},{1,13},{2,14},{3,15},{4,8},{5,9},{6,10},{7,11},{8,4},{9,5},... | collective-permute-start | bytes 89096 | tf_op jit(solution)/shard_map/ppermute | solution.py:563
  49.6 6.1 %collective-permute-start.7 = (bf16[4,4,3712]{2,1,0:T(4,128)(2,1)S(1)}, bf16[4,4,3712]{2,1,0:T(4,128)(2,1)S(1)}, u32[]{:S(2)}, u32[]{:S(2)}) collective-permute-start(bf16[4,4,3712]{2,1,0:T(4,128)(2,1)S(1)} %shard_map.200.passed), channel_id=1, source_target_pairs={{0,16},{1,3},{2,18},{3,1},{4,20},{5,7},{6,22},{7,5},{8,24},{9,11},... | collective-permute-start | bytes 356360 | tf_op jit(solution)/shard_map/ppermute | solution.py:563
  54.3 6.4 %collective-permute-start.8 = (bf16[4,4,3712]{2,1,0:T(4,128)(2,1)S(1)}, bf16[4,4,3712]{2,1,0:T(4,128)(2,1)S(1)}, u32[]{:S(2)}, u32[]{:S(2)}) collective-permute-start(bf16[4,4,3712]{2,1,0:T(4,128)(2,1)S(1)} %get-tuple-element.39.refs_0_), channel_id=1, source_target_pairs={{0,2},{1,17},{2,0},{3,19},{4,6},{5,21},{6,4},{7,23},{8,10},{9,25},... | collective-permute-start | bytes 356360 | tf_op jit(solution)/shard_map/ppermute | solution.py:563
  55.6 5.2 %collective-permute-start.9 = (bf16[4,4,3712]{2,1,0:T(4,128)(2,1)S(1)}, bf16[4,4,3712]{2,1,0:T(4,128)(2,1)S(1)}, u32[]{:S(2)}, u32[]{:S(2)}) collective-permute-start(bf16[4,4,3712]{2,1,0:T(4,128)(2,1)S(1)} %collective-permute-done.7.passed), channel_id=1, source_target_pairs={{0,2},{1,17},{2,0},{3,19},{4,6},{5,21},{6,4},{7,23},{8,10},{9,25},... | collective-permute-start | bytes 356360 | tf_op jit(solution)/shard_map/ppermute | solution.py:563
  56.9 4.3 %collective-permute-start.10 = (bf16[4,4,3712]{2,1,0:T(4,128)(2,1)S(1)}, bf16[4,4,3712]{2,1,0:T(4,128)(2,1)S(1)}, u32[]{:S(2)}, u32[]{:S(2)}) collective-permute-start(bf16[4,4,3712]{2,1,0:T(4,128)(2,1)S(1)} %get-tuple-element.39.refs_0_), channel_id=1, source_target_pairs={{0,1},{1,0},{2,3},{3,2},{4,5},{5,4},{6,7},{7,6},{8,9},{9,8},{10,11... | collective-permute-start | bytes 356360 | tf_op jit(solution)/shard_map/ppermute | solution.py:563
  60.2 1.5 %collective-permute-start.11 = (bf16[4,4,3712]{2,1,0:T(4,128)(2,1)S(1)}, bf16[4,4,3712]{2,1,0:T(4,128)(2,1)S(1)}, u32[]{:S(2)}, u32[]{:S(2)}) collective-permute-start(bf16[4,4,3712]{2,1,0:T(4,128)(2,1)S(1)} %get-tuple-element.42.refs_1_), channel_id=1, source_target_pairs={{0,1},{1,0},{2,3},{3,2},{4,5},{5,4},{6,7},{7,6},{8,9},{9,8},{10,11... | collective-permute-start | bytes 356360 | tf_op jit(solution)/shard_map/ppermute | solution.py:563
  60.7 1.3 %collective-permute-start.12 = (bf16[4,4,3712]{2,1,0:T(4,128)(2,1)S(1)}, bf16[4,4,3712]{2,1,0:T(4,128)(2,1)S(1)}, u32[]{:S(2)}, u32[]{:S(2)}) collective-permute-start(bf16[4,4,3712]{2,1,0:T(4,128)(2,1)S(1)} %collective-permute-done.8.refs_2_), channel_id=1, source_target_pairs={{0,1},{1,0},{2,3},{3,2},{4,5},{5,4},{6,7},{7,6},{8,9},{9,8},{10,11... | collective-permute-start | bytes 356360 | tf_op jit(solution)/shard_map/ppermute | solution.py:563
  60.8 1.4 %collective-permute-start.13 = (bf16[4,4,3712]{2,1,0:T(4,128)(2,1)S(1)}, bf16[4,4,3712]{2,1,0:T(4,128)(2,1)S(1)}, u32[]{:S(2)}, u32[]{:S(2)}) collective-permute-start(bf16[4,4,3712]{2,1,0:T(4,128)(2,1)S(1)} %collective-permute-done.9.refs_3_), channel_id=1, source_target_pairs={{0,1},{1,0},{2,3},{3,2},{4,5},{5,4},{6,7},{7,6},{8,9},{9,8},{10,11... | collective-permute-start | bytes 356360 | tf_op jit(solution)/shard_map/ppermute | solution.py:563
  66.1 1.9 %collective-permute-start.14 = (bf16[64,3584]{1,0:T(8,128)(2,1)S(1)}, bf16[64,3584]{1,0:T(8,128)(2,1)S(1)}, u32[]{:S(2)}, u32[]{:S(2)}) collective-permute-start(bf16[64,3584]{1,0:T(8,128)(2,1)S(1)} %get-tuple-element.47), channel_id=1, source_target_pairs={{0,1},{1,0},{2,3},{3,2},{4,5},{5,4},{6,7},{7,6},{8,9},{9,8},{10,11... | collective-permute-start | bytes 1376264 | tf_op jit(solution)/shard_map/ppermute | solution.py:563
  68.1 6.1 %collective-permute-start.15 = (bf16[32,3584]{1,0:T(8,128)(2,1)S(1)}, bf16[32,3584]{1,0:T(8,128)(2,1)S(1)}, u32[]{:S(2)}, u32[]{:S(2)}) collective-permute-start(bf16[32,3584]{1,0:T(8,128)(2,1)S(1)} %get-tuple-element.49), channel_id=1, source_target_pairs={{0,2},{1,17},{2,0},{3,19},{4,6},{5,21},{6,4},{7,23},{8,10},{9,25},... | collective-permute-start | bytes 688136 | tf_op jit(solution)/shard_map/ppermute | solution.py:563
  74.2 4.9 %collective-permute-start.16 = (bf16[16,3584]{1,0:T(8,128)(2,1)S(1)}, bf16[16,3584]{1,0:T(8,128)(2,1)S(1)}, u32[]{:S(2)}, u32[]{:S(2)}) collective-permute-start(bf16[16,3584]{1,0:T(8,128)(2,1)S(1)} %get-tuple-element.51), channel_id=1, source_target_pairs={{0,16},{1,3},{2,18},{3,1},{4,20},{5,7},{6,22},{7,5},{8,24},{9,11},... | collective-permute-start | bytes 344072 | tf_op jit(solution)/shard_map/ppermute | solution.py:563
  79.1 4.5 %collective-permute-start.17 = (bf16[4,3584]{1,0:T(4,128)(2,1)S(1)}, bf16[4,3584]{1,0:T(4,128)(2,1)S(1)}, u32[]{:S(2)}, u32[]{:S(2)}) collective-permute-start(bf16[4,3584]{1,0:T(4,128)(2,1)S(1)} %get-tuple-element.53), channel_id=1, source_target_pairs={{0,4},{1,5},{2,6},{3,7},{4,0},{5,1},{6,2},{7,3},{8,12},{9,13},{10,... | collective-permute-start | bytes 86024 | tf_op jit(solution)/shard_map/ppermute | solution.py:563
  79.2 4.8 %collective-permute-start.18 = (bf16[4,3584]{1,0:T(4,128)(2,1)S(1)}, bf16[4,3584]{1,0:T(4,128)(2,1)S(1)}, u32[]{:S(2)}, u32[]{:S(2)}) collective-permute-start(bf16[4,3584]{1,0:T(4,128)(2,1)S(1)} %get-tuple-element.54), channel_id=1, source_target_pairs={{0,8},{1,9},{2,10},{3,11},{4,12},{5,13},{6,14},{7,15},{8,0},{9,1},... | collective-permute-start | bytes 86024 | tf_op jit(solution)/shard_map/ppermute | solution.py:563
  82.2 5.7 %collective-permute-start.19 = (bf16[4,3584]{1,0:T(4,128)(2,1)S(1)}, bf16[4,3584]{1,0:T(4,128)(2,1)S(1)}, u32[]{:S(2)}, u32[]{:S(2)}) collective-permute-start(bf16[4,3584]{1,0:T(4,128)(2,1)S(1)} %get-tuple-element.55), channel_id=1, source_target_pairs={{0,12},{1,13},{2,14},{3,15},{4,8},{5,9},{6,10},{7,11},{8,4},{9,5},... | collective-permute-start | bytes 86024 | tf_op jit(solution)/shard_map/ppermute | solution.py:563
  (3 other events, 21.2 us)

commit v8 on v7

--- a/solution.py
+++ b/solution.py
@@ -463,9 +463,11 @@
     refs[-1][...] = total.astype(BF16)
 
 
-def load_kernel(count, held, passed, *refs):
-    sources, passed_out = refs[held : held + count], refs[held + count]
-    outs, sems = refs[2 * held + count + 1 : -1], refs[-1]
+def load_kernel(count, held, passes, *refs):
+    first_out = passes + held + count
+    passed, sources = refs[:passes], refs[passes + held : first_out]
+    passed_outs = refs[first_out : first_out + passes]
+    outs, sems = refs[first_out + passes + held : -1], refs[-1]
     split = sems.shape[1]
     copies = []
     for k, (source, out) in enumerate(zip(sources, outs)):
@@ -476,7 +478,8 @@
                 pltpu.make_async_copy(source.at[0, span], out.at[span], sems.at[k, i])
             )
     fetch(copies)
-    passed_out[...] = passed[...]
+    for source, out in zip(passed, passed_outs):
+        out[...] = source[...]
     for copy in copies:
         copy.wait()
 
@@ -672,36 +675,37 @@
     )
 
     def load(passed, sources, vmem, held=()):
-        outs = [shape(passed.shape, BF16)] + [shape(x.shape, BF16) for x in held]
+        outs = [shape(x.shape, BF16) for x in (*passed, *held)]
+        passes = len(passed)
         return pl.pallas_call(
-            functools.partial(load_kernel, len(sources), len(held)),
+            functools.partial(load_kernel, len(sources), len(held), passes),
             out_shape=outs + [shape(w.shape[1:], BF16) for w in sources],
-            in_specs=[VMEM] + [ANY] * len(held) + [HBM] * len(sources),
-            out_specs=[VMEM] + [ANY] * len(held) + [VMEM] * len(sources),
-            input_output_aliases={1 + i: 1 + i for i in range(len(held))},
+            in_specs=[VMEM] * passes + [ANY] * len(held) + [HBM] * len(sources),
+            out_specs=[VMEM] * passes + [ANY] * len(held) + [VMEM] * len(sources),
+            input_output_aliases={passes + i: passes + i for i in range(len(held))},
             scratch_shapes=[pltpu.SemaphoreType.DMA((len(sources), 8))],
             compiler_params=pltpu.CompilerParams(vmem_limit_bytes=vmem * MIB),
             cost_estimate=pl.CostEstimate(
                 flops=0, bytes_accessed=2 * sum(w.size for w in sources), transcendentals=0
             ),
-        )(passed, *held, *sources)
+        )(*passed, *held, *sources)
 
     if direct:
         others = [swap(own_rows, mask) for mask in masks[1:]]
-        own_rows, down_here = load(own_rows, (w_down,), LOAD_MIB)
+        own_rows, down_here = load((own_rows,), (w_down,), LOAD_MIB)
         piece = call(
             stack_kernel,
             [shape((far_count, tokens, width + LANES), BF16)],
             (own_rows, *others),
         )[0]
     else:
-        own_rows, down_here = load(own_rows, (w_down,), LOAD_MIB)
+        own_rows, down_here = load((own_rows,), (w_down,), LOAD_MIB)
         piece = deal(own_rows, FAR)
     side_piece = swap(piece, top_bit, side_bit)
-    piece, down_here, up_here = load(piece, (w_up,), UP_MIB, (down_here,))
+    piece, down_here, up_here = load((piece,), (w_up,), UP_MIB, (down_here,))
     pieces = [piece, side_piece, swap(piece, side_bit, top_bit), swap(side_piece, side_bit, top_bit)]
-    pieces[1], down_here, up_here, gate_here = load(
-        side_piece, (w_gate,), SIDE_MIB, (down_here, up_here)
+    pieces[0], pieces[1], down_here, up_here, gate_here = load(
+        (piece, side_piece), (w_gate,), SIDE_MIB, (down_here, up_here)
     )
     pieces = pieces + [swap(p, 1) for p in pieces]
 

time: 88.8 us -> 88.7 us (level)
  transfers between devices with their start and end apart: 20 -> 20, of which waited for: 8 -> 9; matrix products, arithmetic and copies ran while one was open for 0% -> 0% of each run, Pallas kernels for 19% -> 19%
where the time goes in v8:
time: 88.7 us; the launch traced here: 88.4 us
  Pallas kernels  26.5 us (30%)
  blocking collectives  24 us (27%)
  starting transfers between devices  20.7 us (23%)
  waiting for transfers between devices  15.2 us (17%)
  local copies, waits for them, and re-layouts  1.11 us (1%)
    all_to_all x2, blocking collectives, deal(): return lax.all_to_all(x, names, split_axis=0, concat_axis=0, tiled=True)  24 us
    ppermute x20, starting transfers between devices, swap(): return lax.ppermute(x, ROWS, pairs)  20.7 us
    pallas_call x11, Pallas kernels, call(): pl.pallas_call(kernel, out_shape=outs, in_specs=in_specs or [VMEM] * len(...  16.9 us
    ppermute x20, waiting for transfers between devices, swap(): return lax.ppermute(x, ROWS, pairs)  15.2 us
    pallas_call x3, Pallas kernels, load(): pl.pallas_call(functools.partial(load_kernel, len(sources), len(held), pa...  9.54 us
  transfers between devices with their start and end apart: 20, of which 9 were waited for; matrix products, arithmetic and copies ran while one was open for 0% of the time, Pallas kernels for 19%

profile of v8, /device:TPU:0, one launch (start us, length us, event | category | flops | bytes accessed | tf_op | source)
XLA Modules:
  0.0 88.4 jit_solution(7663119145598687543)
XLA Ops:
  0.7 2.6 %shard_map.194 = (bf16[4,64,512]{2,1,0:T(8,128)(2,1)}, bf16[8,2176]{1,0:T(8,128)(2,1)}, f32[48]{0:T(128)}) custom-call(s32[1,2,4]{2,1,0:T(2,128)} %move_hbm.3, bf16[48]{0:T(256)(128)(2,1)} %scale_hbm.1, bf16[48,64,512]{2,1,0:T(8,128)(2,1)} %lat_hbm.1, bf16[48,4096]{1,0:T(8,128)(2,1)} %rope_hbm.3), custom_call_target="tpu_custom_call" | custom-call | tf_op jit(solution)/shard_map/pallas_call | solution.py:48
  3.3 3.0 %collective-permute-start = (bf16[4,64,512]{2,1,0:T(8,128)(2,1)}, bf16[4,64,512]{2,1,0:T(8,128)(2,1)S(1)}, u32[]{:S(2)}, u32[]{:S(2)}) collective-permute-start(bf16[4,64,512]{2,1,0:T(8,128)(2,1)} %get-tuple-element.30), channel_id=1, source_target_pairs={{0,16},{1,17},{2,18},{3,19},{4,20},{5,21},{6,22},{7,23},{8,24},{9,... | collective-permute-start | bytes 786440 | tf_op jit(solution)/shard_map/ppermute | solution.py:566
  6.4 7.4 %shard_map.195.refs_2_ = f32[264,640]{1,0:T(8,128)} custom-call(f32[48]{0:T(128)} %get-tuple-element.32.scale_hbm, s32[2,32]{1,0:T(2,128)} %table_hbm.1, s32[2]{0:T(128)} %lengths_hbm.1, s32[1,2,4]{2,1,0:T(2,128)} %move_hbm.3, bf16[48,64,512]{2,1,0:T(8,128)(2,1)} %lat_hbm.1, bf16[48,4096]{1,0:T(8,128)(2,1)} %rope_hbm.3, bf16[2,2,32,512]{3,2,1,0:T(8,128)(2,1)} %q_hbm.1, ...), custom_call_target="tpu_custom_call" | custom-call | flops 905969664 | bytes 4194304 | tf_op jit(solution)/shard_map/pallas_call | solution.py:48
  13.8 1.1 %copy-done = f32[264,640]{1,0:T(8,128)S(1)} copy-done((f32[264,640]{1,0:T(8,128)S(1)}, f32[264,640]{1,0:T(8,128)}, u32[]{:S(2)}) %copy-start) | copy-done | bytes 675864
  16.0 13.4 %all_to_all.10.blocks = bf16[8,16,512]{2,1,0:T(8,128)(2,1)S(1)} all-to-all(bf16[8,16,512]{2,1,0:T(8,128)(2,1)S(1)} %shard_map.196), channel_id=1, replica_groups=mesh['top'=2,'low'=1,'far'=4,'side'=2,'core'=2] {'far','side'}, dimensions={0} | all-to-all | bytes 262144 | tf_op jit(solution)/shard_map/all_to_all | solution.py:569
  29.4 1.1 %shard_map.197 = bf16[8,4,3584]{2,1,0:T(4,128)(2,1)S(1)} custom-call(bf16[8,16,512]{2,1,0:T(8,128)(2,1)S(1)} %all_to_all.10.blocks, bf16[2,512,128]{2,1,0:T(8,128)(2,1)S(1)} %copy-done.2, bf16[2,512,128]{2,1,0:T(8,128)(2,1)S(1)} %collective-permute-done.2.other_uv, bf16[256,3584]{1,0:T(8,128)(2,1)S(1)} %copy-done.1, ...), custom_call_target="tpu_custom_call" | custom-call | flops 117440512 | bytes 8388608 | tf_op jit(solution)/shard_map/pallas_call | solution.py:48
  30.6 10.6 %all_to_all.11.got = bf16[8,4,3584]{2,1,0:T(4,128)(2,1)S(1)} all-to-all(bf16[8,4,3584]{2,1,0:T(4,128)(2,1)S(1)} %shard_map.197), channel_id=1, replica_groups=mesh['top'=2,'low'=1,'far'=4,'side'=2,'core'=2] {'far','side'}, dimensions={0} | all-to-all | bytes 458752 | tf_op jit(solution)/shard_map/all_to_all | solution.py:569
  41.9 0.9 %collective-permute-start.4 = (bf16[1,4,3712]{2,1,0:T(4,128)(2,1)S(1)}, bf16[1,4,3712]{2,1,0:T(4,128)(2,1)S(1)}, u32[]{:S(2)}, u32[]{:S(2)}) collective-permute-start(bf16[1,4,3712]{2,1,0:T(4,128)(2,1)S(1)} %get-tuple-element.37.refs_0_), channel_id=1, source_target_pairs={{0,4},{1,5},{2,6},{3,7},{4,0},{5,1},{6,2},{7,3},{8,12},{9,13},{10,... | collective-permute-start | bytes 89096 | tf_op jit(solution)/shard_map/ppermute | solution.py:566
  43.4 2.9 %collective-permute-start.6 = (bf16[1,4,3712]{2,1,0:T(4,128)(2,1)S(1)}, bf16[1,4,3712]{2,1,0:T(4,128)(2,1)S(1)}, u32[]{:S(2)}, u32[]{:S(2)}) collective-permute-start(bf16[1,4,3712]{2,1,0:T(4,128)(2,1)S(1)} %get-tuple-element.37.refs_0_), channel_id=1, source_target_pairs={{0,12},{1,13},{2,14},{3,15},{4,8},{5,9},{6,10},{7,11},{8,4},{9,5},... | collective-permute-start | bytes 89096 | tf_op jit(solution)/shard_map/ppermute | solution.py:566
  46.3 3.2 %shard_map.199 = (bf16[1,4,3712]{2,1,0:T(4,128)(2,1)S(1)}, bf16[1024,3584]{1,0:T(8,128)(2,1)S(1)}) custom-call(bf16[1,4,3712]{2,1,0:T(4,128)(2,1)S(1)} %get-tuple-element.37.refs_0_, bf16[1,1024,3584]{2,1,0:T(8,128)(2,1)} %refs_1_.1), custom_call_target="tpu_custom_call" | custom-call | bytes 7340032 | tf_op jit(solution)/shard_map/pallas_call | solution.py:680
  49.6 1.6 %collective-permute-start.7 = (bf16[4,4,3712]{2,1,0:T(4,128)(2,1)S(1)}, bf16[4,4,3712]{2,1,0:T(4,128)(2,1)S(1)}, u32[]{:S(2)}, u32[]{:S(2)}) collective-permute-start(bf16[4,4,3712]{2,1,0:T(4,128)(2,1)S(1)} %shard_map.200.refs_0_), channel_id=1, source_target_pairs={{0,16},{1,3},{2,18},{3,1},{4,20},{5,7},{6,22},{7,5},{8,24},{9,11},... | collective-permute-start | bytes 356360 | tf_op jit(solution)/shard_map/ppermute | solution.py:566
  51.1 3.2 %shard_map.201 = (bf16[4,4,3712]{2,1,0:T(4,128)(2,1)S(1)}, bf16[1024,3584]{1,0:T(8,128)(2,1)S(1)}, bf16[3584,1024]{1,0:T(8,128)(2,1)S(1)}) custom-call(bf16[4,4,3712]{2,1,0:T(4,128)(2,1)S(1)} %shard_map.200.refs_0_, bf16[1024,3584]{1,0:T(8,128)(2,1)S(1)} %get-tuple-element.39.refs_1_, bf16[1,3584,1024]{2,1,0:T(8,128)(2,1)} %refs_2_.1), custom_call_target="tpu_custom_call", output_to_operand_aliasing={{1}: (1, {})} | custom-call | bytes 7340032 | tf_op jit(solution)/shard_map/pallas_call | solution.py:680
  54.3 1.4 %collective-permute-start.8 = (bf16[4,4,3712]{2,1,0:T(4,128)(2,1)S(1)}, bf16[4,4,3712]{2,1,0:T(4,128)(2,1)S(1)}, u32[]{:S(2)}, u32[]{:S(2)}) collective-permute-start(bf16[4,4,3712]{2,1,0:T(4,128)(2,1)S(1)} %get-tuple-element.40.refs_0_), channel_id=1, source_target_pairs={{0,2},{1,17},{2,0},{3,19},{4,6},{5,21},{6,4},{7,23},{8,10},{9,25},... | collective-permute-start | bytes 356360 | tf_op jit(solution)/shard_map/ppermute | solution.py:566
  55.6 1.3 %collective-permute-start.9 = (bf16[4,4,3712]{2,1,0:T(4,128)(2,1)S(1)}, bf16[4,4,3712]{2,1,0:T(4,128)(2,1)S(1)}, u32[]{:S(2)}, u32[]{:S(2)}) collective-permute-start(bf16[4,4,3712]{2,1,0:T(4,128)(2,1)S(1)} %collective-permute-done.7.refs_1_), channel_id=1, source_target_pairs={{0,2},{1,17},{2,0},{3,19},{4,6},{5,21},{6,4},{7,23},{8,10},{9,25},... | collective-permute-start | bytes 356360 | tf_op jit(solution)/shard_map/ppermute | solution.py:566
  56.9 3.2 %shard_map.202 = (bf16[4,4,3712]{2,1,0:T(4,128)(2,1)S(1)}, bf16[4,4,3712]{2,1,0:T(4,128)(2,1)S(1)}, bf16[1024,3584]{1,0:T(8,128)(2,1)S(1)}, bf16[3584,1024]{1,0:T(8,128)(2,1)S(1)}, bf16[3584,1024]{1,0:T(8,128)(2,1)S(1)}) custom-call(bf16[4,4,3712]{2,1,0:T(4,128)(2,1)S(1)} %get-tuple-element.40.refs_0_, ...), custom_call_target="tpu_custom_call", output_to_operand_aliasing={{2}: (2, {}), {3}: (3, {})} | custom-call | bytes 7340032 | tf_op jit(solution)/shard_map/pallas_call | solution.py:680
  62.2 3.8 %shard_map.203 = (f32[64,3584]{1,0:T(8,128)S(1)}, bf16[64,3584]{1,0:T(8,128)(2,1)S(1)}) custom-call(bf16[4,4,3712]{2,1,0:T(4,128)(2,1)S(1)} %get-tuple-element.43.refs_0_, bf16[4,4,3712]{2,1,0:T(4,128)(2,1)S(1)} %get-tuple-element.44.refs_1_, bf16[4,4,3712]{2,1,0:T(4,128)(2,1)S(1)} %collective-permute-done.8.refs_2_, ...), custom_call_target="tpu_custom_call" | custom-call | flops 2818572288 | bytes 22020096 | tf_op jit(solution)/shard_map/pallas_call | solution.py:48
  66.4 1.5 %collective-permute-done.14.got = bf16[64,3584]{1,0:T(8,128)(2,1)S(1)} collective-permute-done((bf16[64,3584]{1,0:T(8,128)(2,1)S(1)}, bf16[64,3584]{1,0:T(8,128)(2,1)S(1)}, u32[]{:S(2)}, u32[]{:S(2)}) %collective-permute-start.14) | collective-permute-done | bytes 458784 | tf_op jit(solution)/shard_map/ppermute | solution.py:566
  68.0 0.9 %collective-permute-start.15 = (bf16[32,3584]{1,0:T(8,128)(2,1)S(1)}, bf16[32,3584]{1,0:T(8,128)(2,1)S(1)}, u32[]{:S(2)}, u32[]{:S(2)}) collective-permute-start(bf16[32,3584]{1,0:T(8,128)(2,1)S(1)} %get-tuple-element.51), channel_id=1, source_target_pairs={{0,2},{1,17},{2,0},{3,19},{4,6},{5,21},{6,4},{7,23},{8,10},{9,25},... | collective-permute-start | bytes 688136 | tf_op jit(solution)/shard_map/ppermute | solution.py:566
  68.9 5.1 %collective-permute-done.15.got = bf16[32,3584]{1,0:T(8,128)(2,1)S(1)} collective-permute-done((bf16[32,3584]{1,0:T(8,128)(2,1)S(1)}, bf16[32,3584]{1,0:T(8,128)(2,1)S(1)}, u32[]{:S(2)}, u32[]{:S(2)}) %collective-permute-start.15) | collective-permute-done | bytes 229408 | tf_op jit(solution)/shard_map/ppermute | solution.py:566
  74.1 1.6 %collective-permute-start.16 = (bf16[16,3584]{1,0:T(8,128)(2,1)S(1)}, bf16[16,3584]{1,0:T(8,128)(2,1)S(1)}, u32[]{:S(2)}, u32[]{:S(2)}) collective-permute-start(bf16[16,3584]{1,0:T(8,128)(2,1)S(1)} %get-tuple-element.53), channel_id=1, source_target_pairs={{0,16},{1,3},{2,18},{3,1},{4,20},{5,7},{6,22},{7,5},{8,24},{9,11},... | collective-permute-start | bytes 344072 | tf_op jit(solution)/shard_map/ppermute | solution.py:566
  75.6 3.3 %collective-permute-done.16.got = bf16[16,3584]{1,0:T(8,128)(2,1)S(1)} collective-permute-done((bf16[16,3584]{1,0:T(8,128)(2,1)S(1)}, bf16[16,3584]{1,0:T(8,128)(2,1)S(1)}, u32[]{:S(2)}, u32[]{:S(2)}) %collective-permute-start.16) | collective-permute-done | bytes 114720 | tf_op jit(solution)/shard_map/ppermute | solution.py:566
  79.1 3.0 %collective-permute-start.18 = (bf16[4,3584]{1,0:T(4,128)(2,1)S(1)}, bf16[4,3584]{1,0:T(4,128)(2,1)S(1)}, u32[]{:S(2)}, u32[]{:S(2)}) collective-permute-start(bf16[4,3584]{1,0:T(4,128)(2,1)S(1)} %get-tuple-element.56), channel_id=1, source_target_pairs={{0,8},{1,9},{2,10},{3,11},{4,12},{5,13},{6,14},{7,15},{8,0},{9,1},... | collective-permute-start | bytes 86024 | tf_op jit(solution)/shard_map/ppermute | solution.py:566
  82.1 1.4 %collective-permute-start.19 = (bf16[4,3584]{1,0:T(4,128)(2,1)S(1)}, bf16[4,3584]{1,0:T(4,128)(2,1)S(1)}, u32[]{:S(2)}, u32[]{:S(2)}) collective-permute-start(bf16[4,3584]{1,0:T(4,128)(2,1)S(1)} %get-tuple-element.57), channel_id=1, source_target_pairs={{0,12},{1,13},{2,14},{3,15},{4,8},{5,9},{6,10},{7,11},{8,4},{9,5},... | collective-permute-start | bytes 86024 | tf_op jit(solution)/shard_map/ppermute | solution.py:566
  83.9 3.8 %collective-permute-done.19.refs_3_ = bf16[4,3584]{1,0:T(4,128)(2,1)S(1)} collective-permute-done((bf16[4,3584]{1,0:T(4,128)(2,1)S(1)}, bf16[4,3584]{1,0:T(4,128)(2,1)S(1)}, u32[]{:S(2)}, u32[]{:S(2)}) %collective-permute-start.19) | collective-permute-done | bytes 28704 | tf_op jit(solution)/shard_map/ppermute | solution.py:566
  (46 shorter events, 6.3 us)
Async XLA Ops:
  0.6 14.9 %copy-start.2 = (bf16[2,512,128]{2,1,0:T(8,128)(2,1)S(1)}, bf16[2,512,128]{2,1,0:T(8,128)(2,1)}, u32[]{:S(2)}) copy-start(bf16[2,512,128]{2,1,0:T(8,128)(2,1)} %w_uv.1) | copy-start | bytes 786436
  0.7 40.6 %copy-start.4 = (bf16[4,3584]{1,0:T(4,128)(2,1)S(1)}, bf16[4,3584]{1,0:T(4,128)(2,1)}, u32[]{:S(2)}) copy-start(bf16[4,3584]{1,0:T(4,128)(2,1)} %residual.1) | copy-start | bytes 86020
  0.7 40.5 %copy-start.5 = (f32[3584]{0:T(1024)S(1)}, f32[3584]{0:T(1024)}, u32[]{:S(2)}) copy-start(f32[3584]{0:T(1024)} %gain.1) | copy-start | bytes 43012
  0.7 40.5 %copy-start.6 = (s32[4,8]{1,0:T(4,128)S(1)}, s32[4,8]{1,0:T(4,128)}, u32[]{:S(2)}) copy-start(s32[4,8]{1,0:T(4,128)} %routes.1) | copy-start | bytes 388
  3.3 10.5 %collective-permute-start = (bf16[4,64,512]{2,1,0:T(8,128)(2,1)}, bf16[4,64,512]{2,1,0:T(8,128)(2,1)S(1)}, u32[]{:S(2)}, u32[]{:S(2)}) collective-permute-start(bf16[4,64,512]{2,1,0:T(8,128)(2,1)} %get-tuple-element.30), channel_id=1, source_target_pairs={{0,16},{1,17},{2,18},{3,19},{4,20},{5,21},{6,22},{7,23},{8,24},{9,... | collective-permute-start | bytes 786440 | tf_op jit(solution)/shard_map/ppermute | solution.py:566
  6.3 7.4 %collective-permute-start.1 = (bf16[8,2176]{1,0:T(8,128)(2,1)}, bf16[8,2176]{1,0:T(8,128)(2,1)S(1)}, u32[]{:S(2)}, u32[]{:S(2)}) collective-permute-start(bf16[8,2176]{1,0:T(8,128)(2,1)} %get-tuple-element.31), channel_id=1, source_target_pairs={{0,16},{1,17},{2,18},{3,19},{4,20},{5,21},{6,22},{7,23},{8,24},{9,... | collective-permute-start | bytes 104456 | tf_op jit(solution)/shard_map/ppermute | solution.py:566
  15.4 14.0 %collective-permute-start.3 = (bf16[256,3584]{1,0:T(8,128)(2,1)S(1)}, bf16[256,3584]{1,0:T(8,128)(2,1)S(1)}, u32[]{:S(2)}, u32[]{:S(2)}) collective-permute-start(bf16[256,3584]{1,0:T(8,128)(2,1)S(1)} %copy-done.1), channel_id=1, source_target_pairs={{0,1},{1,0},{2,3},{3,2},{4,5},{5,4},{6,7},{7,6},{8,9},{9,8},{10,11... | collective-permute-start | bytes 5505032 | tf_op jit(solution)/shard_map/ppermute | solution.py:566
  15.5 13.9 %collective-permute-start.2 = (bf16[2,512,128]{2,1,0:T(8,128)(2,1)S(1)}, bf16[2,512,128]{2,1,0:T(8,128)(2,1)S(1)}, u32[]{:S(2)}, u32[]{:S(2)}) collective-permute-start(bf16[2,512,128]{2,1,0:T(8,128)(2,1)S(1)} %copy-done.2), channel_id=1, source_target_pairs={{0,1},{1,0},{2,3},{3,2},{4,5},{5,4},{6,7},{7,6},{8,9},{9,8},{10,11... | collective-permute-start | bytes 786440 | tf_op jit(solution)/shard_map/ppermute | solution.py:566
  41.9 7.6 %collective-permute-start.4 = (bf16[1,4,3712]{2,1,0:T(4,128)(2,1)S(1)}, bf16[1,4,3712]{2,1,0:T(4,128)(2,1)S(1)}, u32[]{:S(2)}, u32[]{:S(2)}) collective-permute-start(bf16[1,4,3712]{2,1,0:T(4,128)(2,1)S(1)} %get-tuple-element.37.refs_0_), channel_id=1, source_target_pairs={{0,4},{1,5},{2,6},{3,7},{4,0},{5,1},{6,2},{7,3},{8,12},{9,13},{10,... | collective-permute-start | bytes 89096 | tf_op jit(solution)/shard_map/ppermute | solution.py:566
  42.8 6.7 %collective-permute-start.5 = (bf16[1,4,3712]{2,1,0:T(4,128)(2,1)S(1)}, bf16[1,4,3712]{2,1,0:T(4,128)(2,1)S(1)}, u32[]{:S(2)}, u32[]{:S(2)}) collective-permute-start(bf16[1,4,3712]{2,1,0:T(4,128)(2,1)S(1)} %get-tuple-element.37.refs_0_), channel_id=1, source_target_pairs={{0,8},{1,9},{2,10},{3,11},{4,12},{5,13},{6,14},{7,15},{8,0},{9,1},... | collective-permute-start | bytes 89096 | tf_op jit(solution)/shard_map/ppermute | solution.py:566
  43.4 6.1 %collective-permute-start.6 = (bf16[1,4,3712]{2,1,0:T(4,128)(2,1)S(1)}, bf16[1,4,3712]{2,1,0:T(4,128)(2,1)S(1)}, u32[]{:S(2)}, u32[]{:S(2)}) collective-permute-start(bf16[1,4,3712]{2,1,0:T(4,128)(2,1)S(1)} %get-tuple-element.37.refs_0_), channel_id=1, source_target_pairs={{0,12},{1,13},{2,14},{3,15},{4,8},{5,9},{6,10},{7,11},{8,4},{9,5},... | collective-permute-start | bytes 89096 | tf_op jit(solution)/shard_map/ppermute | solution.py:566
  49.6 6.1 %collective-permute-start.7 = (bf16[4,4,3712]{2,1,0:T(4,128)(2,1)S(1)}, bf16[4,4,3712]{2,1,0:T(4,128)(2,1)S(1)}, u32[]{:S(2)}, u32[]{:S(2)}) collective-permute-start(bf16[4,4,3712]{2,1,0:T(4,128)(2,1)S(1)} %shard_map.200.refs_0_), channel_id=1, source_target_pairs={{0,16},{1,3},{2,18},{3,1},{4,20},{5,7},{6,22},{7,5},{8,24},{9,11},... | collective-permute-start | bytes 356360 | tf_op jit(solution)/shard_map/ppermute | solution.py:566
  54.3 6.4 %collective-permute-start.8 = (bf16[4,4,3712]{2,1,0:T(4,128)(2,1)S(1)}, bf16[4,4,3712]{2,1,0:T(4,128)(2,1)S(1)}, u32[]{:S(2)}, u32[]{:S(2)}) collective-permute-start(bf16[4,4,3712]{2,1,0:T(4,128)(2,1)S(1)} %get-tuple-element.40.refs_0_), channel_id=1, source_target_pairs={{0,2},{1,17},{2,0},{3,19},{4,6},{5,21},{6,4},{7,23},{8,10},{9,25},... | collective-permute-start | bytes 356360 | tf_op jit(solution)/shard_map/ppermute | solution.py:566
  55.6 5.2 %collective-permute-start.9 = (bf16[4,4,3712]{2,1,0:T(4,128)(2,1)S(1)}, bf16[4,4,3712]{2,1,0:T(4,128)(2,1)S(1)}, u32[]{:S(2)}, u32[]{:S(2)}) collective-permute-start(bf16[4,4,3712]{2,1,0:T(4,128)(2,1)S(1)} %collective-permute-done.7.refs_1_), channel_id=1, source_target_pairs={{0,2},{1,17},{2,0},{3,19},{4,6},{5,21},{6,4},{7,23},{8,10},{9,25},... | collective-permute-start | bytes 356360 | tf_op jit(solution)/shard_map/ppermute | solution.py:566
  60.2 1.4 %collective-permute-start.10 = (bf16[4,4,3712]{2,1,0:T(4,128)(2,1)S(1)}, bf16[4,4,3712]{2,1,0:T(4,128)(2,1)S(1)}, u32[]{:S(2)}, u32[]{:S(2)}) collective-permute-start(bf16[4,4,3712]{2,1,0:T(4,128)(2,1)S(1)} %get-tuple-element.43.refs_0_), channel_id=1, source_target_pairs={{0,1},{1,0},{2,3},{3,2},{4,5},{5,4},{6,7},{7,6},{8,9},{9,8},{10,11... | collective-permute-start | bytes 356360 | tf_op jit(solution)/shard_map/ppermute | solution.py:566
  60.2 1.5 %collective-permute-start.11 = (bf16[4,4,3712]{2,1,0:T(4,128)(2,1)S(1)}, bf16[4,4,3712]{2,1,0:T(4,128)(2,1)S(1)}, u32[]{:S(2)}, u32[]{:S(2)}) collective-permute-start(bf16[4,4,3712]{2,1,0:T(4,128)(2,1)S(1)} %get-tuple-element.44.refs_1_), channel_id=1, source_target_pairs={{0,1},{1,0},{2,3},{3,2},{4,5},{5,4},{6,7},{7,6},{8,9},{9,8},{10,11... | collective-permute-start | bytes 356360 | tf_op jit(solution)/shard_map/ppermute | solution.py:566
  60.7 1.3 %collective-permute-start.12 = (bf16[4,4,3712]{2,1,0:T(4,128)(2,1)S(1)}, bf16[4,4,3712]{2,1,0:T(4,128)(2,1)S(1)}, u32[]{:S(2)}, u32[]{:S(2)}) collective-permute-start(bf16[4,4,3712]{2,1,0:T(4,128)(2,1)S(1)} %collective-permute-done.8.refs_2_), channel_id=1, source_target_pairs={{0,1},{1,0},{2,3},{3,2},{4,5},{5,4},{6,7},{7,6},{8,9},{9,8},{10,11... | collective-permute-start | bytes 356360 | tf_op jit(solution)/shard_map/ppermute | solution.py:566
  60.8 1.4 %collective-permute-start.13 = (bf16[4,4,3712]{2,1,0:T(4,128)(2,1)S(1)}, bf16[4,4,3712]{2,1,0:T(4,128)(2,1)S(1)}, u32[]{:S(2)}, u32[]{:S(2)}) collective-permute-start(bf16[4,4,3712]{2,1,0:T(4,128)(2,1)S(1)} %collective-permute-done.9.refs_3_), channel_id=1, source_target_pairs={{0,1},{1,0},{2,3},{3,2},{4,5},{5,4},{6,7},{7,6},{8,9},{9,8},{10,11... | collective-permute-start | bytes 356360 | tf_op jit(solution)/shard_map/ppermute | solution.py:566
  66.0 1.9 %collective-permute-start.14 = (bf16[64,3584]{1,0:T(8,128)(2,1)S(1)}, bf16[64,3584]{1,0:T(8,128)(2,1)S(1)}, u32[]{:S(2)}, u32[]{:S(2)}) collective-permute-start(bf16[64,3584]{1,0:T(8,128)(2,1)S(1)} %get-tuple-element.49), channel_id=1, source_target_pairs={{0,1},{1,0},{2,3},{3,2},{4,5},{5,4},{6,7},{7,6},{8,9},{9,8},{10,11... | collective-permute-start | bytes 1376264 | tf_op jit(solution)/shard_map/ppermute | solution.py:566
  68.0 6.1 %collective-permute-start.15 = (bf16[32,3584]{1,0:T(8,128)(2,1)S(1)}, bf16[32,3584]{1,0:T(8,128)(2,1)S(1)}, u32[]{:S(2)}, u32[]{:S(2)}) collective-permute-start(bf16[32,3584]{1,0:T(8,128)(2,1)S(1)} %get-tuple-element.51), channel_id=1, source_target_pairs={{0,2},{1,17},{2,0},{3,19},{4,6},{5,21},{6,4},{7,23},{8,10},{9,25},... | collective-permute-start | bytes 688136 | tf_op jit(solution)/shard_map/ppermute | solution.py:566
  74.1 4.9 %collective-permute-start.16 = (bf16[16,3584]{1,0:T(8,128)(2,1)S(1)}, bf16[16,3584]{1,0:T(8,128)(2,1)S(1)}, u32[]{:S(2)}, u32[]{:S(2)}) collective-permute-start(bf16[16,3584]{1,0:T(8,128)(2,1)S(1)} %get-tuple-element.53), channel_id=1, source_target_pairs={{0,16},{1,3},{2,18},{3,1},{4,20},{5,7},{6,22},{7,5},{8,24},{9,11},... | collective-permute-start | bytes 344072 | tf_op jit(solution)/shard_map/ppermute | solution.py:566
  79.0 4.5 %collective-permute-start.17 = (bf16[4,3584]{1,0:T(4,128)(2,1)S(1)}, bf16[4,3584]{1,0:T(4,128)(2,1)S(1)}, u32[]{:S(2)}, u32[]{:S(2)}) collective-permute-start(bf16[4,3584]{1,0:T(4,128)(2,1)S(1)} %get-tuple-element.55), channel_id=1, source_target_pairs={{0,4},{1,5},{2,6},{3,7},{4,0},{5,1},{6,2},{7,3},{8,12},{9,13},{10,... | collective-permute-start | bytes 86024 | tf_op jit(solution)/shard_map/ppermute | solution.py:566
  79.1 4.8 %collective-permute-start.18 = (bf16[4,3584]{1,0:T(4,128)(2,1)S(1)}, bf16[4,3584]{1,0:T(4,128)(2,1)S(1)}, u32[]{:S(2)}, u32[]{:S(2)}) collective-permute-start(bf16[4,3584]{1,0:T(4,128)(2,1)S(1)} %get-tuple-element.56), channel_id=1, source_target_pairs={{0,8},{1,9},{2,10},{3,11},{4,12},{5,13},{6,14},{7,15},{8,0},{9,1},... | collective-permute-start | bytes 86024 | tf_op jit(solution)/shard_map/ppermute | solution.py:566
  82.1 5.7 %collective-permute-start.19 = (bf16[4,3584]{1,0:T(4,128)(2,1)S(1)}, bf16[4,3584]{1,0:T(4,128)(2,1)S(1)}, u32[]{:S(2)}, u32[]{:S(2)}) collective-permute-start(bf16[4,3584]{1,0:T(4,128)(2,1)S(1)} %get-tuple-element.57), channel_id=1, source_target_pairs={{0,12},{1,13},{2,14},{3,15},{4,8},{5,9},{6,10},{7,11},{8,4},{9,5},... | collective-permute-start | bytes 86024 | tf_op jit(solution)/shard_map/ppermute | solution.py:566
  (3 other events, 21.2 us)

commit v9 on v8

--- a/solution.py
+++ b/solution.py
@@ -632,7 +632,7 @@
             pltpu.VMEM(q_rope.shape, BF16),
             pltpu.VMEM(new_lat.shape, BF16),
             pltpu.VMEM(new_rope.shape, BF16),
-            pltpu.VMEM((rows // LANES, slots * page_len, LANES), F32),
+            pltpu.VMEM((rows // LANES, (slots + 1) * page_len, LANES), F32),
             pltpu.SMEM((rollouts * view,), jnp.int32),
             pltpu.VMEM((16, latent), F32),
             pltpu.VMEM((16, 2 * rope_dim), F32),
@@ -647,7 +647,7 @@
         functools.partial(merge_kernel, partners),
         [shape((chips, 2 * tokens * per_device, latent), BF16)],
         (*got_lat, *got_rope, *local),
-        scratch=[pltpu.VMEM((rows // LANES, partners * moves * page_len, LANES), F32)],
+        scratch=[pltpu.VMEM((rows // LANES, (partners * moves + 1) * page_len, LANES), F32)],
         cost=(2 * moves * page_len * rows * 2 * latent, MIB),
     )[0]
 

time: 88.7 us -> 88.7 us (level)
  no operation moved by 1% of the time
where the time goes in v9:
time: 88.7 us; the launch traced here: 88.4 us
  Pallas kernels  26.5 us (30%)
  blocking collectives  24 us (27%)
  starting transfers between devices  20.7 us (23%)
  waiting for transfers between devices  15.2 us (17%)
  local copies, waits for them, and re-layouts  1.11 us (1%)
    all_to_all x2, blocking collectives, deal(): return lax.all_to_all(x, names, split_axis=0, concat_axis=0, tiled=True)  24 us
    ppermute x20, starting transfers between devices, swap(): return lax.ppermute(x, ROWS, pairs)  20.7 us
    pallas_call x11, Pallas kernels, call(): pl.pallas_call(kernel, out_shape=outs, in_specs=in_specs or [VMEM] * len(...  16.9 us
    ppermute x20, waiting for transfers between devices, swap(): return lax.ppermute(x, ROWS, pairs)  15.2 us
    pallas_call x3, Pallas kernels, load(): pl.pallas_call(functools.partial(load_kernel, len(sources), len(held), pa...  9.54 us
  transfers between devices with their start and end apart: 20, of which 9 were waited for; matrix products, arithmetic and copies ran while one was open for 0% of the time, Pallas kernels for 19%

profile of v9, /device:TPU:0, one launch (start us, length us, event | category | flops | bytes accessed | tf_op | source)
XLA Modules:
  0.0 88.4 jit_solution(2958824519453817274)
XLA Ops:
  0.7 2.6 %shard_map.194 = (bf16[4,64,512]{2,1,0:T(8,128)(2,1)}, bf16[8,2176]{1,0:T(8,128)(2,1)}, f32[48]{0:T(128)}) custom-call(s32[1,2,4]{2,1,0:T(2,128)} %move_hbm.3, bf16[48]{0:T(256)(128)(2,1)} %scale_hbm.1, bf16[48,64,512]{2,1,0:T(8,128)(2,1)} %lat_hbm.1, bf16[48,4096]{1,0:T(8,128)(2,1)} %rope_hbm.3), custom_call_target="tpu_custom_call" | custom-call | tf_op jit(solution)/shard_map/pallas_call | solution.py:48
  3.3 3.0 %collective-permute-start = (bf16[4,64,512]{2,1,0:T(8,128)(2,1)}, bf16[4,64,512]{2,1,0:T(8,128)(2,1)S(1)}, u32[]{:S(2)}, u32[]{:S(2)}) collective-permute-start(bf16[4,64,512]{2,1,0:T(8,128)(2,1)} %get-tuple-element.30), channel_id=1, source_target_pairs={{0,16},{1,17},{2,18},{3,19},{4,20},{5,21},{6,22},{7,23},{8,24},{9,... | collective-permute-start | bytes 786440 | tf_op jit(solution)/shard_map/ppermute | solution.py:566
  6.4 7.4 %shard_map.195.refs_2_ = f32[264,640]{1,0:T(8,128)} custom-call(f32[48]{0:T(128)} %get-tuple-element.32.scale_hbm, s32[2,32]{1,0:T(2,128)} %table_hbm.1, s32[2]{0:T(128)} %lengths_hbm.1, s32[1,2,4]{2,1,0:T(2,128)} %move_hbm.3, bf16[48,64,512]{2,1,0:T(8,128)(2,1)} %lat_hbm.1, bf16[48,4096]{1,0:T(8,128)(2,1)} %rope_hbm.3, bf16[2,2,32,512]{3,2,1,0:T(8,128)(2,1)} %q_hbm.1, ...), custom_call_target="tpu_custom_call" | custom-call | flops 905969664 | bytes 4194304 | tf_op jit(solution)/shard_map/pallas_call | solution.py:48
  13.8 1.1 %copy-done = f32[264,640]{1,0:T(8,128)S(1)} copy-done((f32[264,640]{1,0:T(8,128)S(1)}, f32[264,640]{1,0:T(8,128)}, u32[]{:S(2)}) %copy-start) | copy-done | bytes 675864
  16.0 13.4 %all_to_all.10.blocks = bf16[8,16,512]{2,1,0:T(8,128)(2,1)S(1)} all-to-all(bf16[8,16,512]{2,1,0:T(8,128)(2,1)S(1)} %shard_map.196), channel_id=1, replica_groups=mesh['top'=2,'low'=1,'far'=4,'side'=2,'core'=2] {'far','side'}, dimensions={0} | all-to-all | bytes 262144 | tf_op jit(solution)/shard_map/all_to_all | solution.py:569
  29.4 1.1 %shard_map.197 = bf16[8,4,3584]{2,1,0:T(4,128)(2,1)S(1)} custom-call(bf16[8,16,512]{2,1,0:T(8,128)(2,1)S(1)} %all_to_all.10.blocks, bf16[2,512,128]{2,1,0:T(8,128)(2,1)S(1)} %copy-done.2, bf16[2,512,128]{2,1,0:T(8,128)(2,1)S(1)} %collective-permute-done.2.other_uv, bf16[256,3584]{1,0:T(8,128)(2,1)S(1)} %copy-done.1, ...), custom_call_target="tpu_custom_call" | custom-call | flops 117440512 | bytes 8388608 | tf_op jit(solution)/shard_map/pallas_call | solution.py:48
  30.6 10.6 %all_to_all.11.got = bf16[8,4,3584]{2,1,0:T(4,128)(2,1)S(1)} all-to-all(bf16[8,4,3584]{2,1,0:T(4,128)(2,1)S(1)} %shard_map.197), channel_id=1, replica_groups=mesh['top'=2,'low'=1,'far'=4,'side'=2,'core'=2] {'far','side'}, dimensions={0} | all-to-all | bytes 458752 | tf_op jit(solution)/shard_map/all_to_all | solution.py:569
  41.9 0.9 %collective-permute-start.4 = (bf16[1,4,3712]{2,1,0:T(4,128)(2,1)S(1)}, bf16[1,4,3712]{2,1,0:T(4,128)(2,1)S(1)}, u32[]{:S(2)}, u32[]{:S(2)}) collective-permute-start(bf16[1,4,3712]{2,1,0:T(4,128)(2,1)S(1)} %get-tuple-element.37.refs_0_), channel_id=1, source_target_pairs={{0,4},{1,5},{2,6},{3,7},{4,0},{5,1},{6,2},{7,3},{8,12},{9,13},{10,... | collective-permute-start | bytes 89096 | tf_op jit(solution)/shard_map/ppermute | solution.py:566
  43.4 2.9 %collective-permute-start.6 = (bf16[1,4,3712]{2,1,0:T(4,128)(2,1)S(1)}, bf16[1,4,3712]{2,1,0:T(4,128)(2,1)S(1)}, u32[]{:S(2)}, u32[]{:S(2)}) collective-permute-start(bf16[1,4,3712]{2,1,0:T(4,128)(2,1)S(1)} %get-tuple-element.37.refs_0_), channel_id=1, source_target_pairs={{0,12},{1,13},{2,14},{3,15},{4,8},{5,9},{6,10},{7,11},{8,4},{9,5},... | collective-permute-start | bytes 89096 | tf_op jit(solution)/shard_map/ppermute | solution.py:566
  46.3 3.2 %shard_map.199 = (bf16[1,4,3712]{2,1,0:T(4,128)(2,1)S(1)}, bf16[1024,3584]{1,0:T(8,128)(2,1)S(1)}) custom-call(bf16[1,4,3712]{2,1,0:T(4,128)(2,1)S(1)} %get-tuple-element.37.refs_0_, bf16[1,1024,3584]{2,1,0:T(8,128)(2,1)} %refs_1_.1), custom_call_target="tpu_custom_call" | custom-call | bytes 7340032 | tf_op jit(solution)/shard_map/pallas_call | solution.py:680
  49.6 1.6 %collective-permute-start.7 = (bf16[4,4,3712]{2,1,0:T(4,128)(2,1)S(1)}, bf16[4,4,3712]{2,1,0:T(4,128)(2,1)S(1)}, u32[]{:S(2)}, u32[]{:S(2)}) collective-permute-start(bf16[4,4,3712]{2,1,0:T(4,128)(2,1)S(1)} %shard_map.200.refs_0_), channel_id=1, source_target_pairs={{0,16},{1,3},{2,18},{3,1},{4,20},{5,7},{6,22},{7,5},{8,24},{9,11},... | collective-permute-start | bytes 356360 | tf_op jit(solution)/shard_map/ppermute | solution.py:566
  51.1 3.2 %shard_map.201 = (bf16[4,4,3712]{2,1,0:T(4,128)(2,1)S(1)}, bf16[1024,3584]{1,0:T(8,128)(2,1)S(1)}, bf16[3584,1024]{1,0:T(8,128)(2,1)S(1)}) custom-call(bf16[4,4,3712]{2,1,0:T(4,128)(2,1)S(1)} %shard_map.200.refs_0_, bf16[1024,3584]{1,0:T(8,128)(2,1)S(1)} %get-tuple-element.39.refs_1_, bf16[1,3584,1024]{2,1,0:T(8,128)(2,1)} %refs_2_.1), custom_call_target="tpu_custom_call", output_to_operand_aliasing={{1}: (1, {})} | custom-call | bytes 7340032 | tf_op jit(solution)/shard_map/pallas_call | solution.py:680
  54.3 1.4 %collective-permute-start.8 = (bf16[4,4,3712]{2,1,0:T(4,128)(2,1)S(1)}, bf16[4,4,3712]{2,1,0:T(4,128)(2,1)S(1)}, u32[]{:S(2)}, u32[]{:S(2)}) collective-permute-start(bf16[4,4,3712]{2,1,0:T(4,128)(2,1)S(1)} %get-tuple-element.40.refs_0_), channel_id=1, source_target_pairs={{0,2},{1,17},{2,0},{3,19},{4,6},{5,21},{6,4},{7,23},{8,10},{9,25},... | collective-permute-start | bytes 356360 | tf_op jit(solution)/shard_map/ppermute | solution.py:566
  55.6 1.3 %collective-permute-start.9 = (bf16[4,4,3712]{2,1,0:T(4,128)(2,1)S(1)}, bf16[4,4,3712]{2,1,0:T(4,128)(2,1)S(1)}, u32[]{:S(2)}, u32[]{:S(2)}) collective-permute-start(bf16[4,4,3712]{2,1,0:T(4,128)(2,1)S(1)} %collective-permute-done.7.refs_1_), channel_id=1, source_target_pairs={{0,2},{1,17},{2,0},{3,19},{4,6},{5,21},{6,4},{7,23},{8,10},{9,25},... | collective-permute-start | bytes 356360 | tf_op jit(solution)/shard_map/ppermute | solution.py:566
  56.9 3.2 %shard_map.202 = (bf16[4,4,3712]{2,1,0:T(4,128)(2,1)S(1)}, bf16[4,4,3712]{2,1,0:T(4,128)(2,1)S(1)}, bf16[1024,3584]{1,0:T(8,128)(2,1)S(1)}, bf16[3584,1024]{1,0:T(8,128)(2,1)S(1)}, bf16[3584,1024]{1,0:T(8,128)(2,1)S(1)}) custom-call(bf16[4,4,3712]{2,1,0:T(4,128)(2,1)S(1)} %get-tuple-element.40.refs_0_, ...), custom_call_target="tpu_custom_call", output_to_operand_aliasing={{2}: (2, {}), {3}: (3, {})} | custom-call | bytes 7340032 | tf_op jit(solution)/shard_map/pallas_call | solution.py:680
  62.2 3.8 %shard_map.203 = (f32[64,3584]{1,0:T(8,128)S(1)}, bf16[64,3584]{1,0:T(8,128)(2,1)S(1)}) custom-call(bf16[4,4,3712]{2,1,0:T(4,128)(2,1)S(1)} %get-tuple-element.43.refs_0_, bf16[4,4,3712]{2,1,0:T(4,128)(2,1)S(1)} %get-tuple-element.44.refs_1_, bf16[4,4,3712]{2,1,0:T(4,128)(2,1)S(1)} %collective-permute-done.8.refs_2_, ...), custom_call_target="tpu_custom_call" | custom-call | flops 2818572288 | bytes 22020096 | tf_op jit(solution)/shard_map/pallas_call | solution.py:48
  66.4 1.5 %collective-permute-done.14.got = bf16[64,3584]{1,0:T(8,128)(2,1)S(1)} collective-permute-done((bf16[64,3584]{1,0:T(8,128)(2,1)S(1)}, bf16[64,3584]{1,0:T(8,128)(2,1)S(1)}, u32[]{:S(2)}, u32[]{:S(2)}) %collective-permute-start.14) | collective-permute-done | bytes 458784 | tf_op jit(solution)/shard_map/ppermute | solution.py:566
  68.0 0.9 %collective-permute-start.15 = (bf16[32,3584]{1,0:T(8,128)(2,1)S(1)}, bf16[32,3584]{1,0:T(8,128)(2,1)S(1)}, u32[]{:S(2)}, u32[]{:S(2)}) collective-permute-start(bf16[32,3584]{1,0:T(8,128)(2,1)S(1)} %get-tuple-element.51), channel_id=1, source_target_pairs={{0,2},{1,17},{2,0},{3,19},{4,6},{5,21},{6,4},{7,23},{8,10},{9,25},... | collective-permute-start | bytes 688136 | tf_op jit(solution)/shard_map/ppermute | solution.py:566
  68.9 5.1 %collective-permute-done.15.got = bf16[32,3584]{1,0:T(8,128)(2,1)S(1)} collective-permute-done((bf16[32,3584]{1,0:T(8,128)(2,1)S(1)}, bf16[32,3584]{1,0:T(8,128)(2,1)S(1)}, u32[]{:S(2)}, u32[]{:S(2)}) %collective-permute-start.15) | collective-permute-done | bytes 229408 | tf_op jit(solution)/shard_map/ppermute | solution.py:566
  74.1 1.6 %collective-permute-start.16 = (bf16[16,3584]{1,0:T(8,128)(2,1)S(1)}, bf16[16,3584]{1,0:T(8,128)(2,1)S(1)}, u32[]{:S(2)}, u32[]{:S(2)}) collective-permute-start(bf16[16,3584]{1,0:T(8,128)(2,1)S(1)} %get-tuple-element.53), channel_id=1, source_target_pairs={{0,16},{1,3},{2,18},{3,1},{4,20},{5,7},{6,22},{7,5},{8,24},{9,11},... | collective-permute-start | bytes 344072 | tf_op jit(solution)/shard_map/ppermute | solution.py:566
  75.6 3.3 %collective-permute-done.16.got = bf16[16,3584]{1,0:T(8,128)(2,1)S(1)} collective-permute-done((bf16[16,3584]{1,0:T(8,128)(2,1)S(1)}, bf16[16,3584]{1,0:T(8,128)(2,1)S(1)}, u32[]{:S(2)}, u32[]{:S(2)}) %collective-permute-start.16) | collective-permute-done | bytes 114720 | tf_op jit(solution)/shard_map/ppermute | solution.py:566
  79.1 3.0 %collective-permute-start.18 = (bf16[4,3584]{1,0:T(4,128)(2,1)S(1)}, bf16[4,3584]{1,0:T(4,128)(2,1)S(1)}, u32[]{:S(2)}, u32[]{:S(2)}) collective-permute-start(bf16[4,3584]{1,0:T(4,128)(2,1)S(1)} %get-tuple-element.56), channel_id=1, source_target_pairs={{0,8},{1,9},{2,10},{3,11},{4,12},{5,13},{6,14},{7,15},{8,0},{9,1},... | collective-permute-start | bytes 86024 | tf_op jit(solution)/shard_map/ppermute | solution.py:566
  82.1 1.4 %collective-permute-start.19 = (bf16[4,3584]{1,0:T(4,128)(2,1)S(1)}, bf16[4,3584]{1,0:T(4,128)(2,1)S(1)}, u32[]{:S(2)}, u32[]{:S(2)}) collective-permute-start(bf16[4,3584]{1,0:T(4,128)(2,1)S(1)} %get-tuple-element.57), channel_id=1, source_target_pairs={{0,12},{1,13},{2,14},{3,15},{4,8},{5,9},{6,10},{7,11},{8,4},{9,5},... | collective-permute-start | bytes 86024 | tf_op jit(solution)/shard_map/ppermute | solution.py:566
  83.9 3.8 %collective-permute-done.19.refs_3_ = bf16[4,3584]{1,0:T(4,128)(2,1)S(1)} collective-permute-done((bf16[4,3584]{1,0:T(4,128)(2,1)S(1)}, bf16[4,3584]{1,0:T(4,128)(2,1)S(1)}, u32[]{:S(2)}, u32[]{:S(2)}) %collective-permute-start.19) | collective-permute-done | bytes 28704 | tf_op jit(solution)/shard_map/ppermute | solution.py:566
  (46 shorter events, 6.3 us)
Async XLA Ops:
  0.6 14.9 %copy-start.2 = (bf16[2,512,128]{2,1,0:T(8,128)(2,1)S(1)}, bf16[2,512,128]{2,1,0:T(8,128)(2,1)}, u32[]{:S(2)}) copy-start(bf16[2,512,128]{2,1,0:T(8,128)(2,1)} %w_uv.1) | copy-start | bytes 786436
  0.7 40.6 %copy-start.4 = (bf16[4,3584]{1,0:T(4,128)(2,1)S(1)}, bf16[4,3584]{1,0:T(4,128)(2,1)}, u32[]{:S(2)}) copy-start(bf16[4,3584]{1,0:T(4,128)(2,1)} %residual.1) | copy-start | bytes 86020
  0.7 40.5 %copy-start.5 = (f32[3584]{0:T(1024)S(1)}, f32[3584]{0:T(1024)}, u32[]{:S(2)}) copy-start(f32[3584]{0:T(1024)} %gain.1) | copy-start | bytes 43012
  0.7 40.5 %copy-start.6 = (s32[4,8]{1,0:T(4,128)S(1)}, s32[4,8]{1,0:T(4,128)}, u32[]{:S(2)}) copy-start(s32[4,8]{1,0:T(4,128)} %routes.1) | copy-start | bytes 388
  3.3 10.5 %collective-permute-start = (bf16[4,64,512]{2,1,0:T(8,128)(2,1)}, bf16[4,64,512]{2,1,0:T(8,128)(2,1)S(1)}, u32[]{:S(2)}, u32[]{:S(2)}) collective-permute-start(bf16[4,64,512]{2,1,0:T(8,128)(2,1)} %get-tuple-element.30), channel_id=1, source_target_pairs={{0,16},{1,17},{2,18},{3,19},{4,20},{5,21},{6,22},{7,23},{8,24},{9,... | collective-permute-start | bytes 786440 | tf_op jit(solution)/shard_map/ppermute | solution.py:566
  6.3 7.4 %collective-permute-start.1 = (bf16[8,2176]{1,0:T(8,128)(2,1)}, bf16[8,2176]{1,0:T(8,128)(2,1)S(1)}, u32[]{:S(2)}, u32[]{:S(2)}) collective-permute-start(bf16[8,2176]{1,0:T(8,128)(2,1)} %get-tuple-element.31), channel_id=1, source_target_pairs={{0,16},{1,17},{2,18},{3,19},{4,20},{5,21},{6,22},{7,23},{8,24},{9,... | collective-permute-start | bytes 104456 | tf_op jit(solution)/shard_map/ppermute | solution.py:566
  15.4 14.0 %collective-permute-start.3 = (bf16[256,3584]{1,0:T(8,128)(2,1)S(1)}, bf16[256,3584]{1,0:T(8,128)(2,1)S(1)}, u32[]{:S(2)}, u32[]{:S(2)}) collective-permute-start(bf16[256,3584]{1,0:T(8,128)(2,1)S(1)} %copy-done.1), channel_id=1, source_target_pairs={{0,1},{1,0},{2,3},{3,2},{4,5},{5,4},{6,7},{7,6},{8,9},{9,8},{10,11... | collective-permute-start | bytes 5505032 | tf_op jit(solution)/shard_map/ppermute | solution.py:566
  15.5 13.9 %collective-permute-start.2 = (bf16[2,512,128]{2,1,0:T(8,128)(2,1)S(1)}, bf16[2,512,128]{2,1,0:T(8,128)(2,1)S(1)}, u32[]{:S(2)}, u32[]{:S(2)}) collective-permute-start(bf16[2,512,128]{2,1,0:T(8,128)(2,1)S(1)} %copy-done.2), channel_id=1, source_target_pairs={{0,1},{1,0},{2,3},{3,2},{4,5},{5,4},{6,7},{7,6},{8,9},{9,8},{10,11... | collective-permute-start | bytes 786440 | tf_op jit(solution)/shard_map/ppermute | solution.py:566
  41.9 7.6 %collective-permute-start.4 = (bf16[1,4,3712]{2,1,0:T(4,128)(2,1)S(1)}, bf16[1,4,3712]{2,1,0:T(4,128)(2,1)S(1)}, u32[]{:S(2)}, u32[]{:S(2)}) collective-permute-start(bf16[1,4,3712]{2,1,0:T(4,128)(2,1)S(1)} %get-tuple-element.37.refs_0_), channel_id=1, source_target_pairs={{0,4},{1,5},{2,6},{3,7},{4,0},{5,1},{6,2},{7,3},{8,12},{9,13},{10,... | collective-permute-start | bytes 89096 | tf_op jit(solution)/shard_map/ppermute | solution.py:566
  42.8 6.7 %collective-permute-start.5 = (bf16[1,4,3712]{2,1,0:T(4,128)(2,1)S(1)}, bf16[1,4,3712]{2,1,0:T(4,128)(2,1)S(1)}, u32[]{:S(2)}, u32[]{:S(2)}) collective-permute-start(bf16[1,4,3712]{2,1,0:T(4,128)(2,1)S(1)} %get-tuple-element.37.refs_0_), channel_id=1, source_target_pairs={{0,8},{1,9},{2,10},{3,11},{4,12},{5,13},{6,14},{7,15},{8,0},{9,1},... | collective-permute-start | bytes 89096 | tf_op jit(solution)/shard_map/ppermute | solution.py:566
  43.4 6.1 %collective-permute-start.6 = (bf16[1,4,3712]{2,1,0:T(4,128)(2,1)S(1)}, bf16[1,4,3712]{2,1,0:T(4,128)(2,1)S(1)}, u32[]{:S(2)}, u32[]{:S(2)}) collective-permute-start(bf16[1,4,3712]{2,1,0:T(4,128)(2,1)S(1)} %get-tuple-element.37.refs_0_), channel_id=1, source_target_pairs={{0,12},{1,13},{2,14},{3,15},{4,8},{5,9},{6,10},{7,11},{8,4},{9,5},... | collective-permute-start | bytes 89096 | tf_op jit(solution)/shard_map/ppermute | solution.py:566
  49.6 6.1 %collective-permute-start.7 = (bf16[4,4,3712]{2,1,0:T(4,128)(2,1)S(1)}, bf16[4,4,3712]{2,1,0:T(4,128)(2,1)S(1)}, u32[]{:S(2)}, u32[]{:S(2)}) collective-permute-start(bf16[4,4,3712]{2,1,0:T(4,128)(2,1)S(1)} %shard_map.200.refs_0_), channel_id=1, source_target_pairs={{0,16},{1,3},{2,18},{3,1},{4,20},{5,7},{6,22},{7,5},{8,24},{9,11},... | collective-permute-start | bytes 356360 | tf_op jit(solution)/shard_map/ppermute | solution.py:566
  54.3 6.4 %collective-permute-start.8 = (bf16[4,4,3712]{2,1,0:T(4,128)(2,1)S(1)}, bf16[4,4,3712]{2,1,0:T(4,128)(2,1)S(1)}, u32[]{:S(2)}, u32[]{:S(2)}) collective-permute-start(bf16[4,4,3712]{2,1,0:T(4,128)(2,1)S(1)} %get-tuple-element.40.refs_0_), channel_id=1, source_target_pairs={{0,2},{1,17},{2,0},{3,19},{4,6},{5,21},{6,4},{7,23},{8,10},{9,25},... | collective-permute-start | bytes 356360 | tf_op jit(solution)/shard_map/ppermute | solution.py:566
  55.6 5.2 %collective-permute-start.9 = (bf16[4,4,3712]{2,1,0:T(4,128)(2,1)S(1)}, bf16[4,4,3712]{2,1,0:T(4,128)(2,1)S(1)}, u32[]{:S(2)}, u32[]{:S(2)}) collective-permute-start(bf16[4,4,3712]{2,1,0:T(4,128)(2,1)S(1)} %collective-permute-done.7.refs_1_), channel_id=1, source_target_pairs={{0,2},{1,17},{2,0},{3,19},{4,6},{5,21},{6,4},{7,23},{8,10},{9,25},... | collective-permute-start | bytes 356360 | tf_op jit(solution)/shard_map/ppermute | solution.py:566
  60.2 1.4 %collective-permute-start.10 = (bf16[4,4,3712]{2,1,0:T(4,128)(2,1)S(1)}, bf16[4,4,3712]{2,1,0:T(4,128)(2,1)S(1)}, u32[]{:S(2)}, u32[]{:S(2)}) collective-permute-start(bf16[4,4,3712]{2,1,0:T(4,128)(2,1)S(1)} %get-tuple-element.43.refs_0_), channel_id=1, source_target_pairs={{0,1},{1,0},{2,3},{3,2},{4,5},{5,4},{6,7},{7,6},{8,9},{9,8},{10,11... | collective-permute-start | bytes 356360 | tf_op jit(solution)/shard_map/ppermute | solution.py:566
  60.2 1.5 %collective-permute-start.11 = (bf16[4,4,3712]{2,1,0:T(4,128)(2,1)S(1)}, bf16[4,4,3712]{2,1,0:T(4,128)(2,1)S(1)}, u32[]{:S(2)}, u32[]{:S(2)}) collective-permute-start(bf16[4,4,3712]{2,1,0:T(4,128)(2,1)S(1)} %get-tuple-element.44.refs_1_), channel_id=1, source_target_pairs={{0,1},{1,0},{2,3},{3,2},{4,5},{5,4},{6,7},{7,6},{8,9},{9,8},{10,11... | collective-permute-start | bytes 356360 | tf_op jit(solution)/shard_map/ppermute | solution.py:566
  60.7 1.3 %collective-permute-start.12 = (bf16[4,4,3712]{2,1,0:T(4,128)(2,1)S(1)}, bf16[4,4,3712]{2,1,0:T(4,128)(2,1)S(1)}, u32[]{:S(2)}, u32[]{:S(2)}) collective-permute-start(bf16[4,4,3712]{2,1,0:T(4,128)(2,1)S(1)} %collective-permute-done.8.refs_2_), channel_id=1, source_target_pairs={{0,1},{1,0},{2,3},{3,2},{4,5},{5,4},{6,7},{7,6},{8,9},{9,8},{10,11... | collective-permute-start | bytes 356360 | tf_op jit(solution)/shard_map/ppermute | solution.py:566
  60.8 1.4 %collective-permute-start.13 = (bf16[4,4,3712]{2,1,0:T(4,128)(2,1)S(1)}, bf16[4,4,3712]{2,1,0:T(4,128)(2,1)S(1)}, u32[]{:S(2)}, u32[]{:S(2)}) collective-permute-start(bf16[4,4,3712]{2,1,0:T(4,128)(2,1)S(1)} %collective-permute-done.9.refs_3_), channel_id=1, source_target_pairs={{0,1},{1,0},{2,3},{3,2},{4,5},{5,4},{6,7},{7,6},{8,9},{9,8},{10,11... | collective-permute-start | bytes 356360 | tf_op jit(solution)/shard_map/ppermute | solution.py:566
  66.0 1.9 %collective-permute-start.14 = (bf16[64,3584]{1,0:T(8,128)(2,1)S(1)}, bf16[64,3584]{1,0:T(8,128)(2,1)S(1)}, u32[]{:S(2)}, u32[]{:S(2)}) collective-permute-start(bf16[64,3584]{1,0:T(8,128)(2,1)S(1)} %get-tuple-element.49), channel_id=1, source_target_pairs={{0,1},{1,0},{2,3},{3,2},{4,5},{5,4},{6,7},{7,6},{8,9},{9,8},{10,11... | collective-permute-start | bytes 1376264 | tf_op jit(solution)/shard_map/ppermute | solution.py:566
  68.0 6.1 %collective-permute-start.15 = (bf16[32,3584]{1,0:T(8,128)(2,1)S(1)}, bf16[32,3584]{1,0:T(8,128)(2,1)S(1)}, u32[]{:S(2)}, u32[]{:S(2)}) collective-permute-start(bf16[32,3584]{1,0:T(8,128)(2,1)S(1)} %get-tuple-element.51), channel_id=1, source_target_pairs={{0,2},{1,17},{2,0},{3,19},{4,6},{5,21},{6,4},{7,23},{8,10},{9,25},... | collective-permute-start | bytes 688136 | tf_op jit(solution)/shard_map/ppermute | solution.py:566
  74.1 4.9 %collective-permute-start.16 = (bf16[16,3584]{1,0:T(8,128)(2,1)S(1)}, bf16[16,3584]{1,0:T(8,128)(2,1)S(1)}, u32[]{:S(2)}, u32[]{:S(2)}) collective-permute-start(bf16[16,3584]{1,0:T(8,128)(2,1)S(1)} %get-tuple-element.53), channel_id=1, source_target_pairs={{0,16},{1,3},{2,18},{3,1},{4,20},{5,7},{6,22},{7,5},{8,24},{9,11},... | collective-permute-start | bytes 344072 | tf_op jit(solution)/shard_map/ppermute | solution.py:566
  79.0 4.5 %collective-permute-start.17 = (bf16[4,3584]{1,0:T(4,128)(2,1)S(1)}, bf16[4,3584]{1,0:T(4,128)(2,1)S(1)}, u32[]{:S(2)}, u32[]{:S(2)}) collective-permute-start(bf16[4,3584]{1,0:T(4,128)(2,1)S(1)} %get-tuple-element.55), channel_id=1, source_target_pairs={{0,4},{1,5},{2,6},{3,7},{4,0},{5,1},{6,2},{7,3},{8,12},{9,13},{10,... | collective-permute-start | bytes 86024 | tf_op jit(solution)/shard_map/ppermute | solution.py:566
  79.1 4.8 %collective-permute-start.18 = (bf16[4,3584]{1,0:T(4,128)(2,1)S(1)}, bf16[4,3584]{1,0:T(4,128)(2,1)S(1)}, u32[]{:S(2)}, u32[]{:S(2)}) collective-permute-start(bf16[4,3584]{1,0:T(4,128)(2,1)S(1)} %get-tuple-element.56), channel_id=1, source_target_pairs={{0,8},{1,9},{2,10},{3,11},{4,12},{5,13},{6,14},{7,15},{8,0},{9,1},... | collective-permute-start | bytes 86024 | tf_op jit(solution)/shard_map/ppermute | solution.py:566
  82.1 5.7 %collective-permute-start.19 = (bf16[4,3584]{1,0:T(4,128)(2,1)S(1)}, bf16[4,3584]{1,0:T(4,128)(2,1)S(1)}, u32[]{:S(2)}, u32[]{:S(2)}) collective-permute-start(bf16[4,3584]{1,0:T(4,128)(2,1)S(1)} %get-tuple-element.57), channel_id=1, source_target_pairs={{0,12},{1,13},{2,14},{3,15},{4,8},{5,9},{6,10},{7,11},{8,4},{9,5},... | collective-permute-start | bytes 86024 | tf_op jit(solution)/shard_map/ppermute | solution.py:566
  (3 other events, 21.2 us)
